TPU v7x, 128 devices: a whole 4x4x4 slice. The times are simulated.
128 devices in a mesh: role: 2 (over core), rep: 2 (over z_hi), tile: 32 (over x, y, z_lo).
Axes of the slice: x: 4, y: 4, z: 4 (z_hi: 2, z_lo: 2; z = z_hi * 2 + z_lo), core: 2. Of those that a mesh axis runs over, the one named last changes fastest.
Arguments:
- fields: float32 [2, 3, 128, 32, 512], P(None, None, 'tile', 'role', 'rep'), may hold values from -6 to 6
- material: int32 [128, 32, 512], P('tile', 'role', 'rep'), may hold values from 0 to 3
- permittivity: float32 [4], replicated, may hold values from 1 to 4
- conductivity: float32 [4], replicated, may hold values from 0 to 1
- plan: int32 [4], replicated, may hold values from 1 to 3
- mode_counts: int32 [2, 3], replicated, may hold values from 4 to 8
- lift_weight: float32 [64, 6], replicated, may hold values from -2.5 to 2.5
- pointwise: float32 [2, 64, 64], replicated, may hold values from -0.75 to 0.75
- spectral_weight: float32 [2, 256, 16, 64, 64], P(None, 'tile'), may hold values from -6 to 6
- project_weight: float32 [6, 64], replicated, may hold values from -0.75 to 0.75
Outputs:
- new_fields: float32 [2, 3, 128, 32, 512], P(None, None, 'tile', 'role', 'rep')
- lift_grad: float32 [64, 6], replicated
- pointwise_grad: float32 [2, 64, 64], replicated
- spectral_grad: float32 [2, 256, 16, 64, 64], P(None, 'tile')
- project_grad: float32 [6, 64], replicated
- total_loss: float32 [], replicated
All inputs are finite; a program needn't handle non-finite values.
Results may differ from a plain program's by a relative error of at most 0.0003.
Values sent between devices are 32-bit elements; how exact they have to be, the bound alone decides.
No kernel may reach another device: no remote copies, remote signals or barrier semaphores. Data moves between devices by JAX's collectives and lax.ppermute only.
A program may use at most 192 MiB of HBM per device.

v0:
```python
import math

import jax
import jax.numpy as jnp
from jax import lax
from jax.sharding import PartitionSpec as P

STEPS = 4
MODES = 8
LAYERS = 2


STEP_TIME = 0.5
PRECISE = lax.Precision.HIGHEST


def passed_along(value, axis, by):
    length = lax.axis_size(axis)
    pairs = [(i, i + by) for i in range(length) if 0 <= i + by < length]
    return lax.ppermute(value, axis, pairs)


def forward_diff(grid_field, along, border):
    remainder = lax.slice_in_dim(grid_field, 1, grid_field.shape[along], axis=along)
    return jnp.concatenate([remainder, border], axis=along) - grid_field


def backward_diff(grid_field, along, border):
    remainder = lax.slice_in_dim(grid_field, 0, grid_field.shape[along] - 1, axis=along)
    return grid_field - jnp.concatenate([border, remainder], axis=along)


def curl_of(components, x_plane, y_plane, z_plane, difference):
    d_zy = difference(components[2], 1, y_plane[1])
    d_yz = difference(components[1], 2, z_plane[1])
    d_xz = difference(components[0], 2, z_plane[0])
    d_zx = difference(components[2], 0, x_plane[1])
    d_yx = difference(components[1], 0, x_plane[0])
    d_xy = difference(components[0], 1, y_plane[0])
    return jnp.stack([d_zy - d_yz, d_xz - d_zx, d_yx - d_xy])


def coarsen(components):
    a, b, c, d = components.shape
    return components.reshape(a, b // 2, 2, c // 2, 2, d // 2, 2).mean(axis=(2, 4, 6))


def mode_table(number_kept, length):
    frequency = jnp.arange(MODES, dtype=jnp.int32)
    position = jnp.arange(length, dtype=jnp.int32)
    angles = (
        2.0
        * math.pi
        / length
        * (frequency[:, None] * position[None, :] % length).astype(jnp.float32)
    )
    retained = (frequency < number_kept).astype(jnp.float32)[:, None] * math.sqrt(2.0 / length)
    return jnp.concatenate([jnp.cos(angles) * retained, jnp.sin(angles) * retained], axis=0)


def front_borders(electric):
    x_plane = passed_along(electric[1:3, :1], "tile", -1)
    y_plane = passed_along(electric[0::2, :, :1], "role", -1)
    z_plane = passed_along(electric[0:2, :, :, :1], "rep", -1)
    return (x_plane, y_plane, z_plane)


def rear_borders(magnetic):
    x_plane = passed_along(magnetic[1:3, -1:], "tile", 1)
    y_plane = passed_along(magnetic[0::2, :, -1:], "role", 1)
    z_plane = passed_along(magnetic[0:2, :, :, -1:], "rep", 1)
    return (x_plane, y_plane, z_plane)


def spectral_pass(hidden, tables, multiply):
    table_x, table_y, table_z = tables
    a = jnp.einsum("cxyz,kz->cxyk", hidden, table_z, precision=PRECISE)
    b = jnp.einsum("cxyk,jy->cxjk", a, table_y, precision=PRECISE)
    b = b.reshape(b.shape[0], b.shape[1], b.shape[2] * b.shape[3])
    pencil = lax.all_to_all(b, "tile", split_axis=2, concat_axis=1, tiled=True)
    coefficients = jnp.einsum("cxm,lx->clm", pencil, table_x, precision=PRECISE)
    mixed_modes, by_product = multiply(coefficients)
    spatial = jnp.einsum("olm,lx->oxm", mixed_modes, table_x, precision=PRECISE)
    slab_part = lax.all_to_all(spatial, "tile", split_axis=1, concat_axis=2, tiled=True)
    k = table_z.shape[0]
    slab_part = slab_part.reshape(slab_part.shape[0], slab_part.shape[1], k, k)
    a = jnp.einsum("cxjk,jy->cxyk", slab_part, table_y, precision=PRECISE)
    return (jnp.einsum("cxyk,kz->cxyz", a, table_z, precision=PRECISE), coefficients, by_product)


def local(
    fields,
    material,
    permittivity,
    conductivity,
    plan,
    mode_counts,
    lift_weight,
    pointwise,
    spectral_weight,
    project_weight,
):
    permit = jnp.ones(material.shape, jnp.float32)
    conduct = jnp.zeros(material.shape, jnp.float32)
    for material_kind in range(permittivity.shape[0]):
        chosen = material == material_kind
        permit = jnp.where(chosen, permittivity[material_kind], permit)
        conduct = jnp.where(chosen, conductivity[material_kind], conduct)
    damping = conduct * (0.5 * STEP_TIME) / permit
    keep_e = (1.0 - damping) / (1.0 + damping)
    gain_e = STEP_TIME / (permit * (1.0 + damping))
    electric = fields[0]
    magnetic = fields[1]
    sample_total = plan.shape[0]
    cells = electric.shape
    snapshots = jnp.zeros(
        (sample_total, 6, cells[1] // 2, cells[2] // 2, cells[3] // 2), jnp.float32
    )
    reduced = None
    for step_num in range(STEPS):
        x_plane, y_plane, z_plane = front_borders(electric)
        magnetic = magnetic - STEP_TIME * curl_of(electric, x_plane, y_plane, z_plane, forward_diff)
        x_plane, y_plane, z_plane = rear_borders(magnetic)
        electric = keep_e * electric + gain_e * curl_of(
            magnetic, x_plane, y_plane, z_plane, backward_diff
        )
        reduced = jnp.concatenate([coarsen(electric), coarsen(magnetic)], axis=0)
        if step_num + 1 < STEPS:
            picked = (plan == step_num + 1).astype(jnp.float32)
            snapshots = snapshots + picked[:, None, None, None, None] * reduced[None]
    role_count = lax.axis_size("role")
    rep_count = lax.axis_size("rep")

    def arrange(pieces):
        s, c, x, y, z = pieces.shape
        grouped = pieces.reshape(role_count, rep_count, c, x, y, z)
        return grouped.transpose(2, 3, 0, 4, 1, 5).reshape(c, x, role_count * y, rep_count * z)

    inputs = arrange(
        lax.all_to_all(snapshots, ("role", "rep"), split_axis=0, concat_axis=0, tiled=True)
    )
    target = arrange(lax.all_gather(reduced[None], ("role", "rep"), axis=0, tiled=True))
    x_length = inputs.shape[1] * lax.axis_size("tile")
    y_length = inputs.shape[2]
    z_length = inputs.shape[3]
    tables = []
    for layer_idx in range(LAYERS):
        tables.append(
            (
                mode_table(mode_counts[layer_idx, 0], x_length),
                mode_table(mode_counts[layer_idx, 1], y_length),
                mode_table(mode_counts[layer_idx, 2], z_length),
            )
        )
    hidden = jnp.einsum("ca,axyz->cxyz", lift_weight, inputs, precision=PRECISE)
    saved = []
    for layer_idx in range(LAYERS):

        def forward_mix(coefficients, weights=spectral_weight[layer_idx]):
            return (
                jnp.einsum("mloi,ilm->olm", weights, coefficients, precision=PRECISE),
                coefficients,
            )

        spatial, coefficients, _ = spectral_pass(hidden, tables[layer_idx], forward_mix)
        pre_act = spatial + jnp.einsum(
            "oi,ixyz->oxyz", pointwise[layer_idx], hidden, precision=PRECISE
        )
        saved.append((hidden, pre_act, coefficients))
        hidden = jax.nn.gelu(pre_act)
    predicted = jnp.einsum("ac,cxyz->axyz", project_weight, hidden, precision=PRECISE)
    norm_count = 6.0 * x_length * y_length * z_length * sample_total
    errors = predicted - target
    local_loss = jnp.sum(errors * errors) / norm_count
    grad_pred = errors * (2.0 / norm_count)
    project_grad = jnp.einsum("axyz,cxyz->ac", grad_pred, hidden, precision=PRECISE)
    grad_act = jnp.einsum("ac,axyz->cxyz", project_weight, grad_pred, precision=PRECISE)
    pointwise_grads = [None] * LAYERS
    mode_grads = [None] * LAYERS
    for layer_idx in reversed(range(LAYERS)):
        layer_in, pre_act, coefficients = saved[layer_idx]
        _, gelu_pull = jax.vjp(jax.nn.gelu, pre_act)
        grad_pre = gelu_pull(grad_act)[0]
        pointwise_grads[layer_idx] = jnp.einsum(
            "oxyz,ixyz->oi", grad_pre, layer_in, precision=PRECISE
        )

        def backward_mix(grad_coeff, weights=spectral_weight[layer_idx], saved_coeff=coefficients):
            weight_grad = jnp.einsum("olm,ilm->mloi", grad_coeff, saved_coeff, precision=PRECISE)
            return (
                jnp.einsum("mloi,olm->ilm", weights, grad_coeff, precision=PRECISE),
                weight_grad,
            )

        spatial, _, weight_grad = spectral_pass(grad_pre, tables[layer_idx], backward_mix)
        mode_grads[layer_idx] = weight_grad
        grad_act = spatial + jnp.einsum(
            "oi,oxyz->ixyz", pointwise[layer_idx], grad_pre, precision=PRECISE
        )
    lift_grad = jnp.einsum("cxyz,axyz->ca", grad_act, inputs, precision=PRECISE)
    spectral_grad = lax.psum(jnp.stack(mode_grads), ("role", "rep"))
    lift_total, pointwise_total, project_total, loss_total = lax.psum(
        (lift_grad, jnp.stack(pointwise_grads), project_grad, local_loss), ("role", "rep", "tile")
    )
    return (
        jnp.stack([electric, magnetic]),
        lift_total,
        pointwise_total,
        spectral_grad,
        project_total,
        loss_total,
    )


def solution(mesh):
    return jax.shard_map(
        local,
        mesh=mesh,
        in_specs=(
            P(None, None, "tile", "role", "rep"),
            P("tile", "role", "rep"),
            P(),
            P(),
            P(),
            P(),
            P(),
            P(),
            P(None, "tile", None, None, None),
            P(),
        ),
        out_specs=(
            P(None, None, "tile", "role", "rep"),
            P(),
            P(),
            P(None, "tile", None, None, None),
            P(),
            P(),
        ),
        check_vma=False,
    )
```

profile of v0, /device:TPU:1, one launch (start us, length us, event | category | flops | bytes accessed | tf_op | source)
XLA Modules:
  0.0 981.7 jit_solution(18148417942044414509)
XLA Ops:
  19.2 5.1 subtract_divide_fusion
  29.5 5.5 mul.788
  40.2 8.5 slice_bitcast_fusion
  55.4 5.5 mul.785
  63.7 5.5 squeeze.267
  69.3 5.5 squeeze.268
  74.8 5.6 squeeze.269
  82.5 5.8 collective-permute-start.4
  94.1 5.5 concatenate.634
  99.6 5.6 concatenate.635
  105.2 5.6 concatenate.636
  110.7 5.5 concatenate.639
  116.3 5.5 concatenate.637
  121.8 5.5 concatenate.638
  127.3 19.1 %subtract_subtract_fusion.2 = (f32[1,2,2,8,2,128,2]{6,5,4,3,2,1,0:T(8,128)}, f32[1,2,2,8,2,128,2]{6,5,4,3,2,1,0:T(8,128)}, f32[1,2,2,8,2,128,2]{6,5,4,3,2,1,0:T(8,128)}) fusion(f32[1,2,2,8,2,128,2]{6,5,4,3,2,1,0:T(8,128)} %concatenate.635, f32[1,2,2,8,2,128,2]{6,5,4,3,2,1,0:T(8,128)} %squeeze.268, f32[1,2,2,8,2,128,2]{6,5,4,3,2,1,0:T(8,128)} %concatenate.634, ...), kind=kLoop, calls=%fused_computation.7 | loop fusion | flops 147456 | bytes 786432 | tf_op jit(solution)/shard_map/sub | solution.py:40
  157.2 5.5 stack.222
  162.7 5.6 stack.223
  168.3 5.5 stack.224
  187.1 5.8 collective-permute-start.10
  192.9 5.5 stack.231
  198.5 5.6 stack.232
  204.0 5.5 stack.233
  209.5 5.1 collective-permute-start.11
  226.5 5.5 stack.227
  232.1 5.6 stack.228
  237.6 5.5 stack.229
  256.4 5.8 collective-permute-start.16
  262.3 5.5 stack.239
  267.8 5.6 stack.240
  273.4 5.5 stack.241
  278.9 5.8 collective-permute-start.17
  299.0 5.5 stack.235
  304.5 5.6 stack.236
  310.1 5.5 stack.237
  331.7 5.8 collective-permute-start.22
  337.5 5.5 stack.247
  343.1 5.6 stack.248
  348.6 5.5 stack.249
  354.1 5.8 collective-permute-start.23
  370.4 5.5 stack.243
  375.9 5.6 stack.244
  381.5 5.5 stack.245
  387.8 13.9 %squeeze.265 = f32[3,2,2,8,2,128,2]{6,5,4,3,2,1,0:T(8,128)} reshape(f32[1,3,4,16,256]{4,3,2,1,0:T(8,128)S(1)} %get-tuple-element.36) | data formatting | bytes 393216 | tf_op jit(solution)/shard_map/squeeze | solution.py:112
  401.7 7.6 copy.274
  417.8 13.9 %squeeze.266 = f32[3,2,2,8,2,128,2]{6,5,4,3,2,1,0:T(8,128)} reshape(f32[1,3,4,16,256]{4,3,2,1,0:T(8,128)S(1)} %get-tuple-element.38) | data formatting | bytes 393216 | tf_op jit(solution)/shard_map/squeeze | solution.py:113
  431.7 7.6 copy.282
  446.0 5.3 all-to-all-done
  458.1 18.3 %all-to-all-start.1 = ((f32[32,1,1024]{2,1,0:T(1,128)}), f32[32,1,1024]{2,1,0:T(1,128)S(1)}, u32[]{:S(2)}, u32[]{:S(2)}) async-start(f32[32,1,1024]{2,1,0:T(1,128)} %reshape.1354), calls=%async_computation.1 | async-start | bytes 262144 | tf_op jit(solution)/shard_map/all_to_all | solution.py:80
  477.0 6.7 all-to-all-done.1
  485.8 8.4 fusion.6
  511.3 5.9 multiply_multiply_fusion.5
  528.7 16.2 %all-gather = f32[24,2,8,128]{3,2,1,0:T(8,128)S(1)} all-gather(f32[6,2,8,128]{3,2,1,0:T(8,128)S(1)} %pad_maximum_fusion.12), channel_id=2, replica_groups=mesh['role'=2,'rep'=2,'tile'=32] {'role','rep'}, dimensions={0}, use_global_device_ids=true | all-gather | bytes 245760 | tf_op jit(solution)/shard_map/all_gather | solution.py:142
  547.2 8.4 fusion.2
  557.0 8.1 all-to-all-start.4
  565.1 6.1 fusion.42
  594.5 13.8 %all_to_all.137 = f32[32,1,1024]{2,1,0:T(1,128)S(1)} all-to-all(f32[32,1,1024]{2,1,0:T(1,128)S(1)} %reshape.1362), channel_id=1, replica_groups=mesh['role'=2,'rep'=2,'tile'=32] {'tile'}, dimensions={0} | all-to-all | bytes 262144 | tf_op jit(solution)/shard_map/all_to_all | solution.py:80
  609.8 5.3 fusion
  621.0 6.1 fusion.35
  632.4 5.7 fusion.13
  645.3 6.6 all-to-all-start.7
  675.1 6.4 fusion.50
  707.9 181.7 %all-reduce = (f32[64,6]{0,1:T(8,128)}, f32[2,64,64]{2,1,0:T(8,128)}, f32[6,64]{1,0:T(8,128)}, f32[]{:T(128)}) all-reduce(f32[64,6]{0,1:T(8,128)S(1)} %fusion.63, f32[2,64,64]{2,1,0:T(8,128)S(1)} %pad_maximum_fusion.8, f32[6,64]{1,0:T(8,128)S(1)} %fusion.60, f32[]{:T(128)S(6)} %div.51), channel_id=1, replica_groups=mesh['role'=2,'rep'=2,'tile'=32] {'role','rep','tile'}, use_global_device_ids=true, to_apply=%region_8.9 | all-reduce | flops 8961 | bytes 71688 | tf_op jit(solution)/shard_map/psum | solution.py:202
  889.6 76.4 %all-reduce.3.cloned.1.call-done = f32[2,8,16,64,64]{4,3,2,1,0:T(8,128)} async-done(((f32[2,8,16,64,64]{4,3,2,1,0:T(8,128)}), f32[2,8,16,64,64]{4,3,2,1,0:T(8,128)}) %all-reduce.3.cloned.1.call-update) | async-done | bytes 4194320 | tf_op jit(solution)/shard_map/psum | solution.py:201
  966.0 8.4 copy.520
  (485 shorter events, 277.6 us)
Async XLA Ops:
  7.2 573.8 %copy-start = (f32[6,64]{1,0:T(8,128)S(1)}, f32[6,64]{1,0:T(8,128)}, u32[]{:S(2)}) copy-start(f32[6,64]{1,0:T(8,128)} %param.19) | copy-start | bytes 4612
  7.2 10.8 %copy-start.75 = (f32[4]{0:T(128)S(1)}, f32[4]{0:T(128)}, u32[]{:S(2)}) copy-start(f32[4]{0:T(128)} %param.13) | copy-start | bytes 52
  7.2 11.4 %copy-start.76 = (f32[4]{0:T(128)S(1)}, f32[4]{0:T(128)}, u32[]{:S(2)}) copy-start(f32[4]{0:T(128)} %param.12) | copy-start | bytes 52
  7.2 12.0 %copy-start.73 = (s32[4,16,256]{2,1,0:T(8,128)S(1)}, s32[4,16,256]{2,1,0:T(8,128)}, u32[]{:S(2)}) copy-start(s32[4,16,256]{2,1,0:T(8,128)} %param.11) | copy-start | bytes 196612
  8.2 73.4 %collective-permute-start.2 = (f32[2,1,16,256]{3,2,1,0:T(8,128)S(1)}, f32[2,1,16,256]{3,2,1,0:T(8,128)S(1)}, u32[]{:S(2)}, u32[]{:S(2)}) collective-permute-start(f32[2,1,16,256]{3,2,1,0:T(8,128)S(1)} %slice.729), channel_id=1, source_target_pairs={{1,0},{2,1},{3,2},{4,3},{5,4},{6,5},{7,6},{8,7},{9,8},{10,9},{11,1... | collective-permute-start | bytes 98312 | tf_op jit(solution)/shard_map/ppermute | solution.py:20
  9.5 70.8 %collective-permute-start.1 = (f32[2,4,16,1]{3,2,1,0:T(8,128)S(1)}, f32[2,4,16,1]{3,2,1,0:T(8,128)S(1)}, u32[]{:S(2)}, u32[]{:S(2)}) collective-permute-start(f32[2,4,16,1]{3,2,1,0:T(8,128)S(1)} %slice.725), channel_id=1, source_target_pairs={{32,0},{33,1},{34,2},{35,3},{36,4},{37,5},{38,6},{39,7},{40,8},{41... | collective-permute-start | bytes 1544 | tf_op jit(solution)/shard_map/ppermute | solution.py:20
  10.8 70.1 %collective-permute-start = (f32[2,4,1,256]{3,2,1,0:T(1,128)S(1)}, f32[2,4,1,256]{3,2,1,0:T(1,128)S(1)}, u32[]{:S(2)}, u32[]{:S(2)}) collective-permute-start(f32[2,4,1,256]{3,2,1,0:T(1,128)S(1)} %slice.570), channel_id=1, source_target_pairs={{64,0},{65,1},{66,2},{67,3},{68,4},{69,5},{70,6},{71,7},{72,8},{73... | collective-permute-start | bytes 24584 | tf_op jit(solution)/shard_map/ppermute | solution.py:20
  82.5 72.4 %collective-permute-start.4 = (f32[2,4,16,1]{3,2,1,0:T(8,128)S(1)}, f32[2,4,16,1]{3,2,1,0:T(8,128)S(1)}, u32[]{:S(2)}, u32[]{:S(2)}) collective-permute-start(f32[2,4,16,1]{3,2,1,0:T(8,128)S(1)} %slice.738), channel_id=1, source_target_pairs={{0,32},{1,33},{2,34},{3,35},{4,36},{5,37},{6,38},{7,39},{8,40},{9,... | collective-permute-start | bytes 1544 | tf_op jit(solution)/shard_map/ppermute | solution.py:20
  88.3 66.7 %collective-permute-start.5 = (f32[2,1,16,256]{3,2,1,0:T(8,128)S(1)}, f32[2,1,16,256]{3,2,1,0:T(8,128)S(1)}, u32[]{:S(2)}, u32[]{:S(2)}) collective-permute-start(f32[2,1,16,256]{3,2,1,0:T(8,128)S(1)} %slice.744), channel_id=1, source_target_pairs={{0,1},{1,2},{2,3},{3,4},{4,5},{5,6},{6,7},{7,8},{8,9},{9,10},{10,1... | collective-permute-start | bytes 98312 | tf_op jit(solution)/shard_map/ppermute | solution.py:20
  92.6 62.4 %collective-permute-start.3 = (f32[2,4,1,256]{3,2,1,0:T(1,128)S(1)}, f32[2,4,1,256]{3,2,1,0:T(1,128)S(1)}, u32[]{:S(2)}, u32[]{:S(2)}) collective-permute-start(f32[2,4,1,256]{3,2,1,0:T(1,128)S(1)} %slice.587), channel_id=1, source_target_pairs={{0,64},{1,65},{2,66},{3,67},{4,68},{5,69},{6,70},{7,71},{8,72},{9,... | collective-permute-start | bytes 24584 | tf_op jit(solution)/shard_map/ppermute | solution.py:20
  155.5 31.2 %collective-permute-start.7 = (f32[2,4,16,1]{3,2,1,0:T(8,128)S(1)}, f32[2,4,16,1]{3,2,1,0:T(8,128)S(1)}, u32[]{:S(2)}, u32[]{:S(2)}) collective-permute-start(f32[2,4,16,1]{3,2,1,0:T(8,128)S(1)} %slice.756), channel_id=1, source_target_pairs={{32,0},{33,1},{34,2},{35,3},{36,4},{37,5},{38,6},{39,7},{40,8},{41... | collective-permute-start | bytes 1544 | tf_op jit(solution)/shard_map/ppermute | solution.py:20
  173.8 12.9 %collective-permute-start.8 = (f32[2,1,16,256]{3,2,1,0:T(8,128)S(1)}, f32[2,1,16,256]{3,2,1,0:T(8,128)S(1)}, u32[]{:S(2)}, u32[]{:S(2)}) collective-permute-start(f32[2,1,16,256]{3,2,1,0:T(8,128)S(1)} %slice.762), channel_id=1, source_target_pairs={{1,0},{2,1},{3,2},{4,3},{5,4},{6,5},{7,6},{8,7},{9,8},{10,9},{11,1... | collective-permute-start | bytes 98312 | tf_op jit(solution)/shard_map/ppermute | solution.py:20
  175.1 11.6 %collective-permute-start.6 = (f32[2,4,1,256]{3,2,1,0:T(1,128)S(1)}, f32[2,4,1,256]{3,2,1,0:T(1,128)S(1)}, u32[]{:S(2)}, u32[]{:S(2)}) collective-permute-start(f32[2,4,1,256]{3,2,1,0:T(1,128)S(1)} %slice.606), channel_id=1, source_target_pairs={{64,0},{65,1},{66,2},{67,3},{68,4},{69,5},{70,6},{71,7},{72,8},{73... | collective-permute-start | bytes 24584 | tf_op jit(solution)/shard_map/ppermute | solution.py:20
  186.8 143.9 %copy-start.12 = (f32[1,4,16,256]{3,2,1,0:T(8,128)}, f32[1,4,16,256]{3,2,1,0:T(8,128)S(1)}, u32[]{:S(2)}) copy-start(f32[1,4,16,256]{3,2,1,0:T(8,128)S(1)} %get-tuple-element.96) | copy-start | bytes 196612
  186.8 143.9 %copy-start.14 = (f32[1,4,16,256]{3,2,1,0:T(8,128)}, f32[1,4,16,256]{3,2,1,0:T(8,128)S(1)}, u32[]{:S(2)}) copy-start(f32[1,4,16,256]{3,2,1,0:T(8,128)S(1)} %get-tuple-element.97) | copy-start | bytes 196612
  186.9 143.9 %copy-start.16 = (f32[1,4,16,256]{3,2,1,0:T(8,128)}, f32[1,4,16,256]{3,2,1,0:T(8,128)S(1)}, u32[]{:S(2)}) copy-start(f32[1,4,16,256]{3,2,1,0:T(8,128)S(1)} %get-tuple-element.98) | copy-start | bytes 196612
  187.1 37.4 %collective-permute-start.10 = (f32[2,4,16,1]{3,2,1,0:T(8,128)S(1)}, f32[2,4,16,1]{3,2,1,0:T(8,128)S(1)}, u32[]{:S(2)}, u32[]{:S(2)}) collective-permute-start(f32[2,4,16,1]{3,2,1,0:T(8,128)S(1)} %slice.772), channel_id=1, source_target_pairs={{0,32},{1,33},{2,34},{3,35},{4,36},{5,37},{6,38},{7,39},{8,40},{9,... | collective-permute-start | bytes 1544 | tf_op jit(solution)/shard_map/ppermute | solution.py:20
  209.5 15.0 %collective-permute-start.11 = (f32[2,1,16,256]{3,2,1,0:T(8,128)S(1)}, f32[2,1,16,256]{3,2,1,0:T(8,128)S(1)}, u32[]{:S(2)}, u32[]{:S(2)}) collective-permute-start(f32[2,1,16,256]{3,2,1,0:T(8,128)S(1)} %slice.778), channel_id=1, source_target_pairs={{0,1},{1,2},{2,3},{3,4},{4,5},{5,6},{6,7},{7,8},{8,9},{9,10},{10,1... | collective-permute-start | bytes 98312 | tf_op jit(solution)/shard_map/ppermute | solution.py:20
  214.7 9.9 %collective-permute-start.9 = (f32[2,4,1,256]{3,2,1,0:T(1,128)S(1)}, f32[2,4,1,256]{3,2,1,0:T(1,128)S(1)}, u32[]{:S(2)}, u32[]{:S(2)}) collective-permute-start(f32[2,4,1,256]{3,2,1,0:T(1,128)S(1)} %slice.623), channel_id=1, source_target_pairs={{0,64},{1,65},{2,66},{3,67},{4,68},{5,69},{6,70},{7,71},{8,72},{9,... | collective-permute-start | bytes 24584 | tf_op jit(solution)/shard_map/ppermute | solution.py:20
  225.0 31.0 %collective-permute-start.13 = (f32[2,4,16,1]{3,2,1,0:T(8,128)S(1)}, f32[2,4,16,1]{3,2,1,0:T(8,128)S(1)}, u32[]{:S(2)}, u32[]{:S(2)}) collective-permute-start(f32[2,4,16,1]{3,2,1,0:T(8,128)S(1)} %slice.790), channel_id=1, source_target_pairs={{32,0},{33,1},{34,2},{35,3},{36,4},{37,5},{38,6},{39,7},{40,8},{41... | collective-permute-start | bytes 1544 | tf_op jit(solution)/shard_map/ppermute | solution.py:20
  243.1 12.9 %collective-permute-start.14 = (f32[2,1,16,256]{3,2,1,0:T(8,128)S(1)}, f32[2,1,16,256]{3,2,1,0:T(8,128)S(1)}, u32[]{:S(2)}, u32[]{:S(2)}) collective-permute-start(f32[2,1,16,256]{3,2,1,0:T(8,128)S(1)} %slice.796), channel_id=1, source_target_pairs={{1,0},{2,1},{3,2},{4,3},{5,4},{6,5},{7,6},{8,7},{9,8},{10,9},{11,1... | collective-permute-start | bytes 98312 | tf_op jit(solution)/shard_map/ppermute | solution.py:20
  244.4 11.6 %collective-permute-start.12 = (f32[2,4,1,256]{3,2,1,0:T(1,128)S(1)}, f32[2,4,1,256]{3,2,1,0:T(1,128)S(1)}, u32[]{:S(2)}, u32[]{:S(2)}) collective-permute-start(f32[2,4,1,256]{3,2,1,0:T(1,128)S(1)} %slice.642), channel_id=1, source_target_pairs={{64,0},{65,1},{66,2},{67,3},{68,4},{69,5},{70,6},{71,7},{72,8},{73... | collective-permute-start | bytes 24584 | tf_op jit(solution)/shard_map/ppermute | solution.py:20
  256.2 74.6 %copy-start.21 = (f32[1,4,16,256]{3,2,1,0:T(8,128)}, f32[1,4,16,256]{3,2,1,0:T(8,128)S(1)}, u32[]{:S(2)}) copy-start(f32[1,4,16,256]{3,2,1,0:T(8,128)S(1)} %get-tuple-element.80) | copy-start | bytes 196612
  256.2 74.6 %copy-start.23 = (f32[1,4,16,256]{3,2,1,0:T(8,128)}, f32[1,4,16,256]{3,2,1,0:T(8,128)S(1)}, u32[]{:S(2)}) copy-start(f32[1,4,16,256]{3,2,1,0:T(8,128)S(1)} %get-tuple-element.81) | copy-start | bytes 196612
  256.2 74.6 %copy-start.25 = (f32[1,4,16,256]{3,2,1,0:T(8,128)}, f32[1,4,16,256]{3,2,1,0:T(8,128)S(1)}, u32[]{:S(2)}) copy-start(f32[1,4,16,256]{3,2,1,0:T(8,128)S(1)} %get-tuple-element.82) | copy-start | bytes 196612
  256.4 38.0 %collective-permute-start.16 = (f32[2,4,16,1]{3,2,1,0:T(8,128)S(1)}, f32[2,4,16,1]{3,2,1,0:T(8,128)S(1)}, u32[]{:S(2)}, u32[]{:S(2)}) collective-permute-start(f32[2,4,16,1]{3,2,1,0:T(8,128)S(1)} %slice.806), channel_id=1, source_target_pairs={{0,32},{1,33},{2,34},{3,35},{4,36},{5,37},{6,38},{7,39},{8,40},{9,... | collective-permute-start | bytes 1544 | tf_op jit(solution)/shard_map/ppermute | solution.py:20
  278.9 15.7 %collective-permute-start.17 = (f32[2,1,16,256]{3,2,1,0:T(8,128)S(1)}, f32[2,1,16,256]{3,2,1,0:T(8,128)S(1)}, u32[]{:S(2)}, u32[]{:S(2)}) collective-permute-start(f32[2,1,16,256]{3,2,1,0:T(8,128)S(1)} %slice.812), channel_id=1, source_target_pairs={{0,1},{1,2},{2,3},{3,4},{4,5},{5,6},{6,7},{7,8},{8,9},{9,10},{10,1... | collective-permute-start | bytes 98312 | tf_op jit(solution)/shard_map/ppermute | solution.py:20
  284.6 9.9 %collective-permute-start.15 = (f32[2,4,1,256]{3,2,1,0:T(1,128)S(1)}, f32[2,4,1,256]{3,2,1,0:T(1,128)S(1)}, u32[]{:S(2)}, u32[]{:S(2)}) collective-permute-start(f32[2,4,1,256]{3,2,1,0:T(1,128)S(1)} %slice.659), channel_id=1, source_target_pairs={{0,64},{1,65},{2,66},{3,67},{4,68},{5,69},{6,70},{7,71},{8,72},{9,... | collective-permute-start | bytes 24584 | tf_op jit(solution)/shard_map/ppermute | solution.py:20
  296.9 32.1 %collective-permute-start.19 = (f32[2,4,16,1]{3,2,1,0:T(8,128)S(1)}, f32[2,4,16,1]{3,2,1,0:T(8,128)S(1)}, u32[]{:S(2)}, u32[]{:S(2)}) collective-permute-start(f32[2,4,16,1]{3,2,1,0:T(8,128)S(1)} %slice.824), channel_id=1, source_target_pairs={{32,0},{33,1},{34,2},{35,3},{36,4},{37,5},{38,6},{39,7},{40,8},{41... | collective-permute-start | bytes 1544 | tf_op jit(solution)/shard_map/ppermute | solution.py:20
  315.6 14.2 %collective-permute-start.20 = (f32[2,1,16,256]{3,2,1,0:T(8,128)S(1)}, f32[2,1,16,256]{3,2,1,0:T(8,128)S(1)}, u32[]{:S(2)}, u32[]{:S(2)}) collective-permute-start(f32[2,1,16,256]{3,2,1,0:T(8,128)S(1)} %slice.830), channel_id=1, source_target_pairs={{1,0},{2,1},{3,2},{4,3},{5,4},{6,5},{7,6},{8,7},{9,8},{10,9},{11,1... | collective-permute-start | bytes 98312 | tf_op jit(solution)/shard_map/ppermute | solution.py:20
  316.9 12.2 %collective-permute-start.18 = (f32[2,4,1,256]{3,2,1,0:T(1,128)}, f32[2,4,1,256]{3,2,1,0:T(1,128)}, u32[]{:S(2)}, u32[]{:S(2)}) collective-permute-start(f32[2,4,1,256]{3,2,1,0:T(1,128)} %slice.678), channel_id=1, source_target_pairs={{64,0},{65,1},{66,2},{67,3},{68,4},{69,5},{70,6},{71,7},{72,8},{73... | collective-permute-start | bytes 24584 | tf_op jit(solution)/shard_map/ppermute | solution.py:20
  330.7 12.3 %copy-start.28 = (f32[1,4,16,256]{3,2,1,0:T(8,128)}, f32[1,4,16,256]{3,2,1,0:T(8,128)S(1)}, u32[]{:S(2)}) copy-start(f32[1,4,16,256]{3,2,1,0:T(8,128)S(1)} %get-tuple-element.64) | copy-start | bytes 196612
  330.8 12.3 %copy-start.30 = (f32[1,4,16,256]{3,2,1,0:T(8,128)}, f32[1,4,16,256]{3,2,1,0:T(8,128)S(1)}, u32[]{:S(2)}) copy-start(f32[1,4,16,256]{3,2,1,0:T(8,128)S(1)} %get-tuple-element.65) | copy-start | bytes 196612
  330.8 17.9 %copy-start.32 = (f32[1,4,16,256]{3,2,1,0:T(8,128)}, f32[1,4,16,256]{3,2,1,0:T(8,128)S(1)}, u32[]{:S(2)}) copy-start(f32[1,4,16,256]{3,2,1,0:T(8,128)S(1)} %get-tuple-element.66) | copy-start | bytes 196612
  331.7 38.5 %collective-permute-start.22 = (f32[2,4,16,1]{3,2,1,0:T(8,128)S(1)}, f32[2,4,16,1]{3,2,1,0:T(8,128)S(1)}, u32[]{:S(2)}, u32[]{:S(2)}) collective-permute-start(f32[2,4,16,1]{3,2,1,0:T(8,128)S(1)} %slice.840), channel_id=1, source_target_pairs={{0,32},{1,33},{2,34},{3,35},{4,36},{5,37},{6,38},{7,39},{8,40},{9,... | collective-permute-start | bytes 1544 | tf_op jit(solution)/shard_map/ppermute | solution.py:20
  354.1 16.1 %collective-permute-start.23 = (f32[2,1,16,256]{3,2,1,0:T(8,128)S(1)}, f32[2,1,16,256]{3,2,1,0:T(8,128)S(1)}, u32[]{:S(2)}, u32[]{:S(2)}) collective-permute-start(f32[2,1,16,256]{3,2,1,0:T(8,128)S(1)} %slice.846), channel_id=1, source_target_pairs={{0,1},{1,2},{2,3},{3,4},{4,5},{5,6},{6,7},{7,8},{8,9},{9,10},{10,1... | collective-permute-start | bytes 98312 | tf_op jit(solution)/shard_map/ppermute | solution.py:20
  359.9 10.3 %collective-permute-start.21 = (f32[2,4,1,256]{3,2,1,0:T(1,128)S(1)}, f32[2,4,1,256]{3,2,1,0:T(1,128)S(1)}, u32[]{:S(2)}, u32[]{:S(2)}) collective-permute-start(f32[2,4,1,256]{3,2,1,0:T(1,128)S(1)} %slice.695), channel_id=1, source_target_pairs={{0,64},{1,65},{2,66},{3,67},{4,68},{5,69},{6,70},{7,71},{8,72},{9,... | collective-permute-start | bytes 24584 | tf_op jit(solution)/shard_map/ppermute | solution.py:20
  439.3 12.8 %copy-start.77 = (f32[64,6]{0,1:T(8,128)S(1)}, f32[64,6]{0,1:T(8,128)}, u32[]{:S(2)}) copy-start(f32[64,6]{0,1:T(8,128)} %param.16) | copy-start | bytes 4612
  439.6 14.3 %copy-start.47 = (f32[8,256]{1,0:T(8,128)S(1)}, f32[8,256]{1,0:T(8,128)}, u32[]{:S(2)}) copy-start(f32[8,256]{1,0:T(8,128)} %get-tuple-element.191) | copy-start | bytes 24580
  440.8 10.6 %all-to-all-start = ((f32[4,6,2,8,128]{4,3,2,1,0:T(8,128)}), f32[4,6,2,8,128]{4,3,2,1,0:T(8,128)S(1)}, u32[]{:S(2)}, u32[]{:S(2)}) async-start(f32[4,6,2,8,128]{4,3,2,1,0:T(8,128)} %multiply_add_fusion), calls=%async_computation | async-start | bytes 393216 | tf_op jit(solution)/shard_map/all_to_all | solution.py:140
  456.5 29.0 %copy-start.53 = (f32[8,64]{1,0:T(8,128)S(1)}, f32[8,64]{1,0:T(8,128)}, u32[]{:S(2)}) copy-start(f32[8,64]{1,0:T(8,128)} %get-tuple-element.186) | copy-start | bytes 6148
  456.5 29.0 %copy-start.56 = (f32[8,64]{1,0:T(8,128)S(1)}, f32[8,64]{1,0:T(8,128)}, u32[]{:S(2)}) copy-start(f32[8,64]{1,0:T(8,128)} %get-tuple-element.187) | copy-start | bytes 6148
  458.1 25.6 %all-to-all-start.1 = ((f32[32,1,1024]{2,1,0:T(1,128)}), f32[32,1,1024]{2,1,0:T(1,128)S(1)}, u32[]{:S(2)}, u32[]{:S(2)}) async-start(f32[32,1,1024]{2,1,0:T(1,128)} %reshape.1354), calls=%async_computation.1 | async-start | bytes 262144 | tf_op jit(solution)/shard_map/all_to_all | solution.py:80
  485.8 14.1 %copy-start.41 = (f32[2,64,64]{2,1,0:T(8,128)S(1)}, f32[2,64,64]{2,1,0:T(8,128)}, u32[]{:S(2)}) copy-start(f32[2,64,64]{2,1,0:T(8,128)} %param.17) | copy-start | bytes 98308
  495.6 11.6 %all-to-all-start.2 = ((f32[32,1,1024]{2,1,0:T(1,128)}), f32[32,1,1024]{2,1,0:T(1,128)S(1)}, u32[]{:S(2)}, u32[]{:S(2)}) async-start(f32[32,1,1024]{2,1,0:T(1,128)} %reshape.1356), calls=%async_computation.2 | async-start | bytes 262144 | tf_op jit(solution)/shard_map/all_to_all | solution.py:84
  523.6 23.3 %copy-start.63 = (f32[8,64]{1,0:T(8,128)S(1)}, f32[8,64]{1,0:T(8,128)}, u32[]{:S(2)}) copy-start(f32[8,64]{1,0:T(8,128)} %get-tuple-element.180) | copy-start | bytes 6148
  523.6 23.3 %copy-start.65 = (f32[8,64]{1,0:T(8,128)S(1)}, f32[8,64]{1,0:T(8,128)}, u32[]{:S(2)}) copy-start(f32[8,64]{1,0:T(8,128)} %get-tuple-element.181) | copy-start | bytes 6148
  524.8 20.8 %all-to-all-start.3 = ((f32[32,1,1024]{2,1,0:T(1,128)}), f32[32,1,1024]{2,1,0:T(1,128)S(1)}, u32[]{:S(2)}, u32[]{:S(2)}) async-start(f32[32,1,1024]{2,1,0:T(1,128)} %reshape.1358), calls=%async_computation.3 | async-start | bytes 262144 | tf_op jit(solution)/shard_map/all_to_all | solution.py:80
  547.2 17.9 %copy-start.42 = (f32[2,64,64]{2,1,0:T(8,128)S(1)}, f32[2,64,64]{2,1,0:T(8,128)}, u32[]{:S(2)}) copy-start(f32[2,64,64]{2,1,0:T(8,128)} %param.17) | copy-start | bytes 98308
  557.0 15.3 %all-to-all-start.4 = ((f32[32,1,1024]{2,1,0:T(1,128)}), f32[32,1,1024]{2,1,0:T(1,128)S(1)}, u32[]{:S(2)}, u32[]{:S(2)}) async-start(f32[32,1,1024]{2,1,0:T(1,128)} %reshape.1360), calls=%async_computation.4 | async-start | bytes 262144 | tf_op jit(solution)/shard_map/all_to_all | solution.py:84
  592.6 16.9 %copy-start.64 = (f32[8,64]{1,0:T(8,128)S(1)}, f32[8,64]{1,0:T(8,128)}, u32[]{:S(2)}) copy-start(f32[8,64]{1,0:T(8,128)} %get-tuple-element.180) | copy-start | bytes 6148
  592.6 16.9 %copy-start.66 = (f32[8,64]{1,0:T(8,128)S(1)}, f32[8,64]{1,0:T(8,128)}, u32[]{:S(2)}) copy-start(f32[8,64]{1,0:T(8,128)} %get-tuple-element.181) | copy-start | bytes 6148
  609.8 11.2 %copy-start.43 = (f32[2,64,64]{2,1,0:T(8,128)S(1)}, f32[2,64,64]{2,1,0:T(8,128)}, u32[]{:S(2)}) copy-start(f32[2,64,64]{2,1,0:T(8,128)} %param.17) | copy-start | bytes 98308
  616.6 11.7 %all-to-all-start.6 = ((f32[32,1,1024]{2,1,0:T(1,128)}), f32[32,1,1024]{2,1,0:T(1,128)S(1)}, u32[]{:S(2)}, u32[]{:S(2)}) async-start(f32[32,1,1024]{2,1,0:T(1,128)} %reshape.1364), calls=%async_computation.6 | async-start | bytes 262144 | tf_op jit(solution)/shard_map/all_to_all | solution.py:84
  642.7 9.2 copy-start.38
  642.7 9.3 copy-start.40
  645.3 13.9 %all-to-all-start.7 = ((f32[32,1,1024]{2,1,0:T(1,128)}), f32[32,1,1024]{2,1,0:T(1,128)S(1)}, u32[]{:S(2)}, u32[]{:S(2)}) async-start(f32[32,1,1024]{2,1,0:T(1,128)} %reshape.1366), calls=%async_computation.7 | async-start | bytes 262144 | tf_op jit(solution)/shard_map/all_to_all | solution.py:80
  651.9 314.1 %all-reduce.3.cloned.1.call-start = ((), (), s32[]{:S(2)}) async-start(), calls=%async_computation.9 | async-start | bytes 16777216 | tf_op jit(solution)/shard_map/psum | solution.py:201
  652.0 8.5 copy-start.54
  652.0 8.5 copy-start.57
  652.0 8.7 copy-start.36
  691.5 11.2 %all-to-all-start.8 = ((f32[32,1,1024]{2,1,0:T(1,128)}), f32[32,1,1024]{2,1,0:T(1,128)S(1)}, u32[]{:S(2)}, u32[]{:S(2)}) async-start(f32[32,1,1024]{2,1,0:T(1,128)} %reshape.1368), calls=%async_computation.8 | async-start | bytes 262144 | tf_op jit(solution)/shard_map/all_to_all | solution.py:84
  695.4 8.4 copy-start.52
  695.4 8.8 copy-start.49
  (51 other events, 209.9 us)
Sparse Core Ops, SparseCore 0:
  667.5 298.4 all-reduce.2
where the time goes:
time: 993 us; the launch traced here: 982 us
  local copies, waits for them, and re-layouts  352 us (35%)
  blocking collectives  212 us (21%)
  starting transfers between devices  128 us (13%)
  matrix products  107 us (11%)
  waiting for transfers between devices  102 us (10%)
  other arithmetic  62.9 us (6%)
  between operations  17.7 us (2%)
    psum x1, blocking collectives, local(): lax.psum((lift_grad, jnp.stack(pointwise_grads), project_grad, local_loss...  182 us
    another operation x42, local copies, waits for them, and re-layouts, curl_of(): return jnp.stack([d_zy - d_yz, d_xz - d_zx, d_yx - d_xy])  176 us
    psum x1, waiting for transfers between devices, local(): spectral_grad = lax.psum(jnp.stack(mode_grads), ('role', 'rep'))  76.4 us
    ppermute x24, starting transfers between devices, passed_along(): return lax.ppermute(value, axis, pairs)  73.9 us
    concatenate x21, local copies, waits for them, and re-layouts, forward_diff(): return jnp.concatenate([remainder, border], axis=along) - grid_field  37.8 us
    all_to_all x3, starting transfers between devices, spectral_pass(): pencil = lax.all_to_all(b, 'tile', split_axis=2, concat_axis=1, tiled=True)  28.7 us
    unnamed x181, local copies, waits for them, and re-layouts  23 us
    squeeze x3, local copies, waits for them, and re-layouts, local(): electric = fields[0]  22.5 us
  transfers between devices with their start and end apart: 33, of which 8 were waited for; matrix products, arithmetic and copies ran while one was open for 34% of the time, Pallas kernels for 0%

commit v1 on v0

v1 whole, which is shorter than its diff:
```python
import functools
import math

import jax
import jax.numpy as jnp
import ml_dtypes
import numpy as np
from jax import lax
from jax.experimental import pallas as pl
from jax.experimental.pallas import tpu as pltpu
from jax.sharding import PartitionSpec as P

STEPS = 4
MODES = 8
LAYERS = 2
STEP_TIME = 0.5
PRECISE = lax.Precision.HIGHEST
F32 = jnp.float32
BF16 = jnp.bfloat16
NN = (((1,), (0,)), ((), ()))
NT = (((1,), (1,)), ((), ()))
TN = (((0,), (0,)), ((), ()))
ROOM = 56 * 1024 * 1024
GROUP = ("role", "rep")
EVERY = ("role", "rep", "tile")
SX, SY, SZ = 64, 16, 256
CELLS = SY * SZ
TILES = 32


def basis(length):
    frequency = np.arange(MODES)[:, None]
    position = np.arange(length)[None, :]
    angles = 2.0 * np.pi * ((frequency * position) % length) / length
    return np.concatenate([np.cos(angles), np.sin(angles)], axis=0) * math.sqrt(2.0 / length)


def split_const(table):
    table = table.astype(np.float32)
    high = table.astype(ml_dtypes.bfloat16)
    low = (table - high.astype(np.float32)).astype(ml_dtypes.bfloat16)
    return high, low


def both_const(table):
    return np.stack(split_const(table))


TABLE_X, TABLE_Y, TABLE_Z = basis(SX), basis(SY), basis(SZ)
KRON_X = both_const(
    np.einsum("ptx,mn->xmptn", TABLE_X.reshape(16, TILES, 2), np.eye(8)).reshape(256, 256)
)
KRON_XT = np.ascontiguousarray(KRON_X.transpose(0, 2, 1))
KRON_Y = both_const(np.einsum("jy,kl->jkyl", TABLE_Y, np.eye(16)).reshape(256, 256))
KRON_YT = np.ascontiguousarray(KRON_Y.transpose(0, 2, 1))
KRON_Y_HALF = np.stack(
    [
        both_const(
            np.einsum("jy,kl->jkyl", TABLE_Y[:, r * 8 : r * 8 + 8], np.eye(16)).reshape(256, 128)
        )
        for r in range(2)
    ]
)
Z_HIGH, Z_LOW = split_const(TABLE_Z)
Z_ROWS = np.concatenate([Z_HIGH, Z_LOW], axis=0)
Z_COLS = np.concatenate([Z_HIGH.T, Z_HIGH.T, Z_LOW.T], axis=1)
Z_HALF = np.stack([Z_ROWS[:, r * 128 : r * 128 + 128] for r in range(2)])
POOL_Z = np.kron(np.eye(128), np.full((2, 1), 0.125)).astype(np.float32)


def halves(value):
    high = value.astype(BF16)
    return high, (value - high.astype(F32)).astype(BF16)


def dot(a, b, dims=NN):
    return lax.dot_general(a, b, dims, preferred_element_type=F32)


def dot3(a, b, dims=NN):
    return dot(a[0], b[0], dims) + dot(a[0], b[1], dims) + dot(a[1], b[0], dims)


def lanes_of(shape):
    return lax.broadcasted_iota(jnp.int32, shape, len(shape) - 1)


def rows_of(shape):
    return lax.broadcasted_iota(jnp.int32, shape, len(shape) - 2)


def square_weight(matrix):
    high, low = halves(matrix)
    one = jnp.concatenate([high, low], axis=1)
    return jnp.concatenate([one, one], axis=0)


def rows_times(value, weight):
    high, low = halves(value)
    out = dot(jnp.concatenate([high, low], axis=1), weight)
    return out[:, :128] + out[:, 128:]


def vmem(shape, dtype=F32):
    return pltpu.VMEM(shape, dtype)


def params():
    return pltpu.CompilerParams(vmem_limit_bytes=ROOM)


def full(shape):
    return pl.BlockSpec(shape, lambda *_: (0,) * len(shape))


SMEM = pl.BlockSpec(memory_space=pltpu.SMEM)


def shape_of(*shape):
    return jax.ShapeDtypeStruct(shape, F32)


def pack_kernel(fields, material, packed, strip, left, right):
    packed[0:6] = fields[...]
    packed[6] = material[...].astype(F32)
    left[...] = jnp.zeros_like(left)
    right[...] = jnp.zeros_like(right)
    left[0:448] = packed[:, :, :, 0:128].reshape(448, 128)
    right[0:448] = packed[:, :, :, 128:256].reshape(448, 128)
    for b in range(4):
        rows = pl.ds(b * 128, 128)
        strip[0:4, rows] = jnp.transpose(left[rows, :])[0:4]
        strip[4:8, rows] = jnp.transpose(right[rows, :])[124:128]


def pack(fields, material):
    return pl.pallas_call(
        pack_kernel,
        out_shape=[shape_of(7, 4, 16, 256), shape_of(8, 512)],
        scratch_shapes=[vmem((512, 128)), vmem((512, 128))],
        compiler_params=params(),
        name="pack",
    )(fields, material)


def leap_kernel(
    place,
    plan,
    coefs,
    own0,
    own1,
    low0,
    low1,
    high0,
    high1,
    strip_own0,
    strip_own1,
    strip_low0,
    strip_low1,
    strip_high0,
    strip_high1,
    pool,
    kron,
    z_half,
    out_fields,
    out_pieces,
    out_coef,
    grid_f,
    keep,
    gain,
    dt_mask,
    edge0,
    edge1,
    sums0,
    sums1,
    reduced,
    chosen,
    staged,
):
    role, rep, tile = place[0], place[1], place[2]
    shape8 = (8, 384)
    row8 = rows_of(shape8)
    top = jnp.where((row8 < 4) & (role == 0), 1.0, 0.0)
    bottom = jnp.where((row8 >= 4) & (role == 1), 1.0, 0.0)

    def column(strip_ref, edge):
        strip = strip_ref[...]
        row = rows_of((8, 512))
        first = jnp.where((row < 4) & (rep == 0), strip, 0.0)
        last = jnp.where((row >= 4) & (rep == 1), strip, 0.0)
        whole = jnp.concatenate([first, jnp.zeros((112, 512), F32), last], axis=0)
        for b in range(4):
            edge[b * 128 : (b + 1) * 128, :] = jnp.transpose(whole[:, b * 128 : (b + 1) * 128])

    sources = (
        (low0, low1, strip_low0, strip_low1),
        (own0, own1, strip_own0, strip_own1),
        (high0, high1, strip_high0, strip_high1),
    )
    for number, (mine, mate, strip_mine, strip_mate) in enumerate(sources):
        column(strip_mine, edge0)
        column(strip_mate, edge1)

        def fill(n, carry, mine=mine, mate=mate, number=number):
            c = n // 4
            i = n % 4
            at = pl.multiple_of(n * 16, 16)
            plane = jnp.concatenate([mine[c, i], edge0[pl.ds(at, 16), :]], axis=1)
            other = jnp.concatenate([mate[c, i], edge1[pl.ds(at, 16), :]], axis=1)
            halo = other[0:8] * top + other[8:16] * bottom
            grid_f[c, 4 * number + i] = jnp.concatenate([plane, halo], axis=0)
            return carry

        lax.fori_loop(0, 28, fill, 0)

    row = rows_of((24, 384))
    lane = lanes_of((24, 384))
    row_ok = (row < 16) | ((row < 20) & (role == 0)) | ((row >= 20) & (role == 1))
    lane_ok = (lane < 256) | ((lane < 320) & (rep == 0)) | ((lane >= 320) & (rep == 1))
    inside = jnp.where(row_ok & lane_ok, 1.0, 0.0)
    dt_mask[...] = inside * STEP_TIME
    below = jnp.where(tile > 0, 1.0, 0.0)
    above = jnp.where(tile < TILES - 1, 1.0, 0.0)

    def media(p, carry):
        kind = grid_f[6, p]
        level = inside * jnp.where(p >= 8, above, 1.0)

        def choose(base):
            return jnp.where(
                kind < 0.5,
                coefs[base],
                jnp.where(
                    kind < 1.5,
                    coefs[base + 1],
                    jnp.where(kind < 2.5, coefs[base + 2], coefs[base + 3]),
                ),
            )

        keep[p] = choose(0)
        gain[p] = choose(4) * level
        return carry

    lax.fori_loop(1, 11, media, 0)

    def back(value, axis):
        return pltpu.roll(value, value.shape[axis] - 1, axis)

    def step_h(p, carry):
        ex, ey, ez = grid_f[0, p], grid_f[1, p], grid_f[2, p]
        s = dt_mask[...] * jnp.where(p < 4, below, 1.0)
        d_zy = back(ez, 0) - ez
        d_yz = back(ey, 1) - ey
        d_xz = back(ex, 1) - ex
        d_zx = grid_f[2, p + 1] - ez
        d_yx = grid_f[1, p + 1] - ey
        d_xy = back(ex, 0) - ex
        grid_f[3, p] = grid_f[3, p] - s * (d_zy - d_yz)
        grid_f[4, p] = grid_f[4, p] - s * (d_xz - d_zx)
        grid_f[5, p] = grid_f[5, p] - s * (d_yx - d_xy)
        return carry

    def step_e(p, carry):
        hx, hy, hz = grid_f[3, p], grid_f[4, p], grid_f[5, p]
        k, g = keep[p], gain[p]
        d_zy = hz - pltpu.roll(hz, 1, 0)
        d_yz = hy - pltpu.roll(hy, 1, 1)
        d_xz = hx - pltpu.roll(hx, 1, 1)
        d_zx = hz - grid_f[5, p - 1]
        d_yx = hy - grid_f[4, p - 1]
        d_xy = hx - pltpu.roll(hx, 1, 0)
        grid_f[0, p] = k * grid_f[0, p] + g * (d_zy - d_yz)
        grid_f[1, p] = k * grid_f[1, p] + g * (d_xz - d_zx)
        grid_f[2, p] = k * grid_f[2, p] + g * (d_yx - d_xy)
        return carry

    sums0[...] = jnp.zeros_like(sums0)
    sums1[...] = jnp.zeros_like(sums1)
    for step in range(STEPS):
        lax.fori_loop(step, 11 - step, step_h, 0)
        lax.fori_loop(1 + step, 11 - step, step_e, 0)
        for x in range(2):
            for c in range(6):
                at = (x * 8 + c) * 16
                pair = grid_f[c, 4 + 2 * x, 0:16, 0:256] + grid_f[c, 5 + 2 * x, 0:16, 0:256]
                sums0[at : at + 16, :] = pair[:, 0:128]
                sums1[at : at + 16, :] = pair[:, 128:256]
        for part, sums in enumerate((sums0, sums1)):
            staged[:, part * 128 : (part + 1) * 128] = (
                sums[pl.ds(0, 128, stride=2), :] + sums[pl.ds(1, 128, stride=2), :]
            )
        reduced[step] = lax.dot_general(
            staged[...], pool[...], NN, precision=PRECISE, preferred_element_type=F32
        )
    for c in range(6):
        out_fields[c] = grid_f[c, 4:8, 0:16, 0:256]

    me = role * 2 + rep
    for d in range(4):
        own = plan[me ^ d] - 1
        out_pieces[d, 0:128] = reduced[own]
        out_pieces[d, 128:256] = reduced[STEPS - 1]
        chosen[d * 128 : (d + 1) * 128] = reduced[plan[d] - 1]
    parts = []
    z_rows = z_half[rep]
    for y in range(8):
        high, low = halves(chosen[pl.ds(y, 64, stride=8), :])
        out = dot(z_rows, high, NT)
        parts.append(out[0:16] + out[16:32] + dot(z_rows[0:16], low, NT))
    mixed = jnp.concatenate(parts, axis=0)
    coef = dot3((kron[role, 0], kron[role, 1]), halves(mixed))
    out_coef[...] = jnp.zeros_like(out_coef)
    for s in range(4):
        out_coef[s, :, 0:16] = coef[:, s * 16 : (s + 1) * 16]


def leapfrog(place, plan, coefs, blocks):
    count = len(blocks)
    return pl.pallas_call(
        leap_kernel,
        out_shape=[shape_of(6, 4, 16, 256), shape_of(4, 256, 128), shape_of(4, 256, 128)],
        in_specs=[SMEM, SMEM, SMEM] + [pl.BlockSpec(memory_space=pltpu.VMEM)] * (count + 3),
        scratch_shapes=[
            vmem((7, 12, 24, 384)),
            vmem((12, 24, 384)),
            vmem((12, 24, 384)),
            vmem((24, 384)),
            vmem((512, 128)),
            vmem((512, 128)),
            vmem((256, 128)),
            vmem((256, 128)),
            vmem((4, 128, 128)),
            vmem((512, 128)),
            vmem((128, 256)),
        ],
        compiler_params=params(),
        name="leapfrog",
    )(place, plan, coefs, *blocks, jnp.asarray(POOL_Z), jnp.asarray(KRON_Y_HALF), jnp.asarray(Z_HALF))


def prep_kernel(place, piece0, piece1, piece2, piece3, weight, out_pre, out_in, out_target):
    me = place[0] * 2 + place[1]
    weights = square_weight(weight[...])
    lane = lanes_of((128, 128))
    for d, piece in enumerate((piece0, piece1, piece2, piece3)):
        source = me ^ d
        role, rep = source // 2, source % 2
        for kind in range(2):
            whole = jnp.concatenate(
                [piece[pl.ds(kind * 128 + y, 16, stride=8), :] for y in range(8)], axis=0
            )
            turned = jnp.transpose(whole)
            for y in range(8):
                at = pl.multiple_of((role * 8 + y) * 256 + rep * 128, 128)
                own = turned if y == 0 else pltpu.roll(turned, 128 - 16 * y, 1)
                own = jnp.where(lane < 16, own, 0.0)
                if kind == 0:
                    out_in[pl.ds(at, 128), :] = own
                    out_pre[pl.ds(at, 128), :] = rows_times(own, weights)
                else:
                    out_target[pl.ds(at, 128), :] = own


def prepare(place, pieces, weight):
    return pl.pallas_call(
        prep_kernel,
        out_shape=[shape_of(CELLS, 128)] * 3,
        in_specs=[SMEM] + [pl.BlockSpec(memory_space=pltpu.VMEM)] * 5,
        compiler_params=params(),
        name="prepare",
    )(place, *pieces, weight)


GELU_A = math.sqrt(2.0 / math.pi)
GELU_B = 0.044715


def gelu_both(value):
    square = value * value
    t = jnp.tanh(GELU_A * value * (1.0 + GELU_B * square))
    half = 0.5 * (1.0 + t)
    slope = half + 0.5 * value * (1.0 - t * t) * (GELU_A * (1.0 + 3.0 * GELU_B * square))
    return value * half, slope


def open_cells(spectrum, kron_t, c_scr):
    c_scr[...] = dot3((kron_t[0], kron_t[1]), halves(spectrum[...]))


def cells_from(c_scr, z_cols, y):
    high, low = halves(c_scr[pl.ds(pl.multiple_of(y * 16, 16), 16), :])
    return dot(z_cols[...], jnp.concatenate([high, low, high], axis=0))


def cells_to(value, z_rows, d_scr, y):
    high, low = halves(value)
    out = dot(z_rows[...], jnp.concatenate([high, low], axis=1))
    d_scr[pl.ds(pl.multiple_of(y * 16, 16), 16), :] = (
        out[0:16, 0:128] + out[0:16, 128:256] + out[16:32, 0:128]
    )


def close_cells(kron, d_scr, out_coef):
    out_coef[...] = dot3((kron[0], kron[1]), halves(d_scr[...]))


BLOCK_Y = 4


def each_y(step, body):
    for n in range(BLOCK_Y):
        body(step * BLOCK_Y + n, pl.ds(n * SZ, SZ))


def cells0_kernel(spectrum, pre, kron, kron_t, z_rows, z_cols, out_coef, out_h, out_slope, c_scr, d_scr):
    step = pl.program_id(0)

    @pl.when(step == 0)
    def _():
        open_cells(spectrum, kron_t, c_scr)

    def body(y, rows):
        hidden, slope = gelu_both(cells_from(c_scr, z_cols, y) + pre[rows, :])
        out_h[rows, :] = hidden
        out_slope[rows, :] = slope
        cells_to(hidden, z_rows, d_scr, y)

    each_y(step, body)

    @pl.when(step == pl.num_programs(0) - 1)
    def _():
        close_cells(kron, d_scr, out_coef)


def cells1_kernel(
    scale,
    spectrum,
    h1,
    target,
    w_point,
    w_proj,
    w_proj_t,
    kron,
    kron_t,
    z_rows,
    z_cols,
    out_coef,
    out_pre,
    out_h,
    out_err,
    out_loss,
    c_scr,
    d_scr,
    wide,
):
    step = pl.program_id(0)

    @pl.when(step == 0)
    def _():
        open_cells(spectrum, kron_t, c_scr)
        wide[0] = square_weight(w_point[...])
        wide[1] = square_weight(w_proj[...])
        wide[2] = square_weight(w_proj_t[...])
        out_loss[...] = jnp.zeros_like(out_loss)

    def body(y, rows):
        value = cells_from(c_scr, z_cols, y) + rows_times(h1[rows, :], wide[0])
        hidden, slope = gelu_both(value)
        err = rows_times(hidden, wide[1]) - target[rows, :]
        out_loss[...] += jnp.sum((err * err).reshape(SZ // 8, 8, 128), axis=0)
        err = err * scale
        grad = rows_times(err, wide[2]) * slope
        out_h[rows, :] = hidden
        out_err[rows, :] = err
        out_pre[rows, :] = grad
        cells_to(grad, z_rows, d_scr, y)

    each_y(step, body)

    @pl.when(step == pl.num_programs(0) - 1)
    def _():
        close_cells(kron, d_scr, out_coef)


def cells2_kernel(
    spectrum, grad1, slope0, w_point, kron, kron_t, z_rows, z_cols, out_coef, out_pre, c_scr, d_scr, wide
):
    step = pl.program_id(0)

    @pl.when(step == 0)
    def _():
        open_cells(spectrum, kron_t, c_scr)
        wide[...] = square_weight(w_point[...])

    def body(y, rows):
        value = cells_from(c_scr, z_cols, y) + rows_times(grad1[rows, :], wide[...])
        grad = value * slope0[rows, :]
        out_pre[rows, :] = grad
        cells_to(grad, z_rows, d_scr, y)

    each_y(step, body)

    @pl.when(step == pl.num_programs(0) - 1)
    def _():
        close_cells(kron, d_scr, out_coef)


def cell_call(kernel, name, spectrum, streams, weights, n_out, loss=False, wide=None):
    block = pl.BlockSpec((BLOCK_Y * SZ, 128), lambda g: (g, 0))
    consts = (KRON_Y, KRON_YT, Z_ROWS, Z_COLS)
    out_shape = [shape_of(256, 128)] + [shape_of(CELLS, 128)] * n_out
    out_specs = [full((256, 128))] + [block] * n_out
    if loss:
        out_shape.append(shape_of(8, 128))
        out_specs.append(full((8, 128)))
    scratch = [vmem((256, 128)), vmem((256, 128))]
    if wide is not None:
        scratch.append(vmem(wide, BF16))
    return pl.pallas_call(
        kernel,
        grid=(SY // BLOCK_Y,),
        out_shape=out_shape,
        in_specs=[full((256, 128))]
        + [block] * len(streams)
        + [full((128, 128))] * len(weights)
        + [full(c.shape) for c in consts],
        out_specs=out_specs,
        scratch_shapes=scratch,
        compiler_params=params(),
        name=name,
    )(spectrum, *streams, *weights, *[jnp.asarray(c) for c in consts])


def pair_up(rows, low_lanes):
    picked = jnp.where(low_lanes, rows[0:128], rows[128:256])
    return picked + pltpu.roll(picked, 64, 1)


def mix_forward(a_scr, b_scr, mask, weights, step):
    at = pl.multiple_of(step * 16, 16)
    own = halves(a_scr[pl.ds(at, 16), 0:64])
    row, lane = rows_of((16, 256)), lanes_of((16, 256))
    total = jnp.zeros((16, 256), F32)
    for q in range(4):
        out = dot3(own, halves(weights[q * 256 : (q + 1) * 256, :]), NT)
        total = total + jnp.where(row == 4 * q + lane // 64, out, 0.0)
    folded = total[:, 0:128] + total[:, 128:256]
    folded = folded + pltpu.roll(folded, 64, 1)
    b_scr[pl.ds(at, 16), :] = folded * mask[pl.ds(at, 16), :]


def mix_backward(g_scr, b_scr, mask, weights, step):
    at = pl.multiple_of(step * 16, 16)
    one = g_scr[pl.ds(at, 16), :]
    wide = jnp.concatenate([one, one], axis=1)
    row, lane = rows_of((16, 256)), lanes_of((16, 256))
    total = jnp.zeros((16, 64), F32)
    for q in range(4):
        own = jnp.where(row == 4 * q + lane // 64, wide, 0.0)
        total = total + dot3(halves(own), halves(weights[q * 256 : (q + 1) * 256, :]))
    masked = total * mask[pl.ds(at, 16), 0:64]
    b_scr[pl.ds(at, 16), 0:64] = masked
    b_scr[pl.ds(at, 16), 64:128] = masked


def close_modes(b_scr, kron_t, out):
    both = b_scr[...]
    low = lanes_of((128, 128)) < 64
    blocks = jnp.concatenate([jnp.where(low, both, 0.0), jnp.where(low, 0.0, both)], axis=0)
    out[...] = dot3((kron_t[0], kron_t[1]), halves(blocks))


def modes_first_kernel(coef, mask, lift, weights, kron, kron_t, out, out_in, out_a, a_scr, b_scr):
    step = pl.program_id(0)

    @pl.when(step == 0)
    def _():
        value = coef[0] + coef[1] + coef[2] + coef[3]
        rows = dot3((kron[0], kron[1]), halves(value))
        picked = jnp.where(lanes_of((128, 128)) < 8, rows[0:128], rows[128:256]) * mask[...]
        out_in[...] = picked
        lifted = dot3(halves(picked), halves(lift[...]))
        a_scr[...] = lifted
        out_a[...] = lifted

    mix_forward(a_scr, b_scr, mask, weights, step)

    @pl.when(step == pl.num_programs(0) - 1)
    def _():
        close_modes(b_scr, kron_t, out)


def modes_forward_kernel(coef, mask, weights, kron, kron_t, out, out_a, a_scr, b_scr):
    step = pl.program_id(0)

    @pl.when(step == 0)
    def _():
        rows = dot3((kron[0], kron[1]), halves(coef[...]))
        a = pair_up(rows, lanes_of((128, 128)) < 64) * mask[...]
        a_scr[...] = a
        out_a[...] = a

    mix_forward(a_scr, b_scr, mask, weights, step)

    @pl.when(step == pl.num_programs(0) - 1)
    def _():
        close_modes(b_scr, kron_t, out)


def modes_backward_kernel(coef, mask, saved, weights, kron, kron_t, out, out_pair, g_scr, b_scr):
    step = pl.program_id(0)

    @pl.when(step == 0)
    def _():
        rows = dot3((kron[0], kron[1]), halves(coef[...]))
        low = lanes_of((128, 128)) < 64
        g = pair_up(rows, low) * mask[...]
        g_scr[...] = g
        out_pair[...] = jnp.where(low, g, saved[...])

    mix_backward(g_scr, b_scr, mask, weights, step)

    @pl.when(step == pl.num_programs(0) - 1)
    def _():
        close_modes(b_scr, kron_t, out)


def modes_last_kernel(
    coef, mask, saved, inputs, point, weights, kron, kron_t, out_late, out_pair, g_scr, b_scr
):
    step = pl.program_id(0)

    @pl.when(step == 0)
    def _():
        rows = dot3((kron[0], kron[1]), halves(coef[...]))
        low = lanes_of((128, 128)) < 64
        g = pair_up(rows, low) * mask[...]
        g_scr[...] = g
        out_pair[...] = jnp.where(low, g, saved[...])

    mix_backward(g_scr, b_scr, mask, weights, step)

    @pl.when(step == pl.num_programs(0) - 1)
    def _():
        turned = jnp.transpose(inputs[...])[0:16]
        lift = dot3(halves(turned), halves(b_scr[...]))
        lift = lift[0:8] + lift[8:16]
        direct = point[0:8, :] + pltpu.roll(point[8:16, :], 64, 1)
        out_late[...] = jnp.where(lanes_of((8, 128)) < 64, lift, pltpu.roll(direct, 64, 1))


def mode_call(kernel, name, layer, smalls, weights, outs):
    consts = (KRON_X, KRON_XT)
    return pl.pallas_call(
        kernel,
        grid=(8,),
        out_shape=[shape_of(*o) for o in outs],
        in_specs=[full(v.shape) for v in smalls]
        + [pl.BlockSpec((None, None, 1024, 64), lambda m: (layer, m, 0, 0))]
        + [full(c.shape) for c in consts],
        out_specs=[full(o) for o in outs],
        scratch_shapes=[vmem((128, 128)), vmem((128, 128))],
        compiler_params=params(),
        name=name,
    )(*smalls, weights, *[jnp.asarray(c) for c in consts])


def outer_kernel(pair0, pair1, pair2, pair3, out):
    blocks = [p[...] for p in (pair0, pair1, pair2, pair3)]
    turned = [jnp.transpose(b)[0:64] for b in blocks]
    for r in range(16):
        total = None
        for b, t in zip(blocks, turned):
            term = t[:, r : r + 1] * b[r : r + 1, 64:128]
            total = term if total is None else total + term
        out[r] = total


def outer_products(pairs):
    block = pl.BlockSpec((None, 16, 128), lambda l, m: (l, m, 0))
    return pl.pallas_call(
        outer_kernel,
        grid=(LAYERS, 8),
        out_shape=shape_of(LAYERS, 8, 16, 64, 64),
        in_specs=[block] * 4,
        out_specs=pl.BlockSpec((None, None, 16, 64, 64), lambda l, m: (l, m, 0, 0, 0)),
        compiler_params=params(),
        name="outer",
    )(*pairs)


def passed(value, axis, by):
    length = lax.axis_size(axis)
    return lax.ppermute(value, axis, [(i, i + by) for i in range(length) if 0 <= i + by < length])


def across(value, axis):
    return lax.ppermute(value, axis, [(0, 1), (1, 0)])


def diagonal(value, by):
    pairs = []
    for q in range(2):
        for t in range(TILES):
            if 0 <= t + by < TILES:
                pairs.append((q * TILES + t, (1 - q) * TILES + t + by))
    return lax.ppermute(value, ("rep", "tile"), pairs)


def xor_group(value, d):
    return lax.ppermute(value, GROUP, [(i, i ^ d) for i in range(4)])


def parity_blocks(matrix):
    zero = jnp.zeros_like(matrix)
    return jnp.concatenate(
        [jnp.concatenate([matrix, zero], axis=1), jnp.concatenate([zero, matrix], axis=1)], axis=0
    )


def mode_masks(mode_counts):
    row = jnp.arange(128, dtype=jnp.int32)
    pair = lax.axis_index("tile") * 8 + row // 16
    masks = []
    for layer in range(LAYERS):
        kept = (
            (row % 8 < mode_counts[layer, 0])
            & (pair // 16 % 8 < mode_counts[layer, 1])
            & (pair % 8 < mode_counts[layer, 2])
        )
        masks.append(jnp.broadcast_to(kept.astype(F32)[:, None], (128, 128)))
    return masks


def local(
    fields,
    material,
    permittivity,
    conductivity,
    plan,
    mode_counts,
    lift_weight,
    pointwise,
    spectral_weight,
    project_weight,
):
    damping = conductivity * (0.5 * STEP_TIME) / permittivity
    coefs = jnp.concatenate(
        [(1.0 - damping) / (1.0 + damping), STEP_TIME / (permittivity * (1.0 + damping))]
    )
    place = jnp.stack([lax.axis_index("role"), lax.axis_index("rep"), lax.axis_index("tile")])
    weights = spectral_weight.reshape(LAYERS, 8, 1024, 64)

    packed, strip = pack(fields.reshape(6, 4, 16, 256), material)
    low0, high0 = passed(packed, "tile", 1), passed(packed, "tile", -1)
    strip_own0 = across(strip, "rep")
    strip_low0, strip_high0 = diagonal(strip, 1), diagonal(strip, -1)
    blocks = []
    for value in (packed, low0, high0, strip_own0, strip_low0, strip_high0):
        blocks += [value, across(value, "role")]
    new_fields, pieces, coef = leapfrog(place, plan, coefs, blocks)

    masks = mode_masks(mode_counts)
    lift8 = jnp.pad(lift_weight.T, ((0, 2), (0, 0)))
    lift16 = jnp.concatenate([lift8, lift8], axis=0)
    lift_pad = jnp.pad(lift16, ((0, 112), (0, 64)))
    first8 = jnp.dot(lift8, pointwise[0].T, precision=PRECISE)
    first = jnp.pad(parity_blocks(first8), ((0, 112), (0, 0)))
    point1 = parity_blocks(pointwise[1])
    proj8 = jnp.pad(project_weight, ((0, 2), (0, 0)))
    proj_t = jnp.pad(parity_blocks(proj8), ((0, 112), (0, 0)))

    coef = lax.all_to_all(coef.reshape(128, 8, 128), EVERY, 0, 0, tiled=True)
    received = [pieces[0]] + [xor_group(pieces[d], d) for d in range(1, 4)]
    pre0, inputs, target = prepare(place, received, first)

    def swap(value):
        value = value.reshape(TILES, 8, 128)
        return lax.all_to_all(value, "tile", 0, 0, tiled=True).reshape(256, 128)

    spectrum, a_in, a0 = mode_call(
        modes_first_kernel,
        "modes_first",
        0,
        (coef.reshape(4, 256, 128), masks[0], lift_pad),
        weights,
        ((256, 128), (128, 128), (128, 128)),
    )
    a0 = jnp.concatenate([a0[:, 0:64], a0[:, 0:64]], axis=1)
    coef, h1, slope0 = cell_call(cells0_kernel, "cells0", swap(spectrum), (pre0,), (), 2)
    spectrum, a1 = mode_call(
        modes_forward_kernel,
        "modes_forward",
        1,
        (swap(coef), masks[1]),
        weights,
        ((256, 128), (128, 128)),
    )
    norm_count = 6.0 * SX * SY * SZ * plan.shape[0]
    coef, grad1, h2, err, loss = cell_call(
        functools.partial(cells1_kernel, 2.0 / norm_count),
        "cells1",
        swap(spectrum),
        (h1, target),
        (point1.T, proj_t.T, proj_t),
        3,
        loss=True,
        wide=(3, 256, 256),
    )
    spectrum, pair1 = mode_call(
        modes_backward_kernel,
        "modes_backward",
        1,
        (swap(coef), masks[1], a1),
        weights,
        ((256, 128), (128, 128)),
    )
    coef, grad0 = cell_call(
        cells2_kernel,
        "cells2",
        swap(spectrum),
        (grad1, slope0),
        (point1,),
        1,
        wide=(256, 256),
    )

    def over_cells(a, b):
        return lax.dot_general(a, b, TN, precision=PRECISE, preferred_element_type=F32)

    point_blocks = over_cells(grad1, h1)
    point_grad1 = point_blocks[0:64, 0:64] + point_blocks[64:128, 64:128]
    proj_blocks = over_cells(err, h2)
    proj_grad = proj_blocks[0:6, 0:64] + proj_blocks[8:14, 64:128]
    point_grad1, proj_grad, loss = lax.psum(
        (point_grad1, proj_grad, jnp.sum(loss) / norm_count), EVERY
    )
    direct = over_cells(inputs, grad0)[0:16]
    late, pair0 = mode_call(
        modes_last_kernel,
        "modes_last",
        0,
        (swap(coef), masks[0], a0, a_in, direct),
        weights,
        ((8, 128), (128, 128)),
    )
    pairs = jnp.stack([pair0, pair1])
    spectral_grad = outer_products([pairs] + [xor_group(pairs, d) for d in range(1, 4)])
    late = lax.all_to_all(jnp.broadcast_to(late, (128, 8, 128)), EVERY, 0, 0, tiled=True)
    late = jnp.sum(late, axis=0)[0:6]
    through, direct = late[:, 0:64], late[:, 64:128]
    lift_grad = (through + jnp.dot(direct, pointwise[0], precision=PRECISE)).T
    point_grad0 = jnp.dot(direct.T, lift_weight.T, precision=PRECISE)
    return (
        new_fields.reshape(2, 3, 4, 16, 256),
        lift_grad,
        jnp.stack([point_grad0, point_grad1]),
        spectral_grad,
        proj_grad,
        loss,
    )


def solution(mesh):
    return jax.shard_map(
        local,
        mesh=mesh,
        in_specs=(
            P(None, None, "tile", "role", "rep"),
            P("tile", "role", "rep"),
            P(),
            P(),
            P(),
            P(),
            P(),
            P(),
            P(None, "tile", None, None, None),
            P(),
        ),
        out_specs=(
            P(None, None, "tile", "role", "rep"),
            P(),
            P(),
            P(None, "tile", None, None, None),
            P(),
            P(),
        ),
        check_vma=False,
    )
```

time: 993 us -> 333 us (0.34)
  local copies, waits for them, and re-layouts: 352 us -> 16.9 us
  blocking collectives: 212 us -> 67.4 us
  Pallas kernels: 0 us -> 104 us
  matrix products: 107 us -> 17.9 us
  waiting for transfers between devices: 102 us -> 29.4 us
  other arithmetic: 62.9 us -> 10.8 us
  starting transfers between devices: 128 us -> 82.9 us
  between operations: 17.7 us -> 1.68 us
    another operation x42 -> x0, local copies, waits for them, and re-layouts: 176 us -> none  [curl_of(): return jnp.stack([d_zy - d_yz, d_xz - d_zx, d_yx - d_xy])]
    psum x1, blocking collectives: 182 us -> 67.4 us  [local(): lax.psum((point_grad1, proj_grad, jnp.sum(loss) / norm_count), EVERY)]
    pallas_call x0 -> x11, Pallas kernels: none -> 104 us  [the longest x4 30.4 us: mode_call(): pl.pallas_call(kernel, grid=(8,), out_shape=[shape_of(*o) for o in outs],...]
    dot_general x39 -> x6, matrix products: 107 us -> 17.9 us  [the longest x3 15.8 us: over_cells(): lax.dot_general(a, b, TN, precision=PRECISE, preferred_element_type=F32)]
    psum x1 -> x0, waiting for transfers between devices: 76.4 us -> none  [local(): spectral_grad = lax.psum(jnp.stack(mode_grads), ('role', 'rep'))]
    squeeze x16 -> x2, local copies, waits for them, and re-layouts: 69.1 us -> 1.8 us  [the longest x1 1.8 us: local(): received = [pieces[0]] + [xor_group(pieces[d], d) for d in range(1, 4)]]
    ppermute x24 -> x17, starting transfers between devices: 73.9 us -> 29.4 us  [the longest x2 8.27 us: diagonal(): return lax.ppermute(value, ('rep', 'tile'), pairs)]
    concatenate x37 -> x0, local copies, waits for them, and re-layouts: 37.9 us -> none  [the longest x21 37.8 us: forward_diff(): return jnp.concatenate([remainder, border], axis=along) - grid_field]
  transfers between devices with their start and end apart: 33 -> 25, of which waited for: 8 -> 11; matrix products, arithmetic and copies ran while one was open for 34% -> 10% of each run, Pallas kernels for 0% -> 13%
where the time goes in v1:
time: 333 us; the launch traced here: 331 us
  Pallas kernels  104 us (31%)
  starting transfers between devices  82.9 us (25%)
  blocking collectives  67.4 us (20%)
  waiting for transfers between devices  29.4 us (9%)
  matrix products  17.9 us (5%)
  local copies, waits for them, and re-layouts  16.9 us (5%)
  other arithmetic  10.8 us (3%)
    psum x1, blocking collectives, local(): lax.psum((point_grad1, proj_grad, jnp.sum(loss) / norm_count), EVERY)  67.4 us
    all_to_all x6, starting transfers between devices, swap(): return lax.all_to_all(value, 'tile', 0, 0, tiled=True).reshape(256, 128)  31.4 us
    pallas_call x4, Pallas kernels, mode_call(): pl.pallas_call(kernel, grid=(8,), out_shape=[shape_of(*o) for o in outs],...  30.4 us
    pallas_call x1, Pallas kernels, outer_products(): pl.pallas_call(outer_kernel, grid=(LAYERS, 8), out_shape=shape_of(LAYERS,...  30 us
    pallas_call x3, Pallas kernels, cell_call(): pl.pallas_call(kernel, grid=(SY // BLOCK_Y,), out_shape=out_shape, in_spe...  24.5 us
    dot_general x3, matrix products, over_cells(): lax.dot_general(a, b, TN, precision=PRECISE, preferred_element_type=F32)  15.8 us
    all_to_all x6, waiting for transfers between devices, swap(): return lax.all_to_all(value, 'tile', 0, 0, tiled=True).reshape(256, 128)  14.5 us
    pallas_call x1, Pallas kernels, leapfrog(): pl.pallas_call(leap_kernel, out_shape=[shape_of(6, 4, 16, 256), shape_of(...  12.3 us
  transfers between devices with their start and end apart: 25, of which 11 were waited for; matrix products, arithmetic and copies ran while one was open for 10% of the time, Pallas kernels for 13%

profile of v1, /device:TPU:1, one launch (start us, length us, event | category | flops | bytes accessed | tf_op | source)
XLA Modules:
  0.0 331.1 jit_solution(9846719937793118719)
XLA Ops:
  0.6 1.8 pack.1
  2.5 1.3 collective-permute-start.3
  3.7 5.0 %collective-permute-start.1 = (f32[7,4,16,256]{3,2,1,0:T(8,128)}, f32[7,4,16,256]{3,2,1,0:T(8,128)S(1)}, u32[]{:S(2)}, u32[]{:S(2)}) collective-permute-start(f32[7,4,16,256]{3,2,1,0:T(8,128)} %get-tuple-element.33.own0), channel_id=1, source_target_pairs={{0,1},{1,2},{2,3},{3,4},{4,5},{5,6},{6,7},{7,8},{8,9},{9,10},{10,1... | collective-permute-start | bytes 1376264 | tf_op jit(solution)/shard_map/ppermute | solution.py:694
  8.8 1.3 collective-permute-start.9
  10.1 7.0 %collective-permute-start.7 = (f32[8,512]{1,0:T(8,128)}, f32[8,512]{1,0:T(8,128)S(1)}, u32[]{:S(2)}, u32[]{:S(2)}) collective-permute-start(f32[8,512]{1,0:T(8,128)} %get-tuple-element.34), channel_id=1, source_target_pairs={{0,33},{1,34},{2,35},{3,36},{4,37},{5,38},{6,39},{7,40},{8,41},{9,... | collective-permute-start | bytes 49160 | tf_op jit(solution)/shard_map/ppermute | solution.py:707
  17.1 1.6 collective-permute-start
  18.7 0.7 subtract_divide_fusion
  19.3 0.9 fusion.5
  20.4 7.7 %collective-permute-done.1.low0 = f32[7,4,16,256]{3,2,1,0:T(8,128)S(1)} collective-permute-done((f32[7,4,16,256]{3,2,1,0:T(8,128)}, f32[7,4,16,256]{3,2,1,0:T(8,128)S(1)}, u32[]{:S(2)}, u32[]{:S(2)}) %collective-permute-start.1) | collective-permute-done | bytes 458784 | tf_op jit(solution)/shard_map/ppermute | solution.py:694
  28.6 0.7 multiply_divide_fusion
  29.3 0.7 pad.24
  30.6 1.6 fusion.16
  32.2 3.4 %collective-permute-start.5 = (f32[8,512]{1,0:T(8,128)}, f32[8,512]{1,0:T(8,128)S(1)}, u32[]{:S(2)}, u32[]{:S(2)}) collective-permute-start(f32[8,512]{1,0:T(8,128)} %get-tuple-element.34), channel_id=1, source_target_pairs={{0,32},{32,0},{1,33},{33,1},{2,34},{34,2},{3,35},{35,3},{4,36},{36... | collective-permute-start | bytes 49160 | tf_op jit(solution)/shard_map/ppermute | solution.py:698
  36.9 0.9 collective-permute-start.8
  37.9 0.7 pad_add_fusion.place
  40.0 0.8 copy-done.15
  40.7 12.3 %leapfrog.1 = (f32[6,4,16,256]{3,2,1,0:T(8,128)}, f32[4,256,128]{2,1,0:T(8,128)}, f32[4,256,128]{2,1,0:T(8,128)}) custom-call(s32[3]{0:T(128)} %pad_add_fusion.place, s32[4]{0:T(128)} %plan.1, f32[8]{0:T(128)} %pad_maximum_fusion.3.coefs, f32[7,4,16,256]{3,2,1,0:T(8,128)} %get-tuple-element.33.own0, f32[7,4,16,256]{3,2,1,0:T(8,128)} %copy-done.13, ...), custom_call_target="tpu_custom_call" | custom-call | tf_op jit(solution)/shard_map/leapfrog/pallas_call | solution.py:319
  53.0 11.5 %all-to-all-start = ((f32[128,8,128]{2,1,0:T(8,128)}), f32[128,8,128]{2,1,0:T(8,128)S(1)}, u32[]{:S(2)}, u32[]{:S(2)}) async-start(f32[128,8,128]{2,1,0:T(8,128)} %bitcast.72), calls=%async_computation | async-start | bytes 1048576 | tf_op jit(solution)/shard_map/all_to_all | solution.py:773
  64.6 1.9 and_convert_fusion.1
  66.5 1.8 slice_bitcast_fusion
  68.3 3.5 %collective-permute-start.13 = (f32[256,128]{1,0:T(8,128)S(1)}, f32[256,128]{1,0:T(8,128)S(1)}, u32[]{:S(2)}, u32[]{:S(2)}) collective-permute-start(f32[256,128]{1,0:T(8,128)S(1)} %get-tuple-element.65), channel_id=1, source_target_pairs={{0,96},{32,64},{64,32},{96,0},{1,97},{33,65},{65,33},{97,1},{2,98}... | collective-permute-start | bytes 393224 | tf_op jit(solution)/shard_map/ppermute | solution.py:711
  72.2 6.3 %all-to-all-done = f32[128,8,128]{2,1,0:T(8,128)S(1)} async-done(((f32[128,8,128]{2,1,0:T(8,128)}), f32[128,8,128]{2,1,0:T(8,128)S(1)}, u32[]{:S(2)}, u32[]{:S(2)}) %all-to-all-start) | async-done | bytes 524320 | tf_op jit(solution)/shard_map/all_to_all | solution.py:773
  78.5 0.8 broadcast_in_dim.6.mask
  79.3 8.0 %modes_first.1 = (f32[256,128]{1,0:T(8,128)}, f32[128,128]{1,0:T(8,128)}, f32[128,128]{1,0:T(8,128)}) custom-call(f32[4,256,128]{2,1,0:T(8,128)} %bitcast.65, f32[128,128]{1,0:T(8,128)} %broadcast_in_dim.6.mask, f32[128,128]{1,0:T(8,128)} %select_maximum_fusion.1.lift, f32[2,8,1024,64]{3,2,1,0:T(8,128)} %bitcast.61, ...), custom_call_target="tpu_custom_call" | custom-call | tf_op jit(solution)/shard_map/modes_first/pallas_call | solution.py:654
  87.4 3.9 %all-to-all-start.1 = ((f32[32,8,128]{2,1,0:T(8,128)}), f32[32,8,128]{2,1,0:T(8,128)S(1)}, u32[]{:S(2)}, u32[]{:S(2)}) async-start(f32[32,8,128]{2,1,0:T(8,128)} %bitcast.74), calls=%async_computation.1 | async-start | bytes 262144 | tf_op jit(solution)/shard_map/all_to_all | solution.py:779
  92.8 5.0 %prepare.1 = (f32[4096,128]{1,0:T(8,128)}, f32[4096,128]{1,0:T(8,128)}, f32[4096,128]{1,0:T(8,128)}) custom-call(s32[3]{0:T(128)} %pad_add_fusion.place, f32[256,128]{1,0:T(8,128)} %get-tuple-element.68.piece0, f32[256,128]{1,0:T(8,128)} %copy-done.22, f32[256,128]{1,0:T(8,128)} %copy-done.21, f32[256,128]{1,0:T(8,128)} %copy-done.20, f32[128,128]{1,0:T(8,128)} %pad.26.weight), custom_call_target="tpu_custom_call" | custom-call | tf_op jit(solution)/shard_map/prepare/pallas_call | solution.py:365
  97.8 0.7 all-to-all-done.1
  98.5 0.6 copy-done.8
  99.2 6.2 %cells0.1 = (f32[256,128]{1,0:T(8,128)}, f32[4096,128]{1,0:T(8,128)}, f32[4096,128]{1,0:T(8,128)}) custom-call(f32[256,128]{1,0:T(8,128)} %bitcast.69, f32[4096,128]{1,0:T(8,128)} %get-tuple-element.39.pre, bf16[2,256,256]{2,1,0:T(8,128)(2,1)} %constant.114.clone.kron, bf16[2,256,256]{2,1,0:T(8,128)(2,1)} %constant.115.clone.kron_t, ...), custom_call_target="tpu_custom_call" | custom-call | tf_op jit(solution)/shard_map/cells0/pallas_call | solution.py:519
  105.4 7.0 %all-to-all-start.2 = ((f32[32,8,128]{2,1,0:T(8,128)}), f32[32,8,128]{2,1,0:T(8,128)S(1)}, u32[]{:S(2)}, u32[]{:S(2)}) async-start(f32[32,8,128]{2,1,0:T(8,128)} %bitcast.75), calls=%async_computation.2 | async-start | bytes 262144 | tf_op jit(solution)/shard_map/all_to_all | solution.py:779
  112.4 1.8 and_convert_fusion
  114.2 0.7 select_maximum_fusion
  114.9 4.9 %all-to-all-done.2 = f32[32,8,128]{2,1,0:T(8,128)S(1)} async-done(((f32[32,8,128]{2,1,0:T(8,128)}), f32[32,8,128]{2,1,0:T(8,128)S(1)}, u32[]{:S(2)}, u32[]{:S(2)}) %all-to-all-start.2) | async-done | bytes 131104 | tf_op jit(solution)/shard_map/all_to_all | solution.py:779
  119.7 0.7 broadcast_in_dim.7.mask
  120.5 7.8 %modes_forward.1 = (f32[256,128]{1,0:T(8,128)}, f32[128,128]{1,0:T(8,128)}) custom-call(f32[256,128]{1,0:T(8,128)} %bitcast.66, f32[128,128]{1,0:T(8,128)} %broadcast_in_dim.7.mask, f32[2,8,1024,64]{3,2,1,0:T(8,128)} %bitcast.62, bf16[2,256,256]{2,1,0:T(8,128)(2,1)} %constant.112.clone.kron, bf16[2,256,256]{2,1,0:T(8,128)(2,1)} %constant.113.clone.kron_t), custom_call_target="tpu_custom_call" | custom-call | tf_op jit(solution)/shard_map/modes_forward/pallas_call | solution.py:654
  128.2 4.1 %all-to-all-start.3 = ((f32[32,8,128]{2,1,0:T(8,128)}), f32[32,8,128]{2,1,0:T(8,128)S(1)}, u32[]{:S(2)}, u32[]{:S(2)}) async-start(f32[32,8,128]{2,1,0:T(8,128)} %bitcast.77), calls=%async_computation.3 | async-start | bytes 262144 | tf_op jit(solution)/shard_map/all_to_all | solution.py:779
  133.0 0.7 copy.27.w_point
  133.7 0.7 copy.28.w_proj
  134.4 0.7 pad_maximum_fusion.1.saved
  135.1 4.3 %all-to-all-done.3 = f32[32,8,128]{2,1,0:T(8,128)S(1)} async-done(((f32[32,8,128]{2,1,0:T(8,128)}), f32[32,8,128]{2,1,0:T(8,128)S(1)}, u32[]{:S(2)}, u32[]{:S(2)}) %all-to-all-start.3) | async-done | bytes 131104 | tf_op jit(solution)/shard_map/all_to_all | solution.py:779
  140.1 11.4 %cells1.1 = (f32[256,128]{1,0:T(8,128)}, f32[4096,128]{1,0:T(8,128)}, f32[4096,128]{1,0:T(8,128)}, f32[4096,128]{1,0:T(8,128)}, f32[8,128]{1,0:T(8,128)}) custom-call(f32[256,128]{1,0:T(8,128)} %bitcast.71, f32[4096,128]{1,0:T(8,128)} %get-tuple-element.42.h1, f32[4096,128]{1,0:T(8,128)} %get-tuple-element.43.target, f32[128,128]{1,0:T(8,128)} %copy.27.w_point, ...), custom_call_target="tpu_custom_call" | custom-call | tf_op jit(solution)/shard_map/cells1/pallas_call | solution.py:519
  151.5 4.0 %all-to-all-start.4 = ((f32[32,8,128]{2,1,0:T(8,128)}), f32[32,8,128]{2,1,0:T(8,128)S(1)}, u32[]{:S(2)}, u32[]{:S(2)}) async-start(f32[32,8,128]{2,1,0:T(8,128)} %bitcast.79), calls=%async_computation.4 | async-start | bytes 262144 | tf_op jit(solution)/shard_map/all_to_all | solution.py:779
  155.5 5.0 %fusion.18 = f32[128,128]{1,0:T(8,128)S(1)} fusion(f32[4096,128]{1,0:T(8,128)} %get-tuple-element.47.grad1, f32[4096,128]{1,0:T(8,128)S(1)} %copy-done), kind=kOutput, calls=%fused_computation.62 | convolution fusion | flops 805306368 | bytes 4259840 | tf_op jit(solution)/shard_map/dot_general | solution.py:829
  160.5 2.3 all-to-all-done.4
  162.8 0.7 copy-done.7
  163.5 7.4 %modes_backward.1 = (f32[256,128]{1,0:T(8,128)}, f32[128,128]{1,0:T(8,128)}) custom-call(f32[256,128]{1,0:T(8,128)} %bitcast.68, f32[128,128]{1,0:T(8,128)} %broadcast_in_dim.7.mask, f32[128,128]{1,0:T(8,128)} %get-tuple-element.45.saved, f32[2,8,1024,64]{3,2,1,0:T(8,128)} %bitcast.63, bf16[2,256,256]{2,1,0:T(8,128)(2,1)} %constant.112.clone.kron, ...), custom_call_target="tpu_custom_call" | custom-call | tf_op jit(solution)/shard_map/modes_backward/pallas_call | solution.py:654
  170.9 5.5 %all-to-all-start.5 = ((f32[32,8,128]{2,1,0:T(8,128)}), f32[32,8,128]{2,1,0:T(8,128)S(1)}, u32[]{:S(2)}, u32[]{:S(2)}) async-start(f32[32,8,128]{2,1,0:T(8,128)} %bitcast.76), calls=%async_computation.5 | async-start | bytes 262144 | tf_op jit(solution)/shard_map/all_to_all | solution.py:779
  176.4 5.0 %fusion.19 = f32[128,128]{1,0:T(8,128)S(1)} fusion(f32[4096,128]{1,0:T(8,128)} %get-tuple-element.57, f32[4096,128]{1,0:T(8,128)S(1)} %copy-done.3), kind=kOutput, calls=%fused_computation.63 | convolution fusion | flops 805306368 | bytes 4259840 | tf_op jit(solution)/shard_map/dot_general | solution.py:829
  182.7 1.0 all-to-all-done.5
  183.7 0.7 copy-done.9
  184.3 6.9 %cells2.1 = (f32[256,128]{1,0:T(8,128)}, f32[4096,128]{1,0:T(8,128)}) custom-call(f32[256,128]{1,0:T(8,128)} %bitcast.70, f32[4096,128]{1,0:T(8,128)} %get-tuple-element.47.grad1, f32[4096,128]{1,0:T(8,128)} %get-tuple-element.48.slope0, f32[128,128]{1,0:T(8,128)} %get-tuple-element.69.w_point, bf16[2,256,256]{2,1,0:T(8,128)(2,1)} %constant.114.clone.kron, ...), custom_call_target="tpu_custom_call" | custom-call | tf_op jit(solution)/shard_map/cells2/pallas_call | solution.py:519
  191.2 7.0 %all-to-all-start.6 = ((f32[32,8,128]{2,1,0:T(8,128)}), f32[32,8,128]{2,1,0:T(8,128)S(1)}, u32[]{:S(2)}, u32[]{:S(2)}) async-start(f32[32,8,128]{2,1,0:T(8,128)} %bitcast.78), calls=%async_computation.6 | async-start | bytes 262144 | tf_op jit(solution)/shard_map/all_to_all | solution.py:779
  198.2 5.8 %fusion.point = f32[16,128]{1,0:T(8,128)} fusion(f32[4096,128]{1,0:T(8,128)} %get-tuple-element.53, f32[4096,128]{1,0:T(8,128)S(1)} %copy-done.2), kind=kOutput, calls=%fused_computation | convolution fusion | flops 100663296 | bytes 4202496 | tf_op jit(solution)/shard_map/dot_general | solution.py:829
  204.0 1.3 all-to-all-done.6
  205.3 0.7 copy-done.6
  206.0 7.2 %modes_last.1 = (f32[8,128]{1,0:T(8,128)}, f32[128,128]{1,0:T(8,128)}) custom-call(f32[256,128]{1,0:T(8,128)} %bitcast.67, f32[128,128]{1,0:T(8,128)} %broadcast_in_dim.6.mask, f32[128,128]{1,0:T(8,128)} %pad_maximum_fusion.1.saved, f32[128,128]{1,0:T(8,128)} %get-tuple-element.51.inputs, f32[16,128]{1,0:T(8,128)} %fusion.point, ...), custom_call_target="tpu_custom_call" | custom-call | tf_op jit(solution)/shard_map/modes_last/pallas_call | solution.py:654
  213.2 1.6 broadcast_in_dim.8
  214.7 10.6 %all-to-all-start.7 = ((f32[128,8,128]{2,1,0:T(8,128)}), f32[128,8,128]{2,1,0:T(8,128)S(1)}, u32[]{:S(2)}, u32[]{:S(2)}) async-start(f32[128,8,128]{2,1,0:T(8,128)} %broadcast_in_dim.8), calls=%async_computation.7 | async-start | bytes 1048576 | tf_op jit(solution)/shard_map/all_to_all | solution.py:849
  225.4 0.9 pad_maximum_fusion.pair0
  226.3 3.6 %collective-permute-start.16 = (f32[2,128,128]{2,1,0:T(8,128)S(1)}, f32[2,128,128]{2,1,0:T(8,128)S(1)}, u32[]{:S(2)}, u32[]{:S(2)}) collective-permute-start(f32[2,128,128]{2,1,0:T(8,128)S(1)} %pad_maximum_fusion.pair0), channel_id=1, source_target_pairs={{0,96},{32,64},{64,32},{96,0},{1,97},{33,65},{65,33},{97,1},{2,98}... | collective-permute-start | bytes 393224 | tf_op jit(solution)/shard_map/ppermute | solution.py:711
  230.4 67.4 %all-reduce.11 = (f32[1,64,64]{2,1,0:T(8,128)S(1)}, f32[6,64]{1,0:T(8,128)}, f32[]{:T(128)}) all-reduce(f32[1,64,64]{2,1,0:T(8,128)S(1)} %fusion.3, f32[6,64]{1,0:T(8,128)S(1)} %slice_add_fusion.1, f32[]{:T(128)S(6)} %div.38), channel_id=1, replica_groups=mesh['role'=2,'rep'=2,'tile'=32] {'role','rep','tile'}, use_global_device_ids=true, to_apply=%region_1.2 | all-reduce | flops 4481 | bytes 35848 | tf_op jit(solution)/shard_map/psum | solution.py:835
  298.5 0.7 copy-done.19
  299.1 30.0 %outer.1 = f32[2,8,16,64,64]{4,3,2,1,0:T(8,128)} custom-call(f32[2,128,128]{2,1,0:T(8,128)} %copy-done.4, f32[2,128,128]{2,1,0:T(8,128)} %copy-done.19, f32[2,128,128]{2,1,0:T(8,128)} %copy-done.18, f32[2,128,128]{2,1,0:T(8,128)} %copy-done.17), custom_call_target="tpu_custom_call" | custom-call | tf_op jit(solution)/shard_map/outer/pallas_call | solution.py:681
  329.3 0.8 fusion.2
  (101 shorter events, 10.2 us)
Async XLA Ops:
  2.5 17.8 %collective-permute-start.3 = (f32[7,4,16,256]{3,2,1,0:T(8,128)}, f32[7,4,16,256]{3,2,1,0:T(8,128)S(1)}, u32[]{:S(2)}, u32[]{:S(2)}) collective-permute-start(f32[7,4,16,256]{3,2,1,0:T(8,128)} %get-tuple-element.33.own0), channel_id=1, source_target_pairs={{1,0},{2,1},{3,2},{4,3},{5,4},{6,5},{7,6},{8,7},{9,8},{10,9},{11,1... | collective-permute-start | bytes 1376264 | tf_op jit(solution)/shard_map/ppermute | solution.py:694
  3.7 24.3 %collective-permute-start.1 = (f32[7,4,16,256]{3,2,1,0:T(8,128)}, f32[7,4,16,256]{3,2,1,0:T(8,128)S(1)}, u32[]{:S(2)}, u32[]{:S(2)}) collective-permute-start(f32[7,4,16,256]{3,2,1,0:T(8,128)} %get-tuple-element.33.own0), channel_id=1, source_target_pairs={{0,1},{1,2},{2,3},{3,4},{4,5},{5,6},{6,7},{7,8},{8,9},{9,10},{10,1... | collective-permute-start | bytes 1376264 | tf_op jit(solution)/shard_map/ppermute | solution.py:694
  8.8 23.4 %collective-permute-start.9 = (f32[8,512]{1,0:T(8,128)}, f32[8,512]{1,0:T(8,128)S(1)}, u32[]{:S(2)}, u32[]{:S(2)}) collective-permute-start(f32[8,512]{1,0:T(8,128)} %get-tuple-element.34), channel_id=1, source_target_pairs={{1,32},{2,33},{3,34},{4,35},{5,36},{6,37},{7,38},{8,39},{9,40},{10... | collective-permute-start | bytes 49160 | tf_op jit(solution)/shard_map/ppermute | solution.py:707
  10.1 25.5 %collective-permute-start.7 = (f32[8,512]{1,0:T(8,128)}, f32[8,512]{1,0:T(8,128)S(1)}, u32[]{:S(2)}, u32[]{:S(2)}) collective-permute-start(f32[8,512]{1,0:T(8,128)} %get-tuple-element.34), channel_id=1, source_target_pairs={{0,33},{1,34},{2,35},{3,36},{4,37},{5,38},{6,39},{7,40},{8,41},{9,... | collective-permute-start | bytes 49160 | tf_op jit(solution)/shard_map/ppermute | solution.py:707
  17.1 22.0 %collective-permute-start = (f32[7,4,16,256]{3,2,1,0:T(8,128)}, f32[7,4,16,256]{3,2,1,0:T(8,128)S(1)}, u32[]{:S(2)}, u32[]{:S(2)}) collective-permute-start(f32[7,4,16,256]{3,2,1,0:T(8,128)} %get-tuple-element.33.own0), channel_id=1, source_target_pairs={{0,64},{64,0},{1,65},{65,1},{2,66},{66,2},{3,67},{67,3},{4,68},{68... | collective-permute-start | bytes 1376264 | tf_op jit(solution)/shard_map/ppermute | solution.py:698
  20.3 18.8 %copy-start.11 = (f32[7,4,16,256]{3,2,1,0:T(8,128)}, f32[7,4,16,256]{3,2,1,0:T(8,128)S(1)}, u32[]{:S(2)}) copy-start(f32[7,4,16,256]{3,2,1,0:T(8,128)S(1)} %collective-permute-done.3.high0) | copy-start | bytes 1376260
  20.3 18.7 %collective-permute-start.4 = (f32[7,4,16,256]{3,2,1,0:T(8,128)S(1)}, f32[7,4,16,256]{3,2,1,0:T(8,128)S(1)}, u32[]{:S(2)}, u32[]{:S(2)}) collective-permute-start(f32[7,4,16,256]{3,2,1,0:T(8,128)S(1)} %collective-permute-done.3.high0), channel_id=1, source_target_pairs={{0,64},{64,0},{1,65},{65,1},{2,66},{66,2},{3,67},{67,3},{4,68},{68... | collective-permute-start | bytes 1376264 | tf_op jit(solution)/shard_map/ppermute | solution.py:698
  28.1 11.0 %copy-start.12 = (f32[7,4,16,256]{3,2,1,0:T(8,128)}, f32[7,4,16,256]{3,2,1,0:T(8,128)S(1)}, u32[]{:S(2)}) copy-start(f32[7,4,16,256]{3,2,1,0:T(8,128)S(1)} %collective-permute-done.1.low0) | copy-start | bytes 1376260
  28.1 10.9 %collective-permute-start.2 = (f32[7,4,16,256]{3,2,1,0:T(8,128)S(1)}, f32[7,4,16,256]{3,2,1,0:T(8,128)S(1)}, u32[]{:S(2)}, u32[]{:S(2)}) collective-permute-start(f32[7,4,16,256]{3,2,1,0:T(8,128)S(1)} %collective-permute-done.1.low0), channel_id=1, source_target_pairs={{0,64},{64,0},{1,65},{65,1},{2,66},{66,2},{3,67},{67,3},{4,68},{68... | collective-permute-start | bytes 1376264 | tf_op jit(solution)/shard_map/ppermute | solution.py:698
  32.2 6.9 %copy-start.26 = (f32[8,512]{1,0:T(8,128)}, f32[8,512]{1,0:T(8,128)S(1)}, u32[]{:S(2)}) copy-start(f32[8,512]{1,0:T(8,128)S(1)} %collective-permute-done.9.strip_high0) | copy-start | bytes 49156
  32.2 4.7 %collective-permute-start.5 = (f32[8,512]{1,0:T(8,128)}, f32[8,512]{1,0:T(8,128)S(1)}, u32[]{:S(2)}, u32[]{:S(2)}) collective-permute-start(f32[8,512]{1,0:T(8,128)} %get-tuple-element.34), channel_id=1, source_target_pairs={{0,32},{32,0},{1,33},{33,1},{2,34},{34,2},{3,35},{35,3},{4,36},{36... | collective-permute-start | bytes 49160 | tf_op jit(solution)/shard_map/ppermute | solution.py:698
  35.6 3.5 %copy-start.27 = (f32[8,512]{1,0:T(8,128)}, f32[8,512]{1,0:T(8,128)S(1)}, u32[]{:S(2)}) copy-start(f32[8,512]{1,0:T(8,128)S(1)} %collective-permute-done.7.strip_low0) | copy-start | bytes 49156
  35.6 2.3 collective-permute-start.10
  36.9 2.2 copy-start.28
  36.9 1.8 collective-permute-start.8
  37.8 1.3 copy-start.29
  37.8 1.2 collective-permute-start.6
  38.6 27.9 %copy-start.16 = (f32[2,64,64]{2,1,0:T(8,128)S(1)}, f32[2,64,64]{2,1,0:T(8,128)}, u32[]{:S(2)}) copy-start(f32[2,64,64]{2,1,0:T(8,128)} %param.26) | copy-start | bytes 98308
  38.7 0.6 copy-start.30
  39.0 0.6 copy-start.31
  39.0 0.8 copy-start.13
  39.0 1.0 copy-start.14
  40.0 0.8 copy-start.15
  53.0 25.5 %all-to-all-start = ((f32[128,8,128]{2,1,0:T(8,128)}), f32[128,8,128]{2,1,0:T(8,128)S(1)}, u32[]{:S(2)}, u32[]{:S(2)}) async-start(f32[128,8,128]{2,1,0:T(8,128)} %bitcast.72), calls=%async_computation | async-start | bytes 1048576 | tf_op jit(solution)/shard_map/all_to_all | solution.py:773
  68.3 23.7 %collective-permute-start.13 = (f32[256,128]{1,0:T(8,128)S(1)}, f32[256,128]{1,0:T(8,128)S(1)}, u32[]{:S(2)}, u32[]{:S(2)}) collective-permute-start(f32[256,128]{1,0:T(8,128)S(1)} %get-tuple-element.65), channel_id=1, source_target_pairs={{0,96},{32,64},{64,32},{96,0},{1,97},{33,65},{65,33},{97,1},{2,98}... | collective-permute-start | bytes 393224 | tf_op jit(solution)/shard_map/ppermute | solution.py:711
  71.8 20.2 %collective-permute-start.12 = (f32[256,128]{1,0:T(8,128)S(1)}, f32[256,128]{1,0:T(8,128)S(1)}, u32[]{:S(2)}, u32[]{:S(2)}) collective-permute-start(f32[256,128]{1,0:T(8,128)S(1)} %get-tuple-element.66), channel_id=1, source_target_pairs={{0,64},{32,96},{64,0},{96,32},{1,65},{33,97},{65,1},{97,33},{2,66}... | collective-permute-start | bytes 393224 | tf_op jit(solution)/shard_map/ppermute | solution.py:711
  71.9 20.1 %collective-permute-start.11 = (f32[256,128]{1,0:T(8,128)S(1)}, f32[256,128]{1,0:T(8,128)S(1)}, u32[]{:S(2)}, u32[]{:S(2)}) collective-permute-start(f32[256,128]{1,0:T(8,128)S(1)} %get-tuple-element.67), channel_id=1, source_target_pairs={{0,32},{32,0},{64,96},{96,64},{1,33},{33,1},{65,97},{97,65},{2,34}... | collective-permute-start | bytes 393224 | tf_op jit(solution)/shard_map/ppermute | solution.py:711
  78.5 0.8 copy-start.1
  79.3 12.0 %copy-start.33 = (f32[6,64]{1,0:T(8,128)S(1)}, f32[6,64]{1,0:T(8,128)}, u32[]{:S(2)}) copy-start(f32[6,64]{1,0:T(8,128)} %param.28) | copy-start | bytes 4612
  87.4 11.2 %all-to-all-start.1 = ((f32[32,8,128]{2,1,0:T(8,128)}), f32[32,8,128]{2,1,0:T(8,128)S(1)}, u32[]{:S(2)}, u32[]{:S(2)}) async-start(f32[32,8,128]{2,1,0:T(8,128)} %bitcast.74), calls=%async_computation.1 | async-start | bytes 262144 | tf_op jit(solution)/shard_map/all_to_all | solution.py:779
  92.0 0.7 copy-start.20
  92.0 0.7 copy-start.21
  92.0 0.7 copy-start.22
  98.5 0.6 copy-start.8
  105.4 14.4 %all-to-all-start.2 = ((f32[32,8,128]{2,1,0:T(8,128)}), f32[32,8,128]{2,1,0:T(8,128)S(1)}, u32[]{:S(2)}, u32[]{:S(2)}) async-start(f32[32,8,128]{2,1,0:T(8,128)} %bitcast.75), calls=%async_computation.2 | async-start | bytes 262144 | tf_op jit(solution)/shard_map/all_to_all | solution.py:779
  119.7 0.7 copy-start.5
  120.5 14.0 %copy-start.23 = (f32[128,128]{1,0:T(8,128)S(1)}, f32[128,128]{1,0:T(8,128)}, u32[]{:S(2)}) copy-start(f32[128,128]{1,0:T(8,128)} %get-tuple-element.50) | copy-start | bytes 196612
  128.2 11.2 %all-to-all-start.3 = ((f32[32,8,128]{2,1,0:T(8,128)}), f32[32,8,128]{2,1,0:T(8,128)S(1)}, u32[]{:S(2)}, u32[]{:S(2)}) async-start(f32[32,8,128]{2,1,0:T(8,128)} %bitcast.77), calls=%async_computation.3 | async-start | bytes 262144 | tf_op jit(solution)/shard_map/all_to_all | solution.py:779
  139.5 0.6 copy-start.10
  140.1 15.4 %copy-start = (f32[4096,128]{1,0:T(8,128)S(1)}, f32[4096,128]{1,0:T(8,128)}, u32[]{:S(2)}) copy-start(f32[4096,128]{1,0:T(8,128)} %get-tuple-element.42.h1) | copy-start | bytes 6291460
  151.5 11.3 %all-to-all-start.4 = ((f32[32,8,128]{2,1,0:T(8,128)}), f32[32,8,128]{2,1,0:T(8,128)S(1)}, u32[]{:S(2)}, u32[]{:S(2)}) async-start(f32[32,8,128]{2,1,0:T(8,128)} %bitcast.79), calls=%async_computation.4 | async-start | bytes 262144 | tf_op jit(solution)/shard_map/all_to_all | solution.py:779
  162.8 0.7 copy-start.7
  163.5 12.9 %copy-start.3 = (f32[4096,128]{1,0:T(8,128)S(1)}, f32[4096,128]{1,0:T(8,128)}, u32[]{:S(2)}) copy-start(f32[4096,128]{1,0:T(8,128)} %get-tuple-element.58) | copy-start | bytes 6291460
  170.9 12.8 %all-to-all-start.5 = ((f32[32,8,128]{2,1,0:T(8,128)}), f32[32,8,128]{2,1,0:T(8,128)S(1)}, u32[]{:S(2)}, u32[]{:S(2)}) async-start(f32[32,8,128]{2,1,0:T(8,128)} %bitcast.76), calls=%async_computation.5 | async-start | bytes 262144 | tf_op jit(solution)/shard_map/all_to_all | solution.py:779
  176.3 5.1 %copy-start.32 = (f32[8,128]{1,0:T(8,128)S(1)}, f32[8,128]{1,0:T(8,128)}, u32[]{:S(2)}) copy-start(f32[8,128]{1,0:T(8,128)} %get-tuple-element.59) | copy-start | bytes 12292
  183.6 0.7 copy-start.9
  184.3 13.9 %copy-start.2 = (f32[4096,128]{1,0:T(8,128)S(1)}, f32[4096,128]{1,0:T(8,128)}, u32[]{:S(2)}) copy-start(f32[4096,128]{1,0:T(8,128)} %get-tuple-element.52) | copy-start | bytes 6291460
  191.2 14.1 %all-to-all-start.6 = ((f32[32,8,128]{2,1,0:T(8,128)}), f32[32,8,128]{2,1,0:T(8,128)S(1)}, u32[]{:S(2)}, u32[]{:S(2)}) async-start(f32[32,8,128]{2,1,0:T(8,128)} %bitcast.78), calls=%async_computation.6 | async-start | bytes 262144 | tf_op jit(solution)/shard_map/all_to_all | solution.py:779
  205.3 0.7 copy-start.6
  206.0 19.4 %copy-start.24 = (f32[128,128]{1,0:T(8,128)S(1)}, f32[128,128]{1,0:T(8,128)}, u32[]{:S(2)}) copy-start(f32[128,128]{1,0:T(8,128)} %get-tuple-element.56) | copy-start | bytes 196612
  214.7 114.4 %all-to-all-start.7 = ((f32[128,8,128]{2,1,0:T(8,128)}), f32[128,8,128]{2,1,0:T(8,128)S(1)}, u32[]{:S(2)}, u32[]{:S(2)}) async-start(f32[128,8,128]{2,1,0:T(8,128)} %broadcast_in_dim.8), calls=%async_computation.7 | async-start | bytes 1048576 | tf_op jit(solution)/shard_map/all_to_all | solution.py:849
  226.3 71.5 %copy-start.4 = (f32[2,128,128]{2,1,0:T(8,128)}, f32[2,128,128]{2,1,0:T(8,128)S(1)}, u32[]{:S(2)}) copy-start(f32[2,128,128]{2,1,0:T(8,128)S(1)} %pad_maximum_fusion.pair0) | copy-start | bytes 393220
  226.3 71.5 %collective-permute-start.16 = (f32[2,128,128]{2,1,0:T(8,128)S(1)}, f32[2,128,128]{2,1,0:T(8,128)S(1)}, u32[]{:S(2)}, u32[]{:S(2)}) collective-permute-start(f32[2,128,128]{2,1,0:T(8,128)S(1)} %pad_maximum_fusion.pair0), channel_id=1, source_target_pairs={{0,96},{32,64},{64,32},{96,0},{1,97},{33,65},{65,33},{97,1},{2,98}... | collective-permute-start | bytes 393224 | tf_op jit(solution)/shard_map/ppermute | solution.py:711
  229.9 67.9 %collective-permute-start.15 = (f32[2,128,128]{2,1,0:T(8,128)S(1)}, f32[2,128,128]{2,1,0:T(8,128)S(1)}, u32[]{:S(2)}, u32[]{:S(2)}) collective-permute-start(f32[2,128,128]{2,1,0:T(8,128)S(1)} %pad_maximum_fusion.pair0), channel_id=1, source_target_pairs={{0,64},{32,96},{64,0},{96,32},{1,65},{33,97},{65,1},{97,33},{2,66}... | collective-permute-start | bytes 393224 | tf_op jit(solution)/shard_map/ppermute | solution.py:711
  230.0 67.8 %collective-permute-start.14 = (f32[2,128,128]{2,1,0:T(8,128)S(1)}, f32[2,128,128]{2,1,0:T(8,128)S(1)}, u32[]{:S(2)}, u32[]{:S(2)}) collective-permute-start(f32[2,128,128]{2,1,0:T(8,128)S(1)} %pad_maximum_fusion.pair0), channel_id=1, source_target_pairs={{0,32},{32,0},{64,96},{96,64},{1,33},{33,1},{65,97},{97,65},{2,34}... | collective-permute-start | bytes 393224 | tf_op jit(solution)/shard_map/ppermute | solution.py:711
  297.8 32.3 %copy-start.25 = (f32[64,6]{0,1:T(8,128)S(1)}, f32[64,6]{0,1:T(8,128)}, u32[]{:S(2)}) copy-start(f32[64,6]{0,1:T(8,128)} %param.25) | copy-start | bytes 4612
  297.8 0.7 copy-start.17
  297.8 0.7 copy-start.18
  298.5 0.7 copy-start.19

commit v2 on v1

v2 whole, which is shorter than its diff:
```python
import functools
import math

import jax
import jax.numpy as jnp
import ml_dtypes
import numpy as np
from jax import lax
from jax.experimental import pallas as pl
from jax.experimental.pallas import tpu as pltpu
from jax.sharding import PartitionSpec as P

STEPS = 4
MODES = 8
LAYERS = 2
STEP_TIME = 0.5
PRECISE = lax.Precision.HIGHEST
F32 = jnp.float32
BF16 = jnp.bfloat16
NN = (((1,), (0,)), ((), ()))
NT = (((1,), (1,)), ((), ()))
TN = (((0,), (0,)), ((), ()))
ROOM = 62 * 1024 * 1024
LEAP_ROOM = 24 * 1024 * 1024
CELL_ROOM = 62 * 1024 * 1024
MODE_ROOM = 62 * 1024 * 1024
GROUP = ("role", "rep")
EVERY = ("role", "rep", "tile")
SX, SY, SZ = 64, 16, 256
CELLS = SY * SZ
TILES = 32


def basis(length):
    frequency = np.arange(MODES)[:, None]
    position = np.arange(length)[None, :]
    angles = 2.0 * np.pi * ((frequency * position) % length) / length
    return np.concatenate([np.cos(angles), np.sin(angles)], axis=0) * math.sqrt(2.0 / length)


def split_const(table):
    table = table.astype(np.float32)
    high = table.astype(ml_dtypes.bfloat16)
    low = (table - high.astype(np.float32)).astype(ml_dtypes.bfloat16)
    return high, low


def both_const(table):
    return np.stack(split_const(table))


TABLE_X, TABLE_Y, TABLE_Z = basis(SX), basis(SY), basis(SZ)
KRON_X = both_const(
    np.einsum("ptx,mn->xmptn", TABLE_X.reshape(16, TILES, 2), np.eye(8)).reshape(256, 256)
)
KRON_XT = np.ascontiguousarray(KRON_X.transpose(0, 2, 1))
KRON_Y = both_const(np.einsum("jy,kl->jkyl", TABLE_Y, np.eye(16)).reshape(256, 256))
KRON_YT = np.ascontiguousarray(KRON_Y.transpose(0, 2, 1))
Z_HIGH, Z_LOW = split_const(TABLE_Z)
Z_ROWS = np.concatenate([Z_HIGH, Z_LOW], axis=0)
Z_COLS = np.concatenate([Z_HIGH.T, Z_HIGH.T, Z_LOW.T], axis=1)
Z_HALF = np.stack([Z_ROWS[:, r * 128 : r * 128 + 128] for r in range(2)])
POOL_Z = np.kron(np.eye(128), np.full((2, 1), 0.125)).astype(np.float32)


def halves(value):
    high = value.astype(BF16)
    return high, (value - high.astype(F32)).astype(BF16)


def dot(a, b, dims=NN):
    return lax.dot_general(a, b, dims, preferred_element_type=F32)


def dot3(a, b, dims=NN):
    return dot(a[0], b[0], dims) + dot(a[0], b[1], dims) + dot(a[1], b[0], dims)


def lanes_of(shape):
    return lax.broadcasted_iota(jnp.int32, shape, len(shape) - 1)


def rows_of(shape):
    return lax.broadcasted_iota(jnp.int32, shape, len(shape) - 2)


def square_weight(matrix):
    high, low = halves(matrix)
    one = jnp.concatenate([high, low], axis=1)
    return jnp.concatenate([one, one], axis=0)


def rows_times(value, weight):
    high, low = halves(value)
    out = dot(jnp.concatenate([high, low], axis=1), weight)
    return out[:, :128] + out[:, 128:]


def vmem(shape, dtype=F32):
    return pltpu.VMEM(shape, dtype)


def params(room=ROOM):
    return pltpu.CompilerParams(vmem_limit_bytes=room)


def full(shape):
    return pl.BlockSpec(shape, lambda *_: (0,) * len(shape))


SMEM = pl.BlockSpec(memory_space=pltpu.SMEM)
ANY = pl.BlockSpec(memory_space=pl.ANY)


def call(kernel, ins, outs, after=(), carry=(), room=ROOM, **options):
    first, last = len(ins) + len(after), len(ins) + len(after) + len(carry)

    def run(*refs):
        rest = refs[last:]
        kernel(*refs[: len(ins)], *rest[: len(outs)], *rest[len(outs) + len(carry) :])

    return pl.pallas_call(
        run,
        out_shape=[o[0] for o in outs] + [jax.ShapeDtypeStruct(c.shape, c.dtype) for c in carry],
        in_specs=[i[1] for i in ins] + [ANY] * (len(after) + len(carry)),
        out_specs=[o[1] for o in outs] + [ANY] * len(carry),
        input_output_aliases={first + n: len(outs) + n for n in range(len(carry))},
        compiler_params=params(room),
        **options,
    )(*[i[0] for i in ins], *after, *carry)


def shape_of(*shape):
    return jax.ShapeDtypeStruct(shape, F32)


def pack_kernel(fields, material, packed, ends, left, right):
    packed[0:6] = fields[...]
    packed[6] = material[...].astype(F32)
    left[...] = jnp.zeros_like(left)
    right[...] = jnp.zeros_like(right)
    left[0:448] = packed[:, :, :, 0:128].reshape(448, 128)
    right[0:448] = packed[:, :, :, 128:256].reshape(448, 128)
    for b in range(4):
        rows = slice(b * 128, (b + 1) * 128)
        first = jnp.transpose(left[rows, :])[0:8]
        last = jnp.transpose(right[rows, :])[120:128]
        ends[:, rows] = jnp.where(rows_of((8, 128)) < 4, first, last)


def pack(fields, material):
    return pl.pallas_call(
        pack_kernel,
        out_shape=[shape_of(7, 4, 16, 256), shape_of(8, 512)],
        scratch_shapes=[vmem((512, 128)), vmem((512, 128))],
        compiler_params=params(),
        name="pack",
    )(fields, material)


def here():
    return lax.axis_index("role"), lax.axis_index("rep"), lax.axis_index("tile")


def leap_kernel(
    plan,
    permittivity,
    conductivity,
    own0,
    own1,
    low0,
    low1,
    high0,
    high1,
    ends_own0,
    ends_own1,
    ends_low0,
    ends_low1,
    ends_high0,
    ends_high1,
    pool,
    out_fields,
    out_pieces,
    grid_f,
    keep,
    gain,
    dt_mask,
    edge0,
    edge1,
    sums0,
    sums1,
    reduced,
    staged,
):
    role, rep, tile = here()
    shape8 = (8, 384)
    row8 = rows_of(shape8)
    top = jnp.where((row8 < 4) & (role == 0), 1.0, 0.0)
    bottom = jnp.where((row8 >= 4) & (role == 1), 1.0, 0.0)

    def column(ends, edge):
        strip = ends[...]
        row = rows_of((8, 512))
        first = jnp.where((row < 4) & (rep == 0), strip, 0.0)
        last = jnp.where((row >= 4) & (rep == 1), strip, 0.0)
        whole = jnp.concatenate([first, jnp.zeros((112, 512), F32), last], axis=0)
        for b in range(4):
            edge[b * 128 : (b + 1) * 128, :] = jnp.transpose(whole[:, b * 128 : (b + 1) * 128])

    sources = (
        (low0, low1, ends_low0, ends_low1),
        (own0, own1, ends_own0, ends_own1),
        (high0, high1, ends_high0, ends_high1),
    )
    for number, (mine, mate, ends_mine, ends_mate) in enumerate(sources):
        column(ends_mine, edge0)
        column(ends_mate, edge1)

        def fill(n, carry, mine=mine, mate=mate, number=number):
            c = n // 4
            i = n % 4
            at = pl.multiple_of(n * 16, 16)
            plane = jnp.concatenate([mine[c, i], edge0[pl.ds(at, 16), :]], axis=1)
            other = jnp.concatenate([mate[c, i], edge1[pl.ds(at, 16), :]], axis=1)
            halo = other[0:8] * top + other[8:16] * bottom
            grid_f[c, 4 * number + i] = jnp.concatenate([plane, halo], axis=0)
            return carry

        lax.fori_loop(0, 28, fill, 0, unroll=4)

    row = rows_of((24, 384))
    lane = lanes_of((24, 384))
    row_ok = (row < 16) | ((row < 20) & (role == 0)) | ((row >= 20) & (role == 1))
    lane_ok = (lane < 256) | ((lane < 320) & (rep == 0)) | ((lane >= 320) & (rep == 1))
    inside = jnp.where(row_ok & lane_ok, 1.0, 0.0)
    dt_mask[...] = inside * STEP_TIME
    below = jnp.where(tile > 0, 1.0, 0.0)
    above = jnp.where(tile < TILES - 1, 1.0, 0.0)

    def media(p, carry):
        kind = grid_f[6, p]
        level = inside * jnp.where(p >= 8, above, 1.0)

        def choose(values):
            return jnp.where(
                kind < 0.5,
                values[0],
                jnp.where(kind < 1.5, values[1], jnp.where(kind < 2.5, values[2], values[3])),
            )

        permit = choose(permittivity)
        damping = choose(conductivity) * (0.5 * STEP_TIME) / permit
        keep[p] = (1.0 - damping) / (1.0 + damping)
        gain[p] = STEP_TIME / (permit * (1.0 + damping)) * level
        return carry

    lax.fori_loop(1, 11, media, 0, unroll=2)

    def back(value, axis):
        return pltpu.roll(value, value.shape[axis] - 1, axis)

    def step_h(p, carry):
        ex, ey, ez = grid_f[0, p], grid_f[1, p], grid_f[2, p]
        s = dt_mask[...] * below if p < 4 else dt_mask[...]
        d_zy = back(ez, 0) - ez
        d_yz = back(ey, 1) - ey
        d_xz = back(ex, 1) - ex
        d_zx = grid_f[2, p + 1] - ez
        d_yx = grid_f[1, p + 1] - ey
        d_xy = back(ex, 0) - ex
        grid_f[3, p] = grid_f[3, p] - s * (d_zy - d_yz)
        grid_f[4, p] = grid_f[4, p] - s * (d_xz - d_zx)
        grid_f[5, p] = grid_f[5, p] - s * (d_yx - d_xy)
        return carry

    def step_e(p, carry):
        hx, hy, hz = grid_f[3, p], grid_f[4, p], grid_f[5, p]
        k, g = keep[p], gain[p]
        d_zy = hz - pltpu.roll(hz, 1, 0)
        d_yz = hy - pltpu.roll(hy, 1, 1)
        d_xz = hx - pltpu.roll(hx, 1, 1)
        d_zx = hz - grid_f[5, p - 1]
        d_yx = hy - grid_f[4, p - 1]
        d_xy = hx - pltpu.roll(hx, 1, 0)
        grid_f[0, p] = k * grid_f[0, p] + g * (d_zy - d_yz)
        grid_f[1, p] = k * grid_f[1, p] + g * (d_xz - d_zx)
        grid_f[2, p] = k * grid_f[2, p] + g * (d_yx - d_xy)
        return carry

    sums0[...] = jnp.zeros_like(sums0)
    sums1[...] = jnp.zeros_like(sums1)
    for step in range(STEPS):
        for p in range(step, 11 - step):
            step_h(p, 0)
        for p in range(1 + step, 11 - step):
            step_e(p, 0)
        for x in range(2):
            for c in range(6):
                at = (x * 8 + c) * 16
                pair = grid_f[c, 4 + 2 * x, 0:16, 0:256] + grid_f[c, 5 + 2 * x, 0:16, 0:256]
                sums0[at : at + 16, :] = pair[:, 0:128]
                sums1[at : at + 16, :] = pair[:, 128:256]
        for part, sums in enumerate((sums0, sums1)):
            staged[:, part * 128 : (part + 1) * 128] = (
                sums[pl.ds(0, 128, stride=2), :] + sums[pl.ds(1, 128, stride=2), :]
            )
        reduced[step] = lax.dot_general(
            staged[...], pool[...], NN, precision=PRECISE, preferred_element_type=F32
        )
    for c in range(6):
        out_fields[c] = grid_f[c, 4:8, 0:16, 0:256]

    me = role * 2 + rep
    for d in range(4):
        out_pieces[d, 0:128] = reduced[plan[me ^ d] - 1]
        out_pieces[d, 128:256] = reduced[STEPS - 1]


def leapfrog(plan, permittivity, conductivity, blocks):
    whole = pl.BlockSpec(memory_space=pltpu.VMEM)
    return call(
        leap_kernel,
        [(v, SMEM) for v in (plan, permittivity, conductivity)]
        + [(v, whole) for v in (*blocks, jnp.asarray(POOL_Z))],
        [
            (shape_of(6, 4, 16, 256), whole),
            (shape_of(4, 256, 128), whole),
        ],
        room=LEAP_ROOM,
        scratch_shapes=[
            vmem((7, 12, 24, 384)),
            vmem((12, 24, 384)),
            vmem((12, 24, 384)),
            vmem((24, 384)),
            vmem((512, 128)),
            vmem((512, 128)),
            vmem((256, 128)),
            vmem((256, 128)),
            vmem((4, 128, 128)),
            vmem((128, 256)),
        ],
        name="leapfrog",
    )


def fold(value):
    return value[:, 0:128] + value[:, 128:256]


def coef_kernel(piece0, piece1, piece2, piece3, z_half, kron, out, d_scr):
    role, rep, _ = here()
    lane = lanes_of((16, 128))
    for flip, (one, other) in enumerate(((piece0, piece1), (piece2, piece3))):
        total = jnp.zeros((16, 128), F32)
        for z_rows, piece in ((z_half[rep], one), (z_half[1 - rep], other)):
            high, low = halves(
                jnp.concatenate([piece[pl.ds(y, 16, stride=8), :] for y in range(8)], axis=0)
            )
            out_high = dot(z_rows, high, NT)
            total = total + out_high[0:16] + out_high[16:32] + dot(z_rows[0:16], low, NT)
        for y in range(8):
            own = total if y == 0 else pltpu.roll(total, 128 - 16 * y, 1)
            at = pl.multiple_of(((role ^ flip) * 8 + y) * 16, 16)
            d_scr[pl.ds(at, 16), :] = jnp.where(lane < 16, own, 0.0)
    out[...] = dot3((kron[0], kron[1]), halves(d_scr[...]))


def input_coefs(pieces):
    return pl.pallas_call(
        coef_kernel,
        out_shape=shape_of(256, 128),
        scratch_shapes=[vmem((256, 128))],
        compiler_params=params(),
        name="input_coefs",
    )(*pieces, jnp.asarray(Z_HALF), jnp.asarray(KRON_Y))


def prep_kernel(first_row, piece0, piece1, piece2, piece3, weight, out_own, out_mixed):
    role_here, rep_here, _ = here()
    me = role_here * 2 + rep_here
    wide = square_weight(weight[...])
    lane = lanes_of((128, 128))
    for d, piece in enumerate((piece0, piece1, piece2, piece3)):
        source = me ^ d
        role, rep = source // 2, source % 2
        whole = jnp.concatenate(
            [piece[pl.ds(first_row + y, 16, stride=8), :] for y in range(8)], axis=0
        )
        turned = jnp.transpose(whole)
        for y in range(8):
            rows = pl.ds(pl.multiple_of((role * 8 + y) * 256 + rep * 128, 128), 128)
            own = turned if y == 0 else pltpu.roll(turned, 128 - 16 * y, 1)
            own = jnp.where(lane < 16, own, 0.0)
            sides = jnp.concatenate(halves(own), axis=1)
            out_own[rows, :] = sides if out_own.dtype == BF16 else own
            out_mixed[rows, :] = fold(dot(sides, wide))


def prepare(pieces, first_row, weight, as_sides, name):
    own = jax.ShapeDtypeStruct((CELLS, 256), BF16) if as_sides else shape_of(CELLS, 128)
    return pl.pallas_call(
        functools.partial(prep_kernel, first_row),
        out_shape=[own, shape_of(CELLS, 128)],
        compiler_params=params(),
        name=name,
    )(*pieces, weight)


GELU_A = math.sqrt(2.0 / math.pi)
GELU_B = 0.044715


def gelu_both(value):
    square = value * value
    t = jnp.tanh(value * (GELU_A + (GELU_A * GELU_B) * square))
    half = 0.5 + 0.5 * t
    hidden = value * half
    slope = half + hidden * (1.0 - half) * (2.0 * GELU_A + (6.0 * GELU_A * GELU_B) * square)
    return hidden, slope


BLOCK_Y = 4
BLOCK = BLOCK_Y * SZ
CHUNK = 128


def open_cells(spectrum, kron_t, c_scr):
    high, low = halves(dot3((kron_t[0], kron_t[1]), halves(spectrum[...])))
    for y in range(SY):
        lanes = slice(y % BLOCK_Y * 128, y % BLOCK_Y * 128 + 128)
        rows = slice(y * 16, y * 16 + 16)
        c_scr[y // BLOCK_Y, 0:16, lanes] = high[rows]
        c_scr[y // BLOCK_Y, 16:32, lanes] = low[rows]
        c_scr[y // BLOCK_Y, 32:48, lanes] = high[rows]


def chunk_of(wide, n):
    at = n * CHUNK
    return wide[at % SZ : at % SZ + CHUNK, at // SZ * 128 : at // SZ * 128 + 128]


def store_sides(out, rows, value):
    high, low = halves(value)
    out[rows, 0:128] = high
    out[rows, 128:256] = low


def cells_to(sides, z_rows, d_scr, step):
    for n in range(BLOCK_Y):
        out = dot(z_rows[...], sides[n * SZ : (n + 1) * SZ, :])
        at = pl.multiple_of((step * BLOCK_Y + n) * 16, 16)
        d_scr[pl.ds(at, 16), :] = out[0:16, 0:128] + out[0:16, 128:256] + out[16:32, 0:128]


def close_cells(kron, d_scr):
    return dot3((kron[0], kron[1]), halves(d_scr[...]))


def cells0_kernel(spectrum, pre, kron, kron_t, z_rows, z_cols, out_coef, out_h, out_slope, c_scr, d_scr):
    step = pl.program_id(0)

    @pl.when(step == 0)
    def _():
        open_cells(spectrum, kron_t, c_scr)

    spectral = dot(z_cols[...], c_scr[step])
    for n in range(BLOCK // CHUNK):
        rows = slice(n * CHUNK, (n + 1) * CHUNK)
        hidden, slope = gelu_both(chunk_of(spectral, n) + pre[rows, :])
        out_slope[rows, :] = slope
        store_sides(out_h, rows, hidden)
    cells_to(out_h, z_rows, d_scr, step)

    @pl.when(step == pl.num_programs(0) - 1)
    def _():
        out_coef[...] = close_cells(kron, d_scr)


def cells1_kernel(
    spectrum,
    h1,
    pull,
    w_point,
    w_square,
    kron,
    kron_t,
    z_rows,
    z_cols,
    out_coef,
    out_pre,
    out_h,
    c_scr,
    d_scr,
    wide,
    slopes,
):
    step = pl.program_id(0)

    @pl.when(step == 0)
    def _():
        open_cells(spectrum, kron_t, c_scr)
        wide[0] = square_weight(w_point[...])
        wide[1] = square_weight(w_square[...])

    spectral = dot(z_cols[...], c_scr[step])
    direct = dot(h1[...], wide[0])
    for n in range(BLOCK // CHUNK):
        rows = slice(n * CHUNK, (n + 1) * CHUNK)
        hidden, slope = gelu_both(chunk_of(spectral, n) + fold(direct[rows, :]))
        slopes[rows, :] = slope
        store_sides(out_h, rows, hidden)
    back = dot(out_h[...], wide[1])
    for n in range(BLOCK // CHUNK):
        rows = slice(n * CHUNK, (n + 1) * CHUNK)
        store_sides(out_pre, rows, (fold(back[rows, :]) - pull[rows, :]) * slopes[rows, :])
    cells_to(out_pre, z_rows, d_scr, step)

    @pl.when(step == pl.num_programs(0) - 1)
    def _():
        out_coef[...] = close_cells(kron, d_scr)


def cells2_kernel(
    spectrum,
    extra,
    grad1,
    slope0,
    w_point,
    kron,
    kron_t,
    z_rows,
    z_cols,
    out_coef,
    out_pre,
    c_scr,
    d_scr,
    wide,
):
    step = pl.program_id(0)

    @pl.when(step == 0)
    def _():
        open_cells(spectrum, kron_t, c_scr)
        wide[...] = square_weight(w_point[...])

    spectral = dot(z_cols[...], c_scr[step])
    direct = dot(grad1[...], wide[...])
    for n in range(BLOCK // CHUNK):
        rows = slice(n * CHUNK, (n + 1) * CHUNK)
        store_sides(
            out_pre, rows, (chunk_of(spectral, n) + fold(direct[rows, :])) * slope0[rows, :]
        )
    cells_to(out_pre, z_rows, d_scr, step)

    @pl.when(step == pl.num_programs(0) - 1)
    def _():
        out_coef[:, 0:8, :] = close_cells(kron, d_scr).reshape(TILES, 8, 128)
        out_coef[:, 8:16, :] = extra[...]


def cell_call(kernel, name, firsts, streams, weights, outs, scratch=(), coef=(256, 128), **order):
    def block(lanes):
        return pl.BlockSpec((BLOCK, lanes), lambda g: (g, 0))

    consts = [jnp.asarray(c) for c in (KRON_Y, KRON_YT, Z_ROWS, Z_COLS)]
    return call(
        kernel,
        [(v, full(v.shape)) for v in firsts]
        + [(v, block(v.shape[1])) for v in streams]
        + [(v, full(v.shape)) for v in (*weights, *consts)],
        [(shape_of(*coef), full(coef))]
        + [(jax.ShapeDtypeStruct((CELLS, lanes), kind), block(lanes)) for lanes, kind in outs],
        grid=(SY // BLOCK_Y,),
        scratch_shapes=[vmem((4, 48, 512), BF16), vmem((256, 128))] + list(scratch),
        name=name,
        room=CELL_ROOM,
        **order,
    )


def grads_kernel(scale, norm, grad, h1, h2, target, w_proj, out, point_acc, proj_acc, loss_acc, wide, row):
    step = pl.program_id(0)

    @pl.when(step == 0)
    def _():
        wide[...] = square_weight(w_proj[...])
        loss_acc[...] = jnp.zeros_like(loss_acc)

    point_acc[step] = dot(grad[...], h1[...], TN)
    err = fold(dot(h2[...], wide[...])) - target[...]
    loss_acc[...] += jnp.sum((err * err).reshape(BLOCK // 8, 8, 128), axis=0)
    sides = jnp.concatenate(halves(err * scale), axis=1)
    proj_acc[step] = dot(sides, h2[...], TN)

    @pl.when(step == pl.num_programs(0) - 1)
    def _():
        out[...] = jnp.zeros_like(out)
        point = sum(point_acc[n, 0:128, :] + point_acc[n, 128:256, :] for n in range(SY // BLOCK_Y))
        point = fold(point)
        picked = jnp.where(lanes_of((64, 128)) < 64, point[0:64], point[64:128])
        picked = picked + pltpu.roll(picked, 64, 1)
        out[:, 0, :] = jnp.where(lanes_of((32, 128)) < 64, picked[0:32], picked[32:64])
        proj = sum(proj_acc[n, 0:16, :] + proj_acc[n, 128:144, :] for n in range(SY // BLOCK_Y))
        proj = fold(proj)
        picked = jnp.where(lanes_of((8, 128)) < 64, proj[0:8], proj[8:16])
        turned = jnp.transpose(picked + pltpu.roll(picked, 64, 1))
        row[...] = jnp.full((32, 128), jnp.sum(loss_acc[...]) / norm)
        row[:, 0:8] = turned[0:32]
        row[:, 8:16] = turned[32:64]
        out[:, 1, :] = row[...]


def grads(norm, grad, h1, h2, target, w_proj):
    sides = pl.BlockSpec((BLOCK, 256), lambda g: (g, 0))
    return pl.pallas_call(
        functools.partial(grads_kernel, 2.0 / norm, norm),
        grid=(SY // BLOCK_Y,),
        out_shape=shape_of(TILES, 8, 128),
        in_specs=[sides, sides, sides, pl.BlockSpec((BLOCK, 128), lambda g: (g, 0)), full((128, 128))],
        out_specs=full((TILES, 8, 128)),
        scratch_shapes=[
            vmem((SY // BLOCK_Y, 256, 256)),
            vmem((SY // BLOCK_Y, 256, 256)),
            vmem((8, 128)),
            vmem((256, 256), BF16),
            vmem((32, 128)),
        ],
        compiler_params=params(),
        name="grads",
    )(grad, h1, h2, target, w_proj)


def kept_modes(counts, layer):
    row = rows_of((128, 128))
    pair = lax.axis_index("tile") * 8 + row // 16
    kept = (
        (row % 8 < counts[layer, 0])
        & (pair // 16 % 8 < counts[layer, 1])
        & (pair % 8 < counts[layer, 2])
    )
    return jnp.where(kept, 1.0, 0.0)


def pair_up(rows, low_lanes):
    picked = jnp.where(low_lanes, rows[0:128], rows[128:256])
    return picked + pltpu.roll(picked, 64, 1)


MIX_STEPS = 2
MIX_PAIRS = 8 // MIX_STEPS


def mix(g_scr, b_scr, weights, step, turned):
    row, lane = rows_of((16, 256)), lanes_of((16, 256))
    wanted = (lanes_of((16, 128)) >= 64) if turned else (lanes_of((16, 128)) < 64)
    for n in range(MIX_PAIRS):
        at = pl.multiple_of((step * MIX_PAIRS + n) * 16, 16)
        one = g_scr[pl.ds(at, 16), :]
        wide = jnp.concatenate([one, one], axis=1)
        total = jnp.zeros((32, 256), F32)
        for q in range(4):
            own = jnp.where(row == 4 * q + lane // 64, wide, 0.0)
            sides = jnp.concatenate(halves(own), axis=0)
            both = halves(weights[n, q * 256 : (q + 1) * 256, :])
            total = total + dot(sides, jnp.concatenate(both, axis=1))
        folded = fold(total[0:16]) + total[16:32, 0:128]
        folded = jnp.where(wanted, folded, 0.0)
        b_scr[pl.ds(at, 16), :] = folded + pltpu.roll(folded, 64, 1)


def close_modes(b_scr, kept, kron_t, out):
    both = b_scr[...] * kept
    low = lanes_of((128, 128)) < 64
    blocks = jnp.concatenate([jnp.where(low, both, 0.0), jnp.where(low, 0.0, both)], axis=0)
    out[...] = dot3((kron_t[0], kron_t[1]), halves(blocks))


def modes_first_kernel(counts, coef, lift, weights, kron, kron_t, out, out_in, out_a, a_scr, b_scr):
    step = pl.program_id(0)

    @pl.when(step == 0)
    def _():
        rows = dot3((kron[0], kron[1]), halves(coef[...]))
        picked = jnp.where(lanes_of((128, 128)) < 8, rows[0:128], rows[128:256])
        picked = picked * kept_modes(counts, 0)
        out_in[...] = picked
        lifted = dot3(halves(picked), halves(lift[...]))
        a_scr[...] = lifted
        out_a[...] = lifted

    mix(a_scr, b_scr, weights, step, True)

    @pl.when(step == pl.num_programs(0) - 1)
    def _():
        close_modes(b_scr, kept_modes(counts, 0), kron_t, out)


def modes_forward_kernel(counts, coef, weights, kron, kron_t, out, out_a, a_scr, b_scr):
    step = pl.program_id(0)

    @pl.when(step == 0)
    def _():
        rows = dot3((kron[0], kron[1]), halves(coef[...]))
        a = pair_up(rows, lanes_of((128, 128)) < 64) * kept_modes(counts, 1)
        a_scr[...] = a
        out_a[...] = a

    mix(a_scr, b_scr, weights, step, True)

    @pl.when(step == pl.num_programs(0) - 1)
    def _():
        close_modes(b_scr, kept_modes(counts, 1), kron_t, out)


def take_gradient(rows, kept, saved, g_scr, out_pair):
    low = lanes_of((128, 128)) < 64
    g = pair_up(rows, low) * kept
    g_scr[...] = g
    out_pair[...] = jnp.where(low, g, saved[...])


def modes_backward_kernel(
    counts, coef, saved, weights, kron, kron_t, out, out_pair, g_scr, b_scr
):
    step = pl.program_id(0)

    @pl.when(step == 0)
    def _():
        rows = dot3((kron[0], kron[1]), halves(coef[...]))
        take_gradient(rows, kept_modes(counts, 1), saved, g_scr, out_pair)

    mix(g_scr, b_scr, weights, step, False)

    @pl.when(step == pl.num_programs(0) - 1)
    def _():
        close_modes(b_scr, kept_modes(counts, 1), kron_t, out)


def modes_last_kernel(counts, coef, saved, inputs, point, weights, kron, kron_t, out, g_scr, b_scr):
    step = pl.program_id(0)

    @pl.when(step == 0)
    def _():
        value = coef[:, 0:8, :].reshape(256, 128)
        rows = dot3((kron[0], kron[1]), halves(value))
        take_gradient(rows, kept_modes(counts, 0), saved, g_scr, out.at[0:128])

    mix(g_scr, b_scr, weights, step, False)

    @pl.when(step == pl.num_programs(0) - 1)
    def _():
        turned = jnp.transpose(inputs[...])[0:16]
        lift = dot3(halves(turned), halves(b_scr[...]))
        lift = lift[0:8] + lift[8:16]
        direct = fold(point[0:16, :] + point[128:144, :])
        direct = direct[0:8] + pltpu.roll(direct[8:16], 64, 1)
        late = jnp.where(lanes_of((8, 128)) < 64, lift, pltpu.roll(direct, 64, 1))
        extra = pltpu.roll(jnp.sum(coef[:, 8:16, :], axis=0), 6, 0)
        out[128:136] = jnp.where(rows_of((8, 128)) < 6, late, extra)


def mode_call(kernel, name, layer, counts, smalls, weights, outs, **order):
    consts = [jnp.asarray(c) for c in (KRON_X, KRON_XT)]
    return call(
        kernel,
        [(counts, SMEM)]
        + [(v, full(v.shape)) for v in smalls]
        + [(weights, pl.BlockSpec((None, MIX_PAIRS, 1024, 128), lambda m: (layer, m, 0, 0)))]
        + [(v, full(v.shape)) for v in consts],
        [(shape_of(*o), full(o)) for o in outs],
        grid=(MIX_STEPS,),
        scratch_shapes=[vmem((128, 128)), vmem((128, 128))],
        name=name,
        room=MODE_ROOM,
        **order,
    )


OUTER_PAIRS = 4


def outer_kernel(*refs):
    layer = pl.program_id(0)
    out = refs[8]
    row, lane = rows_of((64, 1024)), lanes_of((64, 1024))
    own = row % 16 == lane // 64
    low = lanes_of((64, 128)) < 64
    for n in range(OUTER_PAIRS):
        rows = slice(n * 16, (n + 1) * 16)
        block = jnp.concatenate(
            [jnp.where(layer == 0, refs[d][rows, :], refs[4 + d][rows, :]) for d in range(4)],
            axis=0,
        )
        grads = halves(jnp.transpose(block)[0:64])
        twice = jnp.where(low, pltpu.roll(block, 64, 1), block)
        spread = halves(jnp.where(own, jnp.concatenate([twice] * 8, axis=1), 0.0))
        result = dot3(grads, spread)
        for r in range(16):
            out[n, r] = result[:, r * 64 : (r + 1) * 64]


def outer_products(pairs0, pairs1):
    block = pl.BlockSpec((OUTER_PAIRS * 16, 128), lambda l, m: (m, 0))
    return pl.pallas_call(
        outer_kernel,
        grid=(LAYERS, 8 // OUTER_PAIRS),
        out_shape=shape_of(LAYERS, 8, 16, 64, 64),
        in_specs=[block] * 8,
        out_specs=pl.BlockSpec((None, OUTER_PAIRS, 16, 64, 64), lambda l, m: (l, m, 0, 0, 0)),
        compiler_params=params(),
        name="outer",
    )(*pairs0, *pairs1)


def finish_kernel(late, point, lift, out_lift, out_point, out_proj, out_loss):
    by_tile = late[...]
    total = jnp.sum(by_tile, axis=0)
    total = jnp.where(rows_of((8, 128)) < 6, total, 0.0)
    through, direct = total[:, 0:64], pltpu.roll(total, 64, 1)[:, 0:64]

    def exact(a, b, dims):
        return lax.dot_general(a, b, dims, precision=PRECISE, preferred_element_type=F32)

    out_point[0] = exact(direct, lift[...], TN)
    through = through + exact(direct, point[...], NN)
    out_lift[...] = through[0:6]
    first = by_tile[:, 6, :]
    out_point[1, 0:32, :] = first[:, 0:64]
    out_point[1, 32:64, :] = first[:, 64:128]
    second = jnp.transpose(by_tile[:, 7, :])
    out_proj[:, 0:32] = second[0:6]
    out_proj[:, 32:64] = second[8:14]
    out_loss[...] = second[16:17, 0:1]


def finish(late, point, lift):
    return pl.pallas_call(
        finish_kernel,
        out_shape=[shape_of(6, 64), shape_of(2, 64, 64), shape_of(6, 64), shape_of(1, 1)],
        compiler_params=params(),
        name="finish",
    )(late, point, lift)


def passed(value, axis, by):
    length = lax.axis_size(axis)
    return lax.ppermute(value, axis, [(i, i + by) for i in range(length) if 0 <= i + by < length])


def across(value, axis):
    return lax.ppermute(value, axis, [(0, 1), (1, 0)])


def diagonal(value, by):
    pairs = []
    for q in range(2):
        for t in range(TILES):
            if 0 <= t + by < TILES:
                pairs.append((q * TILES + t, (1 - q) * TILES + t + by))
    return lax.ppermute(value, ("rep", "tile"), pairs)


def xor_group(value, d):
    return lax.ppermute(value, GROUP, [(i, i ^ d) for i in range(4)])


def parity_blocks(matrix):
    zero = jnp.zeros_like(matrix)
    return jnp.concatenate(
        [jnp.concatenate([matrix, zero], axis=1), jnp.concatenate([zero, matrix], axis=1)], axis=0
    )


def local(
    fields,
    material,
    permittivity,
    conductivity,
    plan,
    mode_counts,
    lift_weight,
    pointwise,
    spectral_weight,
    project_weight,
):
    weights = jnp.concatenate([spectral_weight, jnp.swapaxes(spectral_weight, -1, -2)], axis=-1)
    weights = weights.reshape(LAYERS, 8, 1024, 128)

    own0, ends_own0 = pack(fields.reshape(6, 4, 16, 256), material)
    low0, high0 = passed(own0, "tile", 1), passed(own0, "tile", -1)
    ends = (xor_group(ends_own0, 1), diagonal(ends_own0, 1), diagonal(ends_own0, -1))
    blocks = []
    for value in (own0, low0, high0, *ends):
        blocks += [value, across(value, "role")]
    new_fields, pieces = leapfrog(plan, permittivity, conductivity, blocks)
    pieces = [pieces[0]] + [xor_group(pieces[d], d) for d in range(1, 4)]
    coef = input_coefs(pieces)

    lift8 = jnp.pad(lift_weight.T, ((0, 2), (0, 0)))
    lift16 = jnp.concatenate([lift8, lift8], axis=0)
    lift_pad = jnp.pad(jnp.concatenate([lift16, lift16], axis=1), ((0, 112), (0, 0)))
    first8 = jnp.dot(lift8, pointwise[0].T, precision=PRECISE)
    first = jnp.pad(parity_blocks(first8), ((0, 112), (0, 0)))
    point1 = parity_blocks(pointwise[1])
    proj8 = jnp.pad(project_weight, ((0, 2), (0, 0)))
    proj_t = jnp.pad(parity_blocks(proj8), ((0, 112), (0, 0)))
    norm_count = 6.0 * SX * SY * SZ * plan.shape[0]
    scale = 2.0 / norm_count
    proj_square = jnp.dot(project_weight.T, project_weight, precision=PRECISE) * scale

    def swap(value):
        value = value.reshape(TILES, -1, 128)
        return lax.all_to_all(value, "tile", 0, 0, tiled=True)

    def swap_flat(value):
        return swap(value).reshape(256, 128)

    inputs, pre0 = prepare(pieces, 0, first, True, "prepare_inputs")
    spectrum, a_in, a0 = mode_call(
        modes_first_kernel,
        "modes_first",
        0,
        mode_counts,
        (swap_flat(coef), lift_pad),
        weights,
        ((256, 128), (128, 128), (128, 128)),
        after=(pre0,),
    )
    target, pull = prepare(pieces, 128, proj_t * scale, False, "prepare_target")
    sides, plain_out = (256, BF16), (128, F32)
    coef, h1, slope0 = cell_call(
        cells0_kernel,
        "cells0",
        (swap_flat(spectrum),),
        (pre0,),
        (),
        (sides, plain_out),
        after=(pull,),
    )
    spectrum, a1 = mode_call(
        modes_forward_kernel,
        "modes_forward",
        1,
        mode_counts,
        (swap_flat(coef),),
        weights,
        ((256, 128), (128, 128)),
    )
    coef, grad1, h2 = cell_call(
        cells1_kernel,
        "cells1",
        (swap_flat(spectrum),),
        (h1, pull),
        (point1.T, parity_blocks(proj_square)),
        (sides, sides),
        scratch=(vmem((2, 256, 256), BF16), vmem((BLOCK, 128))),
    )
    extra = grads(norm_count, grad1, h1, h2, target, proj_t.T)
    spectrum, pair1 = mode_call(
        modes_backward_kernel,
        "modes_backward",
        1,
        mode_counts,
        (swap_flat(coef), a1),
        weights,
        ((256, 128), (128, 128)),
        after=(extra,),
    )
    pairs = [pair1] + [xor_group(pair1, d) for d in range(1, 4)]
    coef, grad0 = cell_call(
        cells2_kernel,
        "cells2",
        (swap_flat(spectrum), extra),
        (grad1, slope0),
        (point1,),
        (sides,),
        scratch=(vmem((256, 256), BF16),),
        coef=(TILES, 16, 128),
        after=pairs[1:],
    )
    direct = lax.dot_general(inputs, grad0, TN, preferred_element_type=F32)
    (tail,) = mode_call(
        modes_last_kernel,
        "modes_last",
        0,
        mode_counts,
        (swap(coef), a0, a_in, direct),
        weights,
        ((136, 128),),
    )
    tails = [tail] + [xor_group(tail, d) for d in range(1, 4)]
    late = [t[128:136] for t in tails]
    late = (late[0] + late[1]) + (late[2] + late[3])
    late = swap(jnp.broadcast_to(late, (TILES, 8, 128)))
    spectral_grad = outer_products(tails, pairs)
    lift_grad, point_grad, proj_grad, loss = finish(late, pointwise[0], lift8)
    return (
        new_fields.reshape(2, 3, 4, 16, 256),
        lift_grad.T,
        point_grad,
        spectral_grad,
        proj_grad,
        loss[0, 0],
    )


def solution(mesh):
    return jax.shard_map(
        local,
        mesh=mesh,
        in_specs=(
            P(None, None, "tile", "role", "rep"),
            P("tile", "role", "rep"),
            P(),
            P(),
            P(),
            P(),
            P(),
            P(),
            P(None, "tile", None, None, None),
            P(),
        ),
        out_specs=(
            P(None, None, "tile", "role", "rep"),
            P(),
            P(),
            P(None, "tile", None, None, None),
            P(),
            P(),
        ),
        check_vma=False,
    )
```

time: 333 us -> 234 us (0.70)
  blocking collectives: 67.4 us -> 0 us
  Pallas kernels: 104 us -> 69.3 us
  matrix products: 17.9 us -> 4.05 us
  waiting for transfers between devices: 29.4 us -> 42.7 us
  other arithmetic: 10.8 us -> 15.7 us
    psum x1 -> x0, blocking collectives: 67.4 us -> none  [local(): lax.psum((point_grad1, proj_grad, jnp.sum(loss) / norm_count), EVERY)]
    pallas_call x10 -> x14, Pallas kernels: 102 us -> 67.5 us  [the longest x8 42.1 us: call(): pl.pallas_call(run, out_shape=[o[0] for o in outs] + [jax.ShapeDtypeStruc...]
    ppermute x6 -> x10, waiting for transfers between devices: 0.02 us -> 19.2 us  [xor_group(): return lax.ppermute(value, GROUP, [(i, i ^ d) for i in range(4)])]
    dot_general x5 -> x2, matrix products: 17 us -> 3.91 us  [the longest x1 3.67 us: local(): direct = lax.dot_general(inputs, grad0, TN, preferred_element_type=F32)]
    concatenate x3 -> x2, other arithmetic: 1.91 us -> 12.8 us  [the longest x1 12.1 us: local(): jnp.concatenate([spectral_weight, jnp.swapaxes(spectral_weight, -1, -2)],...]
    ppermute x6 -> x10, starting transfers between devices: 7.93 us -> 18.6 us  [xor_group(): return lax.ppermute(value, GROUP, [(i, i ^ d) for i in range(4)])]
    ppermute x2, waiting for transfers between devices: 7.69 us -> 0.01 us  [passed(): lax.ppermute(value, axis, [(i, i + by) for i in range(length) if 0 <= i +...]
    unnamed x68 -> x55, local copies, waits for them, and re-layouts: 7.04 us -> 14.6 us
  transfers between devices with their start and end apart: 25 -> 28, of which waited for: 11 -> 16; matrix products, arithmetic and copies ran while one was open for 10% -> 13% of each run, Pallas kernels for 13% -> 9%
where the time goes in v2:
time: 234 us; the launch traced here: 231 us
  starting transfers between devices  79.8 us (34%)
  Pallas kernels  69.3 us (30%)
  waiting for transfers between devices  42.7 us (18%)
  local copies, waits for them, and re-layouts  18.8 us (8%)
  other arithmetic  15.7 us (7%)
  matrix products  4.05 us (2%)
    all_to_all x8, starting transfers between devices, swap(): return lax.all_to_all(value, 'tile', 0, 0, tiled=True)  46.4 us
    pallas_call x8, Pallas kernels, call(): pl.pallas_call(run, out_shape=[o[0] for o in outs] + [jax.ShapeDtypeStruc...  42.1 us
    all_to_all x8, waiting for transfers between devices, swap(): return lax.all_to_all(value, 'tile', 0, 0, tiled=True)  22.8 us
    ppermute x10, waiting for transfers between devices, xor_group(): return lax.ppermute(value, GROUP, [(i, i ^ d) for i in range(4)])  19.2 us
    ppermute x10, starting transfers between devices, xor_group(): return lax.ppermute(value, GROUP, [(i, i ^ d) for i in range(4)])  18.6 us
    unnamed x55, local copies, waits for them, and re-layouts  14.6 us
    concatenate x1, other arithmetic, local(): jnp.concatenate([spectral_weight, jnp.swapaxes(spectral_weight, -1, -2)],...  12.1 us
    pallas_call x2, Pallas kernels, prepare(): pl.pallas_call(functools.partial(prep_kernel, first_row), out_shape=[own,...  8.04 us
  transfers between devices with their start and end apart: 28, of which 16 were waited for; matrix products, arithmetic and copies ran while one was open for 13% of the time, Pallas kernels for 9%

profile of v2, /device:TPU:1, one launch (start us, length us, event | category | flops | bytes accessed | tf_op | source)
XLA Modules:
  0.0 231.2 jit_solution(7527779013111738469)
XLA Ops:
  0.6 1.9 pack.1
  2.5 4.4 %collective-permute-start.1 = (f32[7,4,16,256]{3,2,1,0:T(8,128)}, f32[7,4,16,256]{3,2,1,0:T(8,128)S(1)}, u32[]{:S(2)}, u32[]{:S(2)}) collective-permute-start(f32[7,4,16,256]{3,2,1,0:T(8,128)} %get-tuple-element.33.refs_3_), channel_id=1, source_target_pairs={{0,1},{1,2},{2,3},{3,4},{4,5},{5,6},{6,7},{7,8},{8,9},{9,10},{10,1... | collective-permute-start | bytes 1376264 | tf_op jit(solution)/shard_map/ppermute | solution.py:847
  6.9 1.3 collective-permute-start.3
  8.2 3.4 %collective-permute-start.5 = (f32[8,512]{1,0:T(8,128)}, f32[8,512]{1,0:T(8,128)S(1)}, u32[]{:S(2)}, u32[]{:S(2)}) collective-permute-start(f32[8,512]{1,0:T(8,128)} %get-tuple-element.34), channel_id=1, source_target_pairs={{0,32},{32,0},{64,96},{96,64},{1,33},{33,1},{65,97},{97,65},{2,34}... | collective-permute-start | bytes 49160 | tf_op jit(solution)/shard_map/ppermute | solution.py:864
  11.6 3.1 %collective-permute-start.7 = (f32[8,512]{1,0:T(8,128)}, f32[8,512]{1,0:T(8,128)S(1)}, u32[]{:S(2)}, u32[]{:S(2)}) collective-permute-start(f32[8,512]{1,0:T(8,128)} %get-tuple-element.34), channel_id=1, source_target_pairs={{0,33},{1,34},{2,35},{3,36},{4,37},{5,38},{6,39},{7,40},{8,41},{9,... | collective-permute-start | bytes 49160 | tf_op jit(solution)/shard_map/ppermute | solution.py:860
  14.6 1.9 collective-permute-start
  16.5 8.7 %copy.28 = f32[2,8,16,64,64]{3,4,2,1,0:T(8,128)} copy(f32[2,8,16,64,64]{4,3,2,1,0:T(8,128)} %param.26) | data formatting | bytes 8388608 | tf_op args[8]
  25.2 5.0 %collective-permute-done.5.refs_9_ = f32[8,512]{1,0:T(8,128)S(1)} collective-permute-done((f32[8,512]{1,0:T(8,128)}, f32[8,512]{1,0:T(8,128)S(1)}, u32[]{:S(2)}, u32[]{:S(2)}) %collective-permute-start.5) | collective-permute-done | bytes 16416 | tf_op jit(solution)/shard_map/ppermute | solution.py:864
  30.2 1.3 collective-permute-start.9
  31.5 1.9 collective-permute-start.6
  34.0 12.1 %pad_maximum_fusion = f32[2,8,16,64,128]{4,3,2,1,0:T(8,128)} fusion(f32[2,8,16,64,64]{4,3,2,1,0:T(8,128)} %bitcast.44, f32[2,8,16,64,64]{4,3,2,1,0:T(8,128)} %param.26), kind=kLoop, calls=%fused_computation | loop fusion | flops 2097152 | bytes 16777216 | tf_op jit(solution)/shard_map/concatenate | solution.py:886
  47.5 5.4 %leapfrog.1 = (f32[6,4,16,256]{3,2,1,0:T(8,128)}, f32[4,256,128]{2,1,0:T(8,128)S(1)}) custom-call(s32[4]{0:T(128)S(1)} %copy-done.2, f32[4]{0:T(128)S(1)} %copy-done.3, f32[4]{0:T(128)S(1)} %copy-done.4, f32[7,4,16,256]{3,2,1,0:T(8,128)S(1)} %copy-done, f32[7,4,16,256]{3,2,1,0:T(8,128)S(1)} %collective-permute-done.refs_4_, ...), custom_call_target="tpu_custom_call" | custom-call | tf_op jit(solution)/shard_map/leapfrog/pallas_call | solution.py:122
  52.9 0.7 slice_bitcast_fusion
  53.9 3.1 %collective-permute-start.13 = (f32[256,128]{1,0:T(8,128)S(1)}, f32[256,128]{1,0:T(8,128)S(1)}, u32[]{:S(2)}, u32[]{:S(2)}) collective-permute-start(f32[256,128]{1,0:T(8,128)S(1)} %get-tuple-element.60), channel_id=1, source_target_pairs={{0,96},{32,64},{64,32},{96,0},{1,97},{33,65},{65,33},{97,1},{2,98}... | collective-permute-start | bytes 393224 | tf_op jit(solution)/shard_map/ppermute | solution.py:864
  57.9 1.9 collective-permute-done.11.piece1
  59.8 3.3 %collective-permute-done.13.piece3 = f32[256,128]{1,0:T(8,128)S(1)} collective-permute-done((f32[256,128]{1,0:T(8,128)S(1)}, f32[256,128]{1,0:T(8,128)S(1)}, u32[]{:S(2)}, u32[]{:S(2)}) %collective-permute-start.13) | collective-permute-done | bytes 131104 | tf_op jit(solution)/shard_map/ppermute | solution.py:864
  63.7 2.5 %input_coefs.1 = f32[256,128]{1,0:T(8,128)} custom-call(f32[256,128]{1,0:T(8,128)} %get-tuple-element.63.piece0, f32[256,128]{1,0:T(8,128)} %copy-done.5, f32[256,128]{1,0:T(8,128)} %copy-done.6, f32[256,128]{1,0:T(8,128)} %copy-done.7, bf16[2,32,128]{2,1,0:T(8,128)(2,1)} %constant.9.clone.z_half, bf16[2,256,256]{2,1,0:T(8,128)(2,1)} %constant.26.clone.kron.refs_2_.refs_5_), custom_call_target="tpu_custom_call" | custom-call | tf_op jit(solution)/shard_map/input_coefs/pallas_call | solution.py:369
  66.3 8.8 %all-to-all-start = ((f32[32,8,128]{2,1,0:T(8,128)}), f32[32,8,128]{2,1,0:T(8,128)S(1)}, u32[]{:S(2)}, u32[]{:S(2)}) async-start(f32[32,8,128]{2,1,0:T(8,128)} %bitcast.50), calls=%async_computation | async-start | bytes 262144 | tf_op jit(solution)/shard_map/all_to_all | solution.py:913
  75.8 0.7 copy.30.weight
  76.5 0.7 fusion.refs_2_
  77.2 4.0 %prepare_inputs.1 = (bf16[4096,256]{1,0:T(8,128)(2,1)}, f32[4096,128]{1,0:T(8,128)}) custom-call(f32[256,128]{1,0:T(8,128)} %get-tuple-element.63.piece0, f32[256,128]{1,0:T(8,128)} %copy-done.5, f32[256,128]{1,0:T(8,128)} %copy-done.6, f32[256,128]{1,0:T(8,128)} %copy-done.7, f32[128,128]{1,0:T(8,128)} %pad.27.weight), custom_call_target="tpu_custom_call" | custom-call | tf_op jit(solution)/shard_map/prepare_inputs/pallas_call | solution.py:401
  81.2 1.3 all-to-all-done
  82.5 0.6 copy-done.9
  83.1 4.3 %modes_first.1 = (f32[256,128]{1,0:T(8,128)}, f32[128,128]{1,0:T(8,128)}, f32[128,128]{1,0:T(8,128)}) custom-call(s32[2,3]{1,0:T(2,128)} %refs_0_.9, f32[256,128]{1,0:T(8,128)} %bitcast.45, f32[128,128]{1,0:T(8,128)} %fusion.refs_2_, f32[2,8,1024,128]{3,2,1,0:T(8,128)} %bitcast.40, bf16[2,256,256]{2,1,0:T(8,128)(2,1)} %constant.27.clone.refs_4_.refs_3_.refs_6_, ...), custom_call_target="tpu_custom_call" | custom-call | tf_op jit(solution)/shard_map/modes_first/pallas_call | solution.py:122
  87.5 6.3 %all-to-all-start.1 = ((f32[32,8,128]{2,1,0:T(8,128)}), f32[32,8,128]{2,1,0:T(8,128)S(1)}, u32[]{:S(2)}, u32[]{:S(2)}) async-start(f32[32,8,128]{2,1,0:T(8,128)} %bitcast.54), calls=%async_computation.1 | async-start | bytes 262144 | tf_op jit(solution)/shard_map/all_to_all | solution.py:913
  94.3 4.0 %prepare_target.1 = (f32[4096,128]{1,0:T(8,128)}, f32[4096,128]{1,0:T(8,128)}) custom-call(f32[256,128]{1,0:T(8,128)} %get-tuple-element.63.piece0, f32[256,128]{1,0:T(8,128)} %copy-done.5, f32[256,128]{1,0:T(8,128)} %copy-done.6, f32[256,128]{1,0:T(8,128)} %copy-done.7, f32[128,128]{1,0:T(8,128)} %copy.30.weight), custom_call_target="tpu_custom_call" | custom-call | tf_op jit(solution)/shard_map/prepare_target/pallas_call | solution.py:401
  98.4 2.7 %all-to-all-done.1 = f32[32,8,128]{2,1,0:T(8,128)S(1)} async-done(((f32[32,8,128]{2,1,0:T(8,128)}), f32[32,8,128]{2,1,0:T(8,128)S(1)}, u32[]{:S(2)}, u32[]{:S(2)}) %all-to-all-start.1) | async-done | bytes 131104 | tf_op jit(solution)/shard_map/all_to_all | solution.py:913
  101.7 6.1 %cells0.1 = (f32[256,128]{1,0:T(8,128)}, bf16[4096,256]{1,0:T(8,128)(2,1)}, f32[4096,128]{1,0:T(8,128)}) custom-call(f32[256,128]{1,0:T(8,128)} %bitcast.48, f32[4096,128]{1,0:T(8,128)} %get-tuple-element.37.refs_6_.refs_1_, bf16[2,256,256]{2,1,0:T(8,128)(2,1)} %constant.26.clone.kron.refs_2_.refs_5_, bf16[2,256,256]{2,1,0:T(8,128)(2,1)} %constant.29.clone.refs_3_.refs_6_, ...), custom_call_target="tpu_custom_call" | custom-call | tf_op jit(solution)/shard_map/cells0/pallas_call | solution.py:122
  107.8 5.0 %all-to-all-start.2 = ((f32[32,8,128]{2,1,0:T(8,128)}), f32[32,8,128]{2,1,0:T(8,128)S(1)}, u32[]{:S(2)}, u32[]{:S(2)}) async-start(f32[32,8,128]{2,1,0:T(8,128)} %bitcast.57), calls=%async_computation.2 | async-start | bytes 262144 | tf_op jit(solution)/shard_map/all_to_all | solution.py:913
  113.1 7.1 %all-to-all-done.2 = f32[32,8,128]{2,1,0:T(8,128)S(1)} async-done(((f32[32,8,128]{2,1,0:T(8,128)}), f32[32,8,128]{2,1,0:T(8,128)S(1)}, u32[]{:S(2)}, u32[]{:S(2)}) %all-to-all-start.2) | async-done | bytes 131104 | tf_op jit(solution)/shard_map/all_to_all | solution.py:913
  120.1 0.7 copy-done.11
  120.8 4.1 %modes_forward.1 = (f32[256,128]{1,0:T(8,128)}, f32[128,128]{1,0:T(8,128)}) custom-call(s32[2,3]{1,0:T(2,128)} %refs_0_.9, f32[256,128]{1,0:T(8,128)} %bitcast.47, f32[2,8,1024,128]{3,2,1,0:T(8,128)} %bitcast.41, bf16[2,256,256]{2,1,0:T(8,128)(2,1)} %constant.27.clone.refs_4_.refs_3_.refs_6_, bf16[2,256,256]{2,1,0:T(8,128)(2,1)} %constant.28.clone.refs_5_.refs_4_.refs_7_), custom_call_target="tpu_custom_call" | custom-call | tf_op jit(solution)/shard_map/modes_forward/pallas_call | solution.py:122
  124.9 4.0 %all-to-all-start.3 = ((f32[32,8,128]{2,1,0:T(8,128)}), f32[32,8,128]{2,1,0:T(8,128)S(1)}, u32[]{:S(2)}, u32[]{:S(2)}) async-start(f32[32,8,128]{2,1,0:T(8,128)} %bitcast.56), calls=%async_computation.3 | async-start | bytes 262144 | tf_op jit(solution)/shard_map/all_to_all | solution.py:913
  128.9 0.7 select_maximum_fusion.1
  129.6 0.7 copy.31.refs_3_
  130.3 0.7 select_maximum_fusion.refs_4_
  131.0 5.2 %all-to-all-done.3 = f32[32,8,128]{2,1,0:T(8,128)S(1)} async-done(((f32[32,8,128]{2,1,0:T(8,128)}), f32[32,8,128]{2,1,0:T(8,128)S(1)}, u32[]{:S(2)}, u32[]{:S(2)}) %all-to-all-start.3) | async-done | bytes 131104 | tf_op jit(solution)/shard_map/all_to_all | solution.py:913
  136.2 0.6 copy-done.13
  136.9 7.7 %cells1.1 = (f32[256,128]{1,0:T(8,128)}, bf16[4096,256]{1,0:T(8,128)(2,1)}, bf16[4096,256]{1,0:T(8,128)(2,1)}) custom-call(f32[256,128]{1,0:T(8,128)} %bitcast.49, bf16[4096,256]{1,0:T(8,128)(2,1)} %get-tuple-element.42.refs_1_.h1, f32[4096,128]{1,0:T(8,128)} %get-tuple-element.39.refs_6_.refs_2_, f32[128,128]{1,0:T(8,128)} %copy.31.refs_3_, ...), custom_call_target="tpu_custom_call" | custom-call | tf_op jit(solution)/shard_map/cells1/pallas_call | solution.py:122
  144.5 4.0 %all-to-all-start.4 = ((f32[32,8,128]{2,1,0:T(8,128)}), f32[32,8,128]{2,1,0:T(8,128)S(1)}, u32[]{:S(2)}, u32[]{:S(2)}) async-start(f32[32,8,128]{2,1,0:T(8,128)} %bitcast.55), calls=%async_computation.4 | async-start | bytes 262144 | tf_op jit(solution)/shard_map/all_to_all | solution.py:913
  148.5 6.7 %grads.1.refs_6_.refs_1_ = f32[32,8,128]{2,1,0:T(8,128)} custom-call(bf16[4096,256]{1,0:T(8,128)(2,1)} %get-tuple-element.45.grad.refs_2_, bf16[4096,256]{1,0:T(8,128)(2,1)} %get-tuple-element.42.refs_1_.h1, bf16[4096,256]{1,0:T(8,128)(2,1)} %get-tuple-element.46.h2, f32[4096,128]{1,0:T(8,128)} %get-tuple-element.47.target, f32[128,128]{1,0:T(8,128)} %get-tuple-element.66.w_proj), custom_call_target="tpu_custom_call" | custom-call | tf_op jit(solution)/shard_map/grads/pallas_call | solution.py:615
  155.2 0.6 all-to-all-done.4
  156.5 4.1 %modes_backward.1 = (f32[256,128]{1,0:T(8,128)}, f32[128,128]{1,0:T(8,128)}) custom-call(s32[2,3]{1,0:T(2,128)} %refs_0_.9, f32[256,128]{1,0:T(8,128)} %bitcast.46, f32[128,128]{1,0:T(8,128)} %get-tuple-element.44.refs_2_, f32[2,8,1024,128]{3,2,1,0:T(8,128)} %bitcast.42, bf16[2,256,256]{2,1,0:T(8,128)(2,1)} %constant.27.clone.refs_4_.refs_3_.refs_6_, ...), custom_call_target="tpu_custom_call" | custom-call | tf_op jit(solution)/shard_map/modes_backward/pallas_call | solution.py:122
  160.6 7.1 %all-to-all-start.5 = ((f32[32,8,128]{2,1,0:T(8,128)}), f32[32,8,128]{2,1,0:T(8,128)S(1)}, u32[]{:S(2)}, u32[]{:S(2)}) async-start(f32[32,8,128]{2,1,0:T(8,128)} %bitcast.53), calls=%async_computation.5 | async-start | bytes 262144 | tf_op jit(solution)/shard_map/all_to_all | solution.py:913
  167.7 2.9 %collective-permute-start.14 = (f32[128,128]{1,0:T(8,128)}, f32[128,128]{1,0:T(8,128)S(1)}, u32[]{:S(2)}, u32[]{:S(2)}) collective-permute-start(f32[128,128]{1,0:T(8,128)} %get-tuple-element.50.refs_4_), channel_id=1, source_target_pairs={{0,32},{32,0},{64,96},{96,64},{1,33},{33,1},{65,97},{97,65},{2,34}... | collective-permute-start | bytes 196616 | tf_op jit(solution)/shard_map/ppermute | solution.py:864
  170.6 4.5 %collective-permute-start.15 = (f32[128,128]{1,0:T(8,128)}, f32[128,128]{1,0:T(8,128)S(1)}, u32[]{:S(2)}, u32[]{:S(2)}) collective-permute-start(f32[128,128]{1,0:T(8,128)} %get-tuple-element.50.refs_4_), channel_id=1, source_target_pairs={{0,64},{32,96},{64,0},{96,32},{1,65},{33,97},{65,1},{97,33},{2,66}... | collective-permute-start | bytes 196616 | tf_op jit(solution)/shard_map/ppermute | solution.py:864
  175.2 1.0 collective-permute-done.15.refs_10_.refs_6_
  176.2 4.5 %collective-permute-done.16.refs_11_.refs_7_ = f32[128,128]{1,0:T(8,128)S(1)} collective-permute-done((f32[128,128]{1,0:T(8,128)}, f32[128,128]{1,0:T(8,128)S(1)}, u32[]{:S(2)}, u32[]{:S(2)}) %collective-permute-start.16) | collective-permute-done | bytes 65568 | tf_op jit(solution)/shard_map/ppermute | solution.py:864
  181.4 6.3 %cells2.1 = (f32[32,16,128]{2,1,0:T(8,128)}, bf16[4096,256]{1,0:T(8,128)(2,1)}) custom-call(f32[256,128]{1,0:T(8,128)} %bitcast.51, f32[32,8,128]{2,1,0:T(8,128)} %grads.1.refs_6_.refs_1_, bf16[4096,256]{1,0:T(8,128)(2,1)} %get-tuple-element.45.grad.refs_2_, f32[4096,128]{1,0:T(8,128)} %get-tuple-element.49.refs_3_, f32[128,128]{1,0:T(8,128)} %get-tuple-element.68.refs_4_, ...), custom_call_target="tpu_custom_call" | custom-call | tf_op jit(solution)/shard_map/cells2/pallas_call | solution.py:122
  187.7 7.4 %all-to-all-start.6 = ((f32[32,16,128]{2,1,0:T(8,128)}), f32[32,16,128]{2,1,0:T(8,128)S(1)}, u32[]{:S(2)}, u32[]{:S(2)}) async-start(f32[32,16,128]{2,1,0:T(8,128)} %get-tuple-element.51), calls=%async_computation.6 | async-start | bytes 524288 | tf_op jit(solution)/shard_map/all_to_all | solution.py:913
  195.2 3.7 %fusion.6.refs_4_ = f32[256,256]{1,0:T(8,128)} fusion(bf16[4096,256]{1,0:T(8,128)(2,1)} %get-tuple-element.54, bf16[4096,256]{1,0:T(8,128)(2,1)} %get-tuple-element.55), kind=kOutput, calls=%fused_computation.29 | convolution fusion | flops 536870912 | bytes 4456448 | tf_op jit(solution)/shard_map/dot_general | solution.py:981
  198.8 4.9 %all-to-all-done.6.refs_1_ = f32[32,16,128]{2,1,0:T(8,128)S(1)} async-done(((f32[32,16,128]{2,1,0:T(8,128)}), f32[32,16,128]{2,1,0:T(8,128)S(1)}, u32[]{:S(2)}, u32[]{:S(2)}) %all-to-all-start.6) | async-done | bytes 262176 | tf_op jit(solution)/shard_map/all_to_all | solution.py:913
  203.7 0.7 copy-done.8
  204.4 4.1 %modes_last.1.refs_0_ = f32[136,128]{1,0:T(8,128)} custom-call(s32[2,3]{1,0:T(2,128)} %refs_0_.9, f32[32,16,128]{2,1,0:T(8,128)} %copy-done.8, f32[128,128]{1,0:T(8,128)} %get-tuple-element.52.refs_2_, f32[128,128]{1,0:T(8,128)} %get-tuple-element.53.refs_3_, f32[256,256]{1,0:T(8,128)} %fusion.6.refs_4_, f32[2,8,1024,128]{3,2,1,0:T(8,128)} %bitcast.43, ...), custom_call_target="tpu_custom_call" | custom-call | tf_op jit(solution)/shard_map/modes_last/pallas_call | solution.py:122
  208.5 2.8 %collective-permute-start.19 = (f32[136,128]{1,0:T(8,128)}, f32[136,128]{1,0:T(8,128)S(1)}, u32[]{:S(2)}, u32[]{:S(2)}) collective-permute-start(f32[136,128]{1,0:T(8,128)} %modes_last.1.refs_0_), channel_id=1, source_target_pairs={{0,96},{32,64},{64,32},{96,0},{1,97},{33,65},{65,33},{97,1},{2,98}... | collective-permute-start | bytes 208904 | tf_op jit(solution)/shard_map/ppermute | solution.py:864
  211.3 1.4 collective-permute-start.17
  212.7 1.7 collective-permute-done.19.refs_3_
  214.4 1.8 collective-permute-done.17.refs_1_
  216.2 0.7 fusion.1
  216.9 0.7 broadcast_in_dim.3
  217.5 3.8 %all-to-all-start.7 = ((f32[32,8,128]{2,1,0:T(8,128)}), f32[32,8,128]{2,1,0:T(8,128)S(1)}, u32[]{:S(2)}, u32[]{:S(2)}) async-start(f32[32,8,128]{2,1,0:T(8,128)} %broadcast_in_dim.3), calls=%async_computation.7 | async-start | bytes 262144 | tf_op jit(solution)/shard_map/all_to_all | solution.py:913
  221.4 6.2 %outer.1 = f32[2,8,16,64,64]{4,3,2,1,0:T(8,128)} custom-call(f32[136,128]{1,0:T(8,128)} %modes_last.1.refs_0_, f32[136,128]{1,0:T(8,128)} %copy-done.22, f32[136,128]{1,0:T(8,128)} %copy-done.21, f32[136,128]{1,0:T(8,128)} %copy-done.20, f32[128,128]{1,0:T(8,128)} %get-tuple-element.50.refs_4_, f32[128,128]{1,0:T(8,128)} %copy-done.16, ...), custom_call_target="tpu_custom_call" | custom-call | tf_op jit(solution)/shard_map/outer/pallas_call | solution.py:804
  227.6 1.1 all-to-all-done.7.late
  229.3 1.9 finish.1
  (82 shorter events, 8.0 us)
Async XLA Ops:
  2.5 30.9 %collective-permute-start.1 = (f32[7,4,16,256]{3,2,1,0:T(8,128)}, f32[7,4,16,256]{3,2,1,0:T(8,128)S(1)}, u32[]{:S(2)}, u32[]{:S(2)}) collective-permute-start(f32[7,4,16,256]{3,2,1,0:T(8,128)} %get-tuple-element.33.refs_3_), channel_id=1, source_target_pairs={{0,1},{1,2},{2,3},{3,4},{4,5},{5,6},{6,7},{7,8},{8,9},{9,10},{10,1... | collective-permute-start | bytes 1376264 | tf_op jit(solution)/shard_map/ppermute | solution.py:847
  6.9 26.6 %collective-permute-start.3 = (f32[7,4,16,256]{3,2,1,0:T(8,128)}, f32[7,4,16,256]{3,2,1,0:T(8,128)S(1)}, u32[]{:S(2)}, u32[]{:S(2)}) collective-permute-start(f32[7,4,16,256]{3,2,1,0:T(8,128)} %get-tuple-element.33.refs_3_), channel_id=1, source_target_pairs={{1,0},{2,1},{3,2},{4,3},{5,4},{6,5},{7,6},{8,7},{9,8},{10,9},{11,1... | collective-permute-start | bytes 1376264 | tf_op jit(solution)/shard_map/ppermute | solution.py:847
  8.2 22.0 %copy-start.26 = (f32[8,512]{1,0:T(8,128)S(1)}, f32[8,512]{1,0:T(8,128)}, u32[]{:S(2)}) copy-start(f32[8,512]{1,0:T(8,128)} %get-tuple-element.34) | copy-start | bytes 49156
  8.2 22.0 %collective-permute-start.5 = (f32[8,512]{1,0:T(8,128)}, f32[8,512]{1,0:T(8,128)S(1)}, u32[]{:S(2)}, u32[]{:S(2)}) collective-permute-start(f32[8,512]{1,0:T(8,128)} %get-tuple-element.34), channel_id=1, source_target_pairs={{0,32},{32,0},{64,96},{96,64},{1,33},{33,1},{65,97},{97,65},{2,34}... | collective-permute-start | bytes 49160 | tf_op jit(solution)/shard_map/ppermute | solution.py:864
  11.6 19.9 %collective-permute-start.7 = (f32[8,512]{1,0:T(8,128)}, f32[8,512]{1,0:T(8,128)S(1)}, u32[]{:S(2)}, u32[]{:S(2)}) collective-permute-start(f32[8,512]{1,0:T(8,128)} %get-tuple-element.34), channel_id=1, source_target_pairs={{0,33},{1,34},{2,35},{3,36},{4,37},{5,38},{6,39},{7,40},{8,41},{9,... | collective-permute-start | bytes 49160 | tf_op jit(solution)/shard_map/ppermute | solution.py:860
  14.6 32.8 %collective-permute-start = (f32[7,4,16,256]{3,2,1,0:T(8,128)}, f32[7,4,16,256]{3,2,1,0:T(8,128)S(1)}, u32[]{:S(2)}, u32[]{:S(2)}) collective-permute-start(f32[7,4,16,256]{3,2,1,0:T(8,128)} %get-tuple-element.33.refs_3_), channel_id=1, source_target_pairs={{0,64},{64,0},{1,65},{65,1},{2,66},{66,2},{3,67},{67,3},{4,68},{68... | collective-permute-start | bytes 1376264 | tf_op jit(solution)/shard_map/ppermute | solution.py:851
  30.2 15.9 %collective-permute-start.9 = (f32[8,512]{1,0:T(8,128)S(1)}, f32[8,512]{1,0:T(8,128)S(1)}, u32[]{:S(2)}, u32[]{:S(2)}) collective-permute-start(f32[8,512]{1,0:T(8,128)S(1)} %copy-done.26), channel_id=1, source_target_pairs={{1,32},{2,33},{3,34},{4,35},{5,36},{6,37},{7,38},{8,39},{9,40},{10... | collective-permute-start | bytes 49160 | tf_op jit(solution)/shard_map/ppermute | solution.py:860
  31.5 14.7 %collective-permute-start.6 = (f32[8,512]{1,0:T(8,128)S(1)}, f32[8,512]{1,0:T(8,128)S(1)}, u32[]{:S(2)}, u32[]{:S(2)}) collective-permute-start(f32[8,512]{1,0:T(8,128)S(1)} %collective-permute-done.5.refs_9_), channel_id=1, source_target_pairs={{0,64},{64,0},{1,65},{65,1},{2,66},{66,2},{3,67},{67,3},{4,68},{68... | collective-permute-start | bytes 49160 | tf_op jit(solution)/shard_map/ppermute | solution.py:851
  33.4 14.0 %collective-permute-start.2 = (f32[7,4,16,256]{3,2,1,0:T(8,128)S(1)}, f32[7,4,16,256]{3,2,1,0:T(8,128)S(1)}, u32[]{:S(2)}, u32[]{:S(2)}) collective-permute-start(f32[7,4,16,256]{3,2,1,0:T(8,128)S(1)} %collective-permute-done.1.refs_5_), channel_id=1, source_target_pairs={{0,64},{64,0},{1,65},{65,1},{2,66},{66,2},{3,67},{67,3},{4,68},{68... | collective-permute-start | bytes 1376264 | tf_op jit(solution)/shard_map/ppermute | solution.py:851
  33.5 13.9 %collective-permute-start.4 = (f32[7,4,16,256]{3,2,1,0:T(8,128)S(1)}, f32[7,4,16,256]{3,2,1,0:T(8,128)S(1)}, u32[]{:S(2)}, u32[]{:S(2)}) collective-permute-start(f32[7,4,16,256]{3,2,1,0:T(8,128)S(1)} %collective-permute-done.3.refs_7_), channel_id=1, source_target_pairs={{0,64},{64,0},{1,65},{65,1},{2,66},{66,2},{3,67},{67,3},{4,68},{68... | collective-permute-start | bytes 1376264 | tf_op jit(solution)/shard_map/ppermute | solution.py:851
  33.9 12.7 %copy-start.19 = (f32[2,64,64]{2,1,0:T(8,128)S(1)}, f32[2,64,64]{2,1,0:T(8,128)}, u32[]{:S(2)}) copy-start(f32[2,64,64]{2,1,0:T(8,128)} %param.25) | copy-start | bytes 98308
  33.9 12.7 %copy-start.25 = (f32[64,6]{0,1:T(8,128)S(1)}, f32[64,6]{0,1:T(8,128)}, u32[]{:S(2)}) copy-start(f32[64,6]{0,1:T(8,128)} %param.24) | copy-start | bytes 4612
  33.9 12.8 %copy-start.23 = (f32[6,64]{1,0:T(8,128)S(1)}, f32[6,64]{1,0:T(8,128)}, u32[]{:S(2)}) copy-start(f32[6,64]{1,0:T(8,128)} %param.27) | copy-start | bytes 4612
  33.9 13.5 %copy-start = (f32[7,4,16,256]{3,2,1,0:T(8,128)S(1)}, f32[7,4,16,256]{3,2,1,0:T(8,128)}, u32[]{:S(2)}) copy-start(f32[7,4,16,256]{3,2,1,0:T(8,128)} %get-tuple-element.33.refs_3_) | copy-start | bytes 1376260
  33.9 13.5 %copy-start.1 = (f32[256,128]{1,0:T(8,128)S(1)}, f32[256,128]{1,0:T(8,128)}, u32[]{:S(2)}) copy-start(f32[256,128]{1,0:T(8,128)} %constant.12.clone.refs_15_) | copy-start | bytes 393220
  33.9 13.5 %copy-start.2 = (s32[4]{0:T(128)S(1)}, s32[4]{0:T(128)}, u32[]{:S(2)}) copy-start(s32[4]{0:T(128)} %refs_0_.5) | copy-start | bytes 52
  33.9 13.5 %copy-start.3 = (f32[4]{0:T(128)S(1)}, f32[4]{0:T(128)}, u32[]{:S(2)}) copy-start(f32[4]{0:T(128)} %refs_1_.1) | copy-start | bytes 52
  33.9 13.5 %copy-start.4 = (f32[4]{0:T(128)S(1)}, f32[4]{0:T(128)}, u32[]{:S(2)}) copy-start(f32[4]{0:T(128)} %refs_2_.2) | copy-start | bytes 52
  46.1 1.2 collective-permute-start.8
  46.2 1.3 collective-permute-start.10
  53.6 6.2 %collective-permute-start.11 = (f32[256,128]{1,0:T(8,128)S(1)}, f32[256,128]{1,0:T(8,128)S(1)}, u32[]{:S(2)}, u32[]{:S(2)}) collective-permute-start(f32[256,128]{1,0:T(8,128)S(1)} %get-tuple-element.62), channel_id=1, source_target_pairs={{0,32},{32,0},{64,96},{96,64},{1,33},{33,1},{65,97},{97,65},{2,34}... | collective-permute-start | bytes 393224 | tf_op jit(solution)/shard_map/ppermute | solution.py:864
  53.6 6.2 %collective-permute-start.12 = (f32[256,128]{1,0:T(8,128)S(1)}, f32[256,128]{1,0:T(8,128)S(1)}, u32[]{:S(2)}, u32[]{:S(2)}) collective-permute-start(f32[256,128]{1,0:T(8,128)S(1)} %get-tuple-element.61), channel_id=1, source_target_pairs={{0,64},{32,96},{64,0},{96,32},{1,65},{33,97},{65,1},{97,33},{2,66}... | collective-permute-start | bytes 393224 | tf_op jit(solution)/shard_map/ppermute | solution.py:864
  53.9 9.2 %collective-permute-start.13 = (f32[256,128]{1,0:T(8,128)S(1)}, f32[256,128]{1,0:T(8,128)S(1)}, u32[]{:S(2)}, u32[]{:S(2)}) collective-permute-start(f32[256,128]{1,0:T(8,128)S(1)} %get-tuple-element.60), channel_id=1, source_target_pairs={{0,96},{32,64},{64,32},{96,0},{1,97},{33,65},{65,33},{97,1},{2,98}... | collective-permute-start | bytes 393224 | tf_op jit(solution)/shard_map/ppermute | solution.py:864
  59.8 3.3 %copy-start.5 = (f32[256,128]{1,0:T(8,128)}, f32[256,128]{1,0:T(8,128)S(1)}, u32[]{:S(2)}) copy-start(f32[256,128]{1,0:T(8,128)S(1)} %collective-permute-done.11.piece1) | copy-start | bytes 393220
  59.8 3.3 %copy-start.6 = (f32[256,128]{1,0:T(8,128)}, f32[256,128]{1,0:T(8,128)S(1)}, u32[]{:S(2)}) copy-start(f32[256,128]{1,0:T(8,128)S(1)} %collective-permute-done.12.piece2) | copy-start | bytes 393220
  63.1 0.6 copy-start.7
  66.3 16.2 %all-to-all-start = ((f32[32,8,128]{2,1,0:T(8,128)}), f32[32,8,128]{2,1,0:T(8,128)S(1)}, u32[]{:S(2)}, u32[]{:S(2)}) async-start(f32[32,8,128]{2,1,0:T(8,128)} %bitcast.50), calls=%async_computation | async-start | bytes 262144 | tf_op jit(solution)/shard_map/all_to_all | solution.py:913
  75.2 12.3 %copy-start.24 = (f32[8,64]{1,0:T(8,128)}, f32[8,64]{1,0:T(8,128)S(1)}, u32[]{:S(2)}) copy-start(f32[8,64]{1,0:T(8,128)S(1)} %pad.25.lift) | copy-start | bytes 6148
  82.5 0.7 copy-start.9
  87.5 13.6 %all-to-all-start.1 = ((f32[32,8,128]{2,1,0:T(8,128)}), f32[32,8,128]{2,1,0:T(8,128)S(1)}, u32[]{:S(2)}, u32[]{:S(2)}) async-start(f32[32,8,128]{2,1,0:T(8,128)} %bitcast.54), calls=%async_computation.1 | async-start | bytes 262144 | tf_op jit(solution)/shard_map/all_to_all | solution.py:913
  101.1 0.6 copy-start.12
  107.8 12.3 %all-to-all-start.2 = ((f32[32,8,128]{2,1,0:T(8,128)}), f32[32,8,128]{2,1,0:T(8,128)S(1)}, u32[]{:S(2)}, u32[]{:S(2)}) async-start(f32[32,8,128]{2,1,0:T(8,128)} %bitcast.57), calls=%async_computation.2 | async-start | bytes 262144 | tf_op jit(solution)/shard_map/all_to_all | solution.py:913
  120.1 0.7 copy-start.11
  124.9 11.3 %all-to-all-start.3 = ((f32[32,8,128]{2,1,0:T(8,128)}), f32[32,8,128]{2,1,0:T(8,128)S(1)}, u32[]{:S(2)}, u32[]{:S(2)}) async-start(f32[32,8,128]{2,1,0:T(8,128)} %bitcast.56), calls=%async_computation.3 | async-start | bytes 262144 | tf_op jit(solution)/shard_map/all_to_all | solution.py:913
  136.2 0.7 copy-start.13
  144.5 11.3 %all-to-all-start.4 = ((f32[32,8,128]{2,1,0:T(8,128)}), f32[32,8,128]{2,1,0:T(8,128)S(1)}, u32[]{:S(2)}, u32[]{:S(2)}) async-start(f32[32,8,128]{2,1,0:T(8,128)} %bitcast.55), calls=%async_computation.4 | async-start | bytes 262144 | tf_op jit(solution)/shard_map/all_to_all | solution.py:913
  155.8 0.6 copy-start.10
  160.6 20.1 %all-to-all-start.5 = ((f32[32,8,128]{2,1,0:T(8,128)}), f32[32,8,128]{2,1,0:T(8,128)S(1)}, u32[]{:S(2)}, u32[]{:S(2)}) async-start(f32[32,8,128]{2,1,0:T(8,128)} %bitcast.53), calls=%async_computation.5 | async-start | bytes 262144 | tf_op jit(solution)/shard_map/all_to_all | solution.py:913
  167.7 7.5 %collective-permute-start.14 = (f32[128,128]{1,0:T(8,128)}, f32[128,128]{1,0:T(8,128)S(1)}, u32[]{:S(2)}, u32[]{:S(2)}) collective-permute-start(f32[128,128]{1,0:T(8,128)} %get-tuple-element.50.refs_4_), channel_id=1, source_target_pairs={{0,32},{32,0},{64,96},{96,64},{1,33},{33,1},{65,97},{97,65},{2,34}... | collective-permute-start | bytes 196616 | tf_op jit(solution)/shard_map/ppermute | solution.py:864
  170.6 5.6 %collective-permute-start.15 = (f32[128,128]{1,0:T(8,128)}, f32[128,128]{1,0:T(8,128)S(1)}, u32[]{:S(2)}, u32[]{:S(2)}) collective-permute-start(f32[128,128]{1,0:T(8,128)} %get-tuple-element.50.refs_4_), channel_id=1, source_target_pairs={{0,64},{32,96},{64,0},{96,32},{1,65},{33,97},{65,1},{97,33},{2,66}... | collective-permute-start | bytes 196616 | tf_op jit(solution)/shard_map/ppermute | solution.py:864
  175.1 5.6 %collective-permute-start.16 = (f32[128,128]{1,0:T(8,128)}, f32[128,128]{1,0:T(8,128)S(1)}, u32[]{:S(2)}, u32[]{:S(2)}) collective-permute-start(f32[128,128]{1,0:T(8,128)} %get-tuple-element.50.refs_4_), channel_id=1, source_target_pairs={{0,96},{32,64},{64,32},{96,0},{1,97},{33,65},{65,33},{97,1},{2,98}... | collective-permute-start | bytes 196616 | tf_op jit(solution)/shard_map/ppermute | solution.py:864
  175.2 5.5 %copy-start.16 = (f32[128,128]{1,0:T(8,128)}, f32[128,128]{1,0:T(8,128)S(1)}, u32[]{:S(2)}) copy-start(f32[128,128]{1,0:T(8,128)S(1)} %collective-permute-done.14.refs_9_.refs_5_) | copy-start | bytes 196612
  176.2 4.5 %copy-start.17 = (f32[128,128]{1,0:T(8,128)}, f32[128,128]{1,0:T(8,128)S(1)}, u32[]{:S(2)}) copy-start(f32[128,128]{1,0:T(8,128)S(1)} %collective-permute-done.15.refs_10_.refs_6_) | copy-start | bytes 196612
  180.7 0.6 copy-start.18
  180.7 0.7 copy-start.15
  187.7 16.0 %all-to-all-start.6 = ((f32[32,16,128]{2,1,0:T(8,128)}), f32[32,16,128]{2,1,0:T(8,128)S(1)}, u32[]{:S(2)}, u32[]{:S(2)}) async-start(f32[32,16,128]{2,1,0:T(8,128)} %get-tuple-element.51), calls=%async_computation.6 | async-start | bytes 524288 | tf_op jit(solution)/shard_map/all_to_all | solution.py:913
  203.7 0.7 copy-start.8
  208.5 5.9 %collective-permute-start.19 = (f32[136,128]{1,0:T(8,128)}, f32[136,128]{1,0:T(8,128)S(1)}, u32[]{:S(2)}, u32[]{:S(2)}) collective-permute-start(f32[136,128]{1,0:T(8,128)} %modes_last.1.refs_0_), channel_id=1, source_target_pairs={{0,96},{32,64},{64,32},{96,0},{1,97},{33,65},{65,33},{97,1},{2,98}... | collective-permute-start | bytes 208904 | tf_op jit(solution)/shard_map/ppermute | solution.py:864
  211.3 3.0 %collective-permute-start.18 = (f32[136,128]{1,0:T(8,128)}, f32[136,128]{1,0:T(8,128)S(1)}, u32[]{:S(2)}, u32[]{:S(2)}) collective-permute-start(f32[136,128]{1,0:T(8,128)} %modes_last.1.refs_0_), channel_id=1, source_target_pairs={{0,64},{32,96},{64,0},{96,32},{1,65},{33,97},{65,1},{97,33},{2,66}... | collective-permute-start | bytes 208904 | tf_op jit(solution)/shard_map/ppermute | solution.py:864
  211.3 4.9 %collective-permute-start.17 = (f32[136,128]{1,0:T(8,128)}, f32[136,128]{1,0:T(8,128)S(1)}, u32[]{:S(2)}, u32[]{:S(2)}) collective-permute-start(f32[136,128]{1,0:T(8,128)} %modes_last.1.refs_0_), channel_id=1, source_target_pairs={{0,32},{32,0},{64,96},{96,64},{1,33},{33,1},{65,97},{97,65},{2,34}... | collective-permute-start | bytes 208904 | tf_op jit(solution)/shard_map/ppermute | solution.py:864
  214.3 7.0 %copy-start.20 = (f32[136,128]{1,0:T(8,128)}, f32[136,128]{1,0:T(8,128)S(1)}, u32[]{:S(2)}) copy-start(f32[136,128]{1,0:T(8,128)S(1)} %collective-permute-done.19.refs_3_) | copy-start | bytes 208900
  214.3 7.0 %copy-start.21 = (f32[136,128]{1,0:T(8,128)}, f32[136,128]{1,0:T(8,128)S(1)}, u32[]{:S(2)}) copy-start(f32[136,128]{1,0:T(8,128)S(1)} %collective-permute-done.18.refs_2_) | copy-start | bytes 208900
  216.2 5.2 %copy-start.22 = (f32[136,128]{1,0:T(8,128)}, f32[136,128]{1,0:T(8,128)S(1)}, u32[]{:S(2)}) copy-start(f32[136,128]{1,0:T(8,128)S(1)} %collective-permute-done.17.refs_1_) | copy-start | bytes 208900
  217.5 11.2 %all-to-all-start.7 = ((f32[32,8,128]{2,1,0:T(8,128)}), f32[32,8,128]{2,1,0:T(8,128)S(1)}, u32[]{:S(2)}, u32[]{:S(2)}) async-start(f32[32,8,128]{2,1,0:T(8,128)} %broadcast_in_dim.3), calls=%async_computation.7 | async-start | bytes 262144 | tf_op jit(solution)/shard_map/all_to_all | solution.py:913
  228.7 0.6 copy-start.14

commit v3 on v2

--- a/solution.py
+++ b/solution.py
@@ -23,7 +23,7 @@
 ROOM = 62 * 1024 * 1024
 LEAP_ROOM = 24 * 1024 * 1024
 CELL_ROOM = 62 * 1024 * 1024
-MODE_ROOM = 62 * 1024 * 1024
+MODE_ROOM = 48 * 1024 * 1024
 GROUP = ("role", "rep")
 EVERY = ("role", "rep", "tile")
 SX, SY, SZ = 64, 16, 256
@@ -134,28 +134,65 @@
     return jax.ShapeDtypeStruct(shape, F32)
 
 
-def pack_kernel(fields, material, packed, ends, left, right):
-    packed[0:6] = fields[...]
-    packed[6] = material[...].astype(F32)
+ONLY_AFTER = [(0, 3), (3, 3), (4, 3), (5, 3), (6, 3)]
+ONLY_BEFORE = [(6, 0), (3, 0)]
+PLANES = [(c, i) for c in range(7) for i in range(4)]
+PLANES = (
+    ONLY_AFTER + [p for p in PLANES if p not in ONLY_AFTER and p not in ONLY_BEFORE] + ONLY_BEFORE
+)
+FIRST, LAST = len(ONLY_AFTER), len(PLANES) - len(ONLY_BEFORE)
+
+
+def ends_kernel(fields, material, ends, left, right):
     left[...] = jnp.zeros_like(left)
     right[...] = jnp.zeros_like(right)
-    left[0:448] = packed[:, :, :, 0:128].reshape(448, 128)
-    right[0:448] = packed[:, :, :, 128:256].reshape(448, 128)
+    for c in range(7):
+        rows = slice(c * 64, (c + 1) * 64)
+        own = (fields[c] if c < 6 else material[...].astype(F32)).reshape(64, 256)
+        left[rows, :] = own[:, 0:128]
+        right[rows, :] = own[:, 128:256]
     for b in range(4):
         rows = slice(b * 128, (b + 1) * 128)
         first = jnp.transpose(left[rows, :])[0:8]
         last = jnp.transpose(right[rows, :])[120:128]
-        ends[:, rows] = jnp.where(rows_of((8, 128)) < 4, first, last)
-
-
-def pack(fields, material):
+        at, lanes = b // 2 * 8, slice(b % 2 * 128, b % 2 * 128 + 128)
+        ends[at : at + 8, lanes] = jnp.where(rows_of((8, 128)) < 4, first, last)
+
+
+def ends_along_z(fields, material):
+    return pl.pallas_call(
+        ends_kernel,
+        out_shape=shape_of(16, 256),
+        scratch_shapes=[vmem((512, 128)), vmem((512, 128))],
+        compiler_params=params(),
+        name="ends",
+    )(fields, material)
+
+
+def pack_kernel(fields, material, ends, packed, after, before):
+    for n, (c, i) in enumerate(PLANES):
+        plane = fields[c, i] if c < 6 else material[i].astype(F32)
+        packed[n] = plane
+        if n < LAST:
+            after[n] = plane
+        if n >= FIRST:
+            before[n - FIRST] = plane
+    for out in (packed, after, before):
+        out[out.shape[0] - 1] = ends[...]
+
+
+def pack(fields, material, ends):
+    count = len(PLANES)
     return pl.pallas_call(
         pack_kernel,
-        out_shape=[shape_of(7, 4, 16, 256), shape_of(8, 512)],
-        scratch_shapes=[vmem((512, 128)), vmem((512, 128))],
+        out_shape=[
+            shape_of(count + 1, 16, 256),
+            shape_of(LAST + 1, 16, 256),
+            shape_of(count - FIRST + 1, 16, 256),
+        ],
         compiler_params=params(),
         name="pack",
-    )(fields, material)
+    )(fields, material, ends)
 
 
 def here():
@@ -172,15 +209,12 @@
     low1,
     high0,
     high1,
-    ends_own0,
-    ends_own1,
-    ends_low0,
-    ends_low1,
-    ends_high0,
-    ends_high1,
     pool,
     out_fields,
-    out_pieces,
+    out_piece0,
+    out_piece1,
+    out_piece2,
+    out_piece3,
     grid_f,
     keep,
     gain,
@@ -198,8 +232,9 @@
     top = jnp.where((row8 < 4) & (role == 0), 1.0, 0.0)
     bottom = jnp.where((row8 >= 4) & (role == 1), 1.0, 0.0)
 
-    def column(ends, edge):
-        strip = ends[...]
+    def column(planes, edge):
+        ends = planes[planes.shape[0] - 1]
+        strip = jnp.concatenate([ends[0:8], ends[8:16]], axis=1)
         row = rows_of((8, 512))
         first = jnp.where((row < 4) & (rep == 0), strip, 0.0)
         last = jnp.where((row >= 4) & (rep == 1), strip, 0.0)
@@ -207,26 +242,21 @@
         for b in range(4):
             edge[b * 128 : (b + 1) * 128, :] = jnp.transpose(whole[:, b * 128 : (b + 1) * 128])
 
-    sources = (
-        (low0, low1, ends_low0, ends_low1),
-        (own0, own1, ends_own0, ends_own1),
-        (high0, high1, ends_high0, ends_high1),
-    )
-    for number, (mine, mate, ends_mine, ends_mate) in enumerate(sources):
-        column(ends_mine, edge0)
-        column(ends_mate, edge1)
-
-        def fill(n, carry, mine=mine, mate=mate, number=number):
-            c = n // 4
-            i = n % 4
-            at = pl.multiple_of(n * 16, 16)
-            plane = jnp.concatenate([mine[c, i], edge0[pl.ds(at, 16), :]], axis=1)
-            other = jnp.concatenate([mate[c, i], edge1[pl.ds(at, 16), :]], axis=1)
-            halo = other[0:8] * top + other[8:16] * bottom
-            grid_f[c, 4 * number + i] = jnp.concatenate([plane, halo], axis=0)
-            return carry
-
-        lax.fori_loop(0, 28, fill, 0, unroll=4)
+    for number, (mine, mate) in enumerate(((low0, low1), (own0, own1), (high0, high1))):
+        column(mine, edge0)
+        column(mate, edge1)
+
+        for c in range(7):
+            for i in range(4):
+                n = PLANES.index((c, i)) - (FIRST if number == 2 else 0)
+                if not 0 <= n < mine.shape[0] - 1:
+                    grid_f[c, 4 * number + i] = jnp.zeros((24, 384), F32)
+                    continue
+                rows = slice((c * 4 + i) * 16, (c * 4 + i + 1) * 16)
+                plane = jnp.concatenate([mine[n], edge0[rows, :]], axis=1)
+                other = jnp.concatenate([mate[n], edge1[rows, :]], axis=1)
+                halo = other[0:8] * top + other[8:16] * bottom
+                grid_f[c, 4 * number + i] = jnp.concatenate([plane, halo], axis=0)
 
     row = rows_of((24, 384))
     lane = lanes_of((24, 384))
@@ -311,9 +341,9 @@
         out_fields[c] = grid_f[c, 4:8, 0:16, 0:256]
 
     me = role * 2 + rep
-    for d in range(4):
-        out_pieces[d, 0:128] = reduced[plan[me ^ d] - 1]
-        out_pieces[d, 128:256] = reduced[STEPS - 1]
+    for d, out in enumerate((out_piece0, out_piece1, out_piece2, out_piece3)):
+        out[0:128] = reduced[plan[me ^ d] - 1]
+        out[128:256] = reduced[STEPS - 1]
 
 
 def leapfrog(plan, permittivity, conductivity, blocks):
@@ -324,8 +354,8 @@
         + [(v, whole) for v in (*blocks, jnp.asarray(POOL_Z))],
         [
             (shape_of(6, 4, 16, 256), whole),
-            (shape_of(4, 256, 128), whole),
-        ],
+        ]
+        + [(shape_of(256, 128), whole)] * 4,
         room=LEAP_ROOM,
         scratch_shapes=[
             vmem((7, 12, 24, 384)),
@@ -419,7 +449,7 @@
     return hidden, slope
 
 
-BLOCK_Y = 4
+BLOCK_Y = 8
 BLOCK = BLOCK_Y * SZ
 CHUNK = 128
 
@@ -571,14 +601,42 @@
         [(shape_of(*coef), full(coef))]
         + [(jax.ShapeDtypeStruct((CELLS, lanes), kind), block(lanes)) for lanes, kind in outs],
         grid=(SY // BLOCK_Y,),
-        scratch_shapes=[vmem((4, 48, 512), BF16), vmem((256, 128))] + list(scratch),
+        scratch_shapes=[vmem((SY // BLOCK_Y, 48, BLOCK_Y * 128), BF16), vmem((256, 128))] + list(scratch),
         name=name,
         room=CELL_ROOM,
         **order,
     )
 
 
-def grads_kernel(scale, norm, grad, h1, h2, target, w_proj, out, point_acc, proj_acc, loss_acc, wide, row):
+SIDES = pl.BlockSpec((BLOCK, 256), lambda g: (g, 0))
+
+
+def point_grad_kernel(grad, h1, out, acc):
+    step = pl.program_id(0)
+    acc[step] = dot(grad[...], h1[...], TN)
+
+    @pl.when(step == pl.num_programs(0) - 1)
+    def _():
+        point = sum(acc[n, 0:128, :] + acc[n, 128:256, :] for n in range(SY // BLOCK_Y))
+        point = fold(point)
+        picked = jnp.where(lanes_of((64, 128)) < 64, point[0:64], point[64:128])
+        picked = picked + pltpu.roll(picked, 64, 1)
+        out[...] = jnp.where(lanes_of((32, 128)) < 64, picked[0:32], picked[32:64])
+
+
+def point_gradient(grad, h1):
+    (out,) = call(
+        point_grad_kernel,
+        [(grad, SIDES), (h1, SIDES)],
+        [(shape_of(32, 128), full((32, 128)))],
+        grid=(SY // BLOCK_Y,),
+        scratch_shapes=[vmem((SY // BLOCK_Y, 256, 256))],
+        name="point_grad",
+    )
+    return out
+
+
+def proj_grad_kernel(scale, norm, h2, target, w_proj, point, out, acc, loss_acc, wide, row):
     step = pl.program_id(0)
 
     @pl.when(step == 0)
@@ -586,21 +644,16 @@
         wide[...] = square_weight(w_proj[...])
         loss_acc[...] = jnp.zeros_like(loss_acc)
 
-    point_acc[step] = dot(grad[...], h1[...], TN)
     err = fold(dot(h2[...], wide[...])) - target[...]
     loss_acc[...] += jnp.sum((err * err).reshape(BLOCK // 8, 8, 128), axis=0)
     sides = jnp.concatenate(halves(err * scale), axis=1)
-    proj_acc[step] = dot(sides, h2[...], TN)
+    acc[step] = dot(sides, h2[...], TN)
 
     @pl.when(step == pl.num_programs(0) - 1)
     def _():
         out[...] = jnp.zeros_like(out)
-        point = sum(point_acc[n, 0:128, :] + point_acc[n, 128:256, :] for n in range(SY // BLOCK_Y))
-        point = fold(point)
-        picked = jnp.where(lanes_of((64, 128)) < 64, point[0:64], point[64:128])
-        picked = picked + pltpu.roll(picked, 64, 1)
-        out[:, 0, :] = jnp.where(lanes_of((32, 128)) < 64, picked[0:32], picked[32:64])
-        proj = sum(proj_acc[n, 0:16, :] + proj_acc[n, 128:144, :] for n in range(SY // BLOCK_Y))
+        out[:, 0, :] = point[...]
+        proj = sum(acc[n, 0:16, :] + acc[n, 128:144, :] for n in range(SY // BLOCK_Y))
         proj = fold(proj)
         picked = jnp.where(lanes_of((8, 128)) < 64, proj[0:8], proj[8:16])
         turned = jnp.transpose(picked + pltpu.roll(picked, 64, 1))
@@ -610,24 +663,27 @@
         out[:, 1, :] = row[...]
 
 
-def grads(norm, grad, h1, h2, target, w_proj):
-    sides = pl.BlockSpec((BLOCK, 256), lambda g: (g, 0))
-    return pl.pallas_call(
-        functools.partial(grads_kernel, 2.0 / norm, norm),
+def proj_gradient(norm, h2, target, w_proj, point, after):
+    (out,) = call(
+        functools.partial(proj_grad_kernel, 2.0 / norm, norm),
+        [
+            (h2, SIDES),
+            (target, pl.BlockSpec((BLOCK, 128), lambda g: (g, 0))),
+            (w_proj, full((128, 128))),
+            (point, full((32, 128))),
+        ],
+        [(shape_of(TILES, 8, 128), full((TILES, 8, 128)))],
+        after=(after,),
         grid=(SY // BLOCK_Y,),
-        out_shape=shape_of(TILES, 8, 128),
-        in_specs=[sides, sides, sides, pl.BlockSpec((BLOCK, 128), lambda g: (g, 0)), full((128, 128))],
-        out_specs=full((TILES, 8, 128)),
         scratch_shapes=[
-            vmem((SY // BLOCK_Y, 256, 256)),
             vmem((SY // BLOCK_Y, 256, 256)),
             vmem((8, 128)),
             vmem((256, 256), BF16),
             vmem((32, 128)),
         ],
-        compiler_params=params(),
-        name="grads",
-    )(grad, h1, h2, target, w_proj)
+        name="proj_grad",
+    )
+    return out
 
 
 def kept_modes(counts, layer):
@@ -650,21 +706,20 @@
 MIX_PAIRS = 8 // MIX_STEPS
 
 
-def mix(g_scr, b_scr, weights, step, turned):
+def mix(g_scr, b_scr, weights, step):
     row, lane = rows_of((16, 256)), lanes_of((16, 256))
-    wanted = (lanes_of((16, 128)) >= 64) if turned else (lanes_of((16, 128)) < 64)
+    low = lanes_of((16, 128)) < 64
     for n in range(MIX_PAIRS):
         at = pl.multiple_of((step * MIX_PAIRS + n) * 16, 16)
         one = g_scr[pl.ds(at, 16), :]
         wide = jnp.concatenate([one, one], axis=1)
-        total = jnp.zeros((32, 256), F32)
+        total = jnp.zeros((32, 128), F32)
         for q in range(4):
             own = jnp.where(row == 4 * q + lane // 64, wide, 0.0)
             sides = jnp.concatenate(halves(own), axis=0)
             both = halves(weights[n, q * 256 : (q + 1) * 256, :])
             total = total + dot(sides, jnp.concatenate(both, axis=1))
-        folded = fold(total[0:16]) + total[16:32, 0:128]
-        folded = jnp.where(wanted, folded, 0.0)
+        folded = total[0:16] + jnp.where(low, total[16:32], 0.0)
         b_scr[pl.ds(at, 16), :] = folded + pltpu.roll(folded, 64, 1)
 
 
@@ -688,7 +743,7 @@
         a_scr[...] = lifted
         out_a[...] = lifted
 
-    mix(a_scr, b_scr, weights, step, True)
+    mix(a_scr, b_scr, weights, step)
 
     @pl.when(step == pl.num_programs(0) - 1)
     def _():
@@ -705,7 +760,7 @@
         a_scr[...] = a
         out_a[...] = a
 
-    mix(a_scr, b_scr, weights, step, True)
+    mix(a_scr, b_scr, weights, step)
 
     @pl.when(step == pl.num_programs(0) - 1)
     def _():
@@ -729,23 +784,26 @@
         rows = dot3((kron[0], kron[1]), halves(coef[...]))
         take_gradient(rows, kept_modes(counts, 1), saved, g_scr, out_pair)
 
-    mix(g_scr, b_scr, weights, step, False)
+    mix(g_scr, b_scr, weights, step)
 
     @pl.when(step == pl.num_programs(0) - 1)
     def _():
         close_modes(b_scr, kept_modes(counts, 1), kron_t, out)
 
 
-def modes_last_kernel(counts, coef, saved, inputs, point, weights, kron, kron_t, out, g_scr, b_scr):
+def modes_last_kernel(
+    counts, coef, saved, inputs, point, pair1, weights, kron, kron_t, out, g_scr, b_scr
+):
     step = pl.program_id(0)
 
     @pl.when(step == 0)
     def _():
         value = coef[:, 0:8, :].reshape(256, 128)
         rows = dot3((kron[0], kron[1]), halves(value))
-        take_gradient(rows, kept_modes(counts, 0), saved, g_scr, out.at[0:128])
-
-    mix(g_scr, b_scr, weights, step, False)
+        take_gradient(rows, kept_modes(counts, 0), saved, g_scr, out.at[8:136])
+        out[136:264] = pair1[...]
+
+    mix(g_scr, b_scr, weights, step)
 
     @pl.when(step == pl.num_programs(0) - 1)
     def _():
@@ -756,7 +814,7 @@
         direct = direct[0:8] + pltpu.roll(direct[8:16], 64, 1)
         late = jnp.where(lanes_of((8, 128)) < 64, lift, pltpu.roll(direct, 64, 1))
         extra = pltpu.roll(jnp.sum(coef[:, 8:16, :], axis=0), 6, 0)
-        out[128:136] = jnp.where(rows_of((8, 128)) < 6, late, extra)
+        out[0:8] = jnp.where(rows_of((8, 128)) < 6, late, extra)
 
 
 def mode_call(kernel, name, layer, counts, smalls, weights, outs, **order):
@@ -765,7 +823,7 @@
         kernel,
         [(counts, SMEM)]
         + [(v, full(v.shape)) for v in smalls]
-        + [(weights, pl.BlockSpec((None, MIX_PAIRS, 1024, 128), lambda m: (layer, m, 0, 0)))]
+        + [(weights, pl.BlockSpec((None, MIX_PAIRS, 1024, 64), lambda m: (layer, m, 0, 0)))]
         + [(v, full(v.shape)) for v in consts],
         [(shape_of(*o), full(o)) for o in outs],
         grid=(MIX_STEPS,),
@@ -779,18 +837,14 @@
 OUTER_PAIRS = 4
 
 
-def outer_kernel(*refs):
-    layer = pl.program_id(0)
-    out = refs[8]
+def outer_kernel(tail0, tail1, tail2, tail3, out):
+    layer, part = pl.program_id(0), pl.program_id(1)
     row, lane = rows_of((64, 1024)), lanes_of((64, 1024))
     own = row % 16 == lane // 64
     low = lanes_of((64, 128)) < 64
     for n in range(OUTER_PAIRS):
-        rows = slice(n * 16, (n + 1) * 16)
-        block = jnp.concatenate(
-            [jnp.where(layer == 0, refs[d][rows, :], refs[4 + d][rows, :]) for d in range(4)],
-            axis=0,
-        )
+        at = pl.multiple_of(8 + layer * 128 + (part * OUTER_PAIRS + n) * 16, 8)
+        block = jnp.concatenate([t[pl.ds(at, 16), :] for t in (tail0, tail1, tail2, tail3)], axis=0)
         grads = halves(jnp.transpose(block)[0:64])
         twice = jnp.where(low, pltpu.roll(block, 64, 1), block)
         spread = halves(jnp.where(own, jnp.concatenate([twice] * 8, axis=1), 0.0))
@@ -799,23 +853,38 @@
             out[n, r] = result[:, r * 64 : (r + 1) * 64]
 
 
-def outer_products(pairs0, pairs1):
-    block = pl.BlockSpec((OUTER_PAIRS * 16, 128), lambda l, m: (m, 0))
+def outer_products(tails):
     return pl.pallas_call(
         outer_kernel,
         grid=(LAYERS, 8 // OUTER_PAIRS),
         out_shape=shape_of(LAYERS, 8, 16, 64, 64),
-        in_specs=[block] * 8,
+        in_specs=[full((264, 128))] * 4,
         out_specs=pl.BlockSpec((None, OUTER_PAIRS, 16, 64, 64), lambda l, m: (l, m, 0, 0, 0)),
         compiler_params=params(),
         name="outer",
-    )(*pairs0, *pairs1)
+    )(*tails)
+
+
+def spread_kernel(tail0, tail1, tail2, tail3, out):
+    late = (tail0[...] + tail1[...]) + (tail2[...] + tail3[...])
+    out[...] = jnp.broadcast_to(late[None], (TILES, 8, 128))
+
+
+def spread(tails):
+    return pl.pallas_call(
+        spread_kernel,
+        grid=(1,),
+        out_shape=shape_of(TILES, 8, 128),
+        in_specs=[pl.BlockSpec((8, 128), lambda n: (0, 0))] * 4,
+        out_specs=full((TILES, 8, 128)),
+        compiler_params=params(),
+        name="spread",
+    )(*tails)
 
 
 def finish_kernel(late, point, lift, out_lift, out_point, out_proj, out_loss):
     by_tile = late[...]
-    total = jnp.sum(by_tile, axis=0)
-    total = jnp.where(rows_of((8, 128)) < 6, total, 0.0)
+    total = jnp.where(rows_of((8, 128)) < 6, jnp.sum(by_tile, axis=0), 0.0)
     through, direct = total[:, 0:64], pltpu.roll(total, 64, 1)[:, 0:64]
 
     def exact(a, b, dims):
@@ -849,15 +918,6 @@
 
 def across(value, axis):
     return lax.ppermute(value, axis, [(0, 1), (1, 0)])
-
-
-def diagonal(value, by):
-    pairs = []
-    for q in range(2):
-        for t in range(TILES):
-            if 0 <= t + by < TILES:
-                pairs.append((q * TILES + t, (1 - q) * TILES + t + by))
-    return lax.ppermute(value, ("rep", "tile"), pairs)
 
 
 def xor_group(value, d):
@@ -883,16 +943,18 @@
     spectral_weight,
     project_weight,
 ):
-    weights = jnp.concatenate([spectral_weight, jnp.swapaxes(spectral_weight, -1, -2)], axis=-1)
-    weights = weights.reshape(LAYERS, 8, 1024, 128)
-
-    own0, ends_own0 = pack(fields.reshape(6, 4, 16, 256), material)
-    low0, high0 = passed(own0, "tile", 1), passed(own0, "tile", -1)
-    ends = (xor_group(ends_own0, 1), diagonal(ends_own0, 1), diagonal(ends_own0, -1))
+    plain = spectral_weight.reshape(LAYERS, 8, 1024, 64)
+    turned = jnp.swapaxes(spectral_weight, -1, -2).reshape(LAYERS, 8, 1024, 64)
+
+    fields6 = fields.reshape(6, 4, 16, 256)
+    ends = xor_group(ends_along_z(fields6, material), 1)
+    own0, after, before = pack(fields6, material, ends)
+    low0, high0 = passed(after, "tile", 1), passed(before, "tile", -1)
+    low0, high0 = call(lambda *refs: None, [], [], after=(turned,), carry=(low0, high0), name="hold")
     blocks = []
-    for value in (own0, low0, high0, *ends):
+    for value in (own0, low0, high0):
         blocks += [value, across(value, "role")]
-    new_fields, pieces = leapfrog(plan, permittivity, conductivity, blocks)
+    new_fields, *pieces = leapfrog(plan, permittivity, conductivity, blocks)
     pieces = [pieces[0]] + [xor_group(pieces[d], d) for d in range(1, 4)]
     coef = input_coefs(pieces)
 
@@ -922,7 +984,7 @@
         0,
         mode_counts,
         (swap_flat(coef), lift_pad),
-        weights,
+        turned,
         ((256, 128), (128, 128), (128, 128)),
         after=(pre0,),
     )
@@ -943,7 +1005,7 @@
         1,
         mode_counts,
         (swap_flat(coef),),
-        weights,
+        turned,
         ((256, 128), (128, 128)),
     )
     coef, grad1, h2 = cell_call(
@@ -955,18 +1017,18 @@
         (sides, sides),
         scratch=(vmem((2, 256, 256), BF16), vmem((BLOCK, 128))),
     )
-    extra = grads(norm_count, grad1, h1, h2, target, proj_t.T)
+    point = point_gradient(grad1, h1)
     spectrum, pair1 = mode_call(
         modes_backward_kernel,
         "modes_backward",
         1,
         mode_counts,
         (swap_flat(coef), a1),
-        weights,
+        plain,
         ((256, 128), (128, 128)),
-        after=(extra,),
-    )
-    pairs = [pair1] + [xor_group(pair1, d) for d in range(1, 4)]
+        after=(point,),
+    )
+    extra = proj_gradient(norm_count, h2, target, proj_t.T, point, pair1)
     coef, grad0 = cell_call(
         cells2_kernel,
         "cells2",
@@ -976,7 +1038,6 @@
         (sides,),
         scratch=(vmem((256, 256), BF16),),
         coef=(TILES, 16, 128),
-        after=pairs[1:],
     )
     direct = lax.dot_general(inputs, grad0, TN, preferred_element_type=F32)
     (tail,) = mode_call(
@@ -984,15 +1045,13 @@
         "modes_last",
         0,
         mode_counts,
-        (swap(coef), a0, a_in, direct),
-        weights,
-        ((136, 128),),
+        (swap(coef), a0, a_in, direct, pair1),
+        plain,
+        ((264, 128),),
     )
     tails = [tail] + [xor_group(tail, d) for d in range(1, 4)]
-    late = [t[128:136] for t in tails]
-    late = (late[0] + late[1]) + (late[2] + late[3])
-    late = swap(jnp.broadcast_to(late, (TILES, 8, 128)))
-    spectral_grad = outer_products(tails, pairs)
+    late = swap(spread(tails))
+    spectral_grad = outer_products(tails)
     lift_grad, point_grad, proj_grad, loss = finish(late, pointwise[0], lift8)
     return (
         new_fields.reshape(2, 3, 4, 16, 256),

time: 234 us -> 217 us (0.927)
  other arithmetic: 15.7 us -> 2.26 us
  starting transfers between devices: 79.8 us -> 67.5 us
  waiting for transfers between devices: 42.7 us -> 49.6 us
  local copies, waits for them, and re-layouts: 18.8 us -> 22.3 us
    concatenate x1 -> x0, other arithmetic: 12.1 us -> none  [local(): jnp.concatenate([spectral_weight, jnp.swapaxes(spectral_weight, -1, -2)],...]
    transpose x0 -> x1, local copies, waits for them, and re-layouts: none -> 8.66 us  [local(): turned = jnp.swapaxes(spectral_weight, -1, -2).reshape(LAYERS, 8, 1024, 64)]
    all_to_all x8, waiting for transfers between devices: 22.8 us -> 30.4 us  [swap(): return lax.all_to_all(value, 'tile', 0, 0, tiled=True)]
    all_to_all x8, starting transfers between devices: 46.4 us -> 39.9 us  [swap(): return lax.all_to_all(value, 'tile', 0, 0, tiled=True)]
    ppermute x10 -> x7, waiting for transfers between devices: 19.2 us -> 13.1 us  [xor_group(): return lax.ppermute(value, GROUP, [(i, i ^ d) for i in range(4)])]
    ppermute x2 -> x0, starting transfers between devices: 4.34 us -> none  [diagonal(): return lax.ppermute(value, ('rep', 'tile'), pairs)]
    ppermute x2, waiting for transfers between devices: 0.01 us -> 4.18 us  [passed(): lax.ppermute(value, axis, [(i, i + by) for i in range(length) if 0 <= i +...]
    pallas_call x8 -> x11, Pallas kernels: 42.1 us -> 46 us  [call(): pl.pallas_call(run, out_shape=[o[0] for o in outs] + [jax.ShapeDtypeStruc...]
  transfers between devices with their start and end apart: 28 -> 20, of which waited for: 16 -> 15; matrix products, arithmetic and copies ran while one was open for 13% -> 8% of each run, Pallas kernels for 9% -> 10%
where the time goes in v3:
time: 217 us; the launch traced here: 216 us
  Pallas kernels  70 us (32%)
  starting transfers between devices  67.5 us (31%)
  waiting for transfers between devices  49.6 us (23%)
  local copies, waits for them, and re-layouts  22.3 us (10%)
  matrix products  3.36 us (2%)
  other arithmetic  2.26 us (1%)
    pallas_call x11, Pallas kernels, call(): pl.pallas_call(run, out_shape=[o[0] for o in outs] + [jax.ShapeDtypeStruc...  46 us
    all_to_all x8, starting transfers between devices, swap(): return lax.all_to_all(value, 'tile', 0, 0, tiled=True)  39.9 us
    all_to_all x8, waiting for transfers between devices, swap(): return lax.all_to_all(value, 'tile', 0, 0, tiled=True)  30.4 us
    ppermute x7, starting transfers between devices, xor_group(): return lax.ppermute(value, GROUP, [(i, i ^ d) for i in range(4)])  18.3 us
    ppermute x7, waiting for transfers between devices, xor_group(): return lax.ppermute(value, GROUP, [(i, i ^ d) for i in range(4)])  13.1 us
    unnamed x66, local copies, waits for them, and re-layouts  10.9 us
    transpose x1, local copies, waits for them, and re-layouts, local(): turned = jnp.swapaxes(spectral_weight, -1, -2).reshape(LAYERS, 8, 1024, 64)  8.66 us
    pallas_call x2, Pallas kernels, prepare(): pl.pallas_call(functools.partial(prep_kernel, first_row), out_shape=[own,...  8.05 us
  transfers between devices with their start and end apart: 20, of which 15 were waited for; matrix products, arithmetic and copies ran while one was open for 8% of the time, Pallas kernels for 10%

profile of v3, /device:TPU:1, one launch (start us, length us, event | category | flops | bytes accessed | tf_op | source)
XLA Modules:
  0.0 216.0 jit_solution(11447900650042676387)
XLA Ops:
  0.6 1.8 ends.1
  2.4 4.4 %collective-permute-start = (f32[16,256]{1,0:T(8,128)}, f32[16,256]{1,0:T(8,128)S(1)}, u32[]{:S(2)}, u32[]{:S(2)}) collective-permute-start(f32[16,256]{1,0:T(8,128)} %ends.1), channel_id=1, source_target_pairs={{0,32},{32,0},{64,96},{96,64},{1,33},{33,1},{65,97},{97,65},{2,34}... | collective-permute-start | bytes 49160 | tf_op jit(solution)/shard_map/ppermute | solution.py:924
  6.9 1.3 collective-permute-done.ends
  8.8 2.2 %pack.1 = (f32[29,16,256]{2,1,0:T(8,128)}, f32[27,16,256]{2,1,0:T(8,128)}, f32[24,16,256]{2,1,0:T(8,128)}) custom-call(f32[6,4,16,256]{3,2,1,0:T(8,128)} %bitcast.43, s32[4,16,256]{2,1,0:T(8,128)} %material.3, f32[16,256]{1,0:T(8,128)} %copy-done.32), custom_call_target="tpu_custom_call" | custom-call | tf_op jit(solution)/shard_map/pack/pallas_call | solution.py:186
  11.0 2.9 %collective-permute-start.2 = (f32[27,16,256]{2,1,0:T(8,128)}, f32[27,16,256]{2,1,0:T(8,128)S(1)}, u32[]{:S(2)}, u32[]{:S(2)}) collective-permute-start(f32[27,16,256]{2,1,0:T(8,128)} %get-tuple-element.40), channel_id=1, source_target_pairs={{0,1},{1,2},{2,3},{3,4},{4,5},{5,6},{6,7},{7,8},{8,9},{9,10},{10,1... | collective-permute-start | bytes 1327112 | tf_op jit(solution)/shard_map/ppermute | solution.py:916
  13.9 1.3 collective-permute-start.3
  15.2 2.2 %collective-permute-start.1 = (f32[29,16,256]{2,1,0:T(8,128)}, f32[29,16,256]{2,1,0:T(8,128)}, u32[]{:S(2)}, u32[]{:S(2)}) collective-permute-start(f32[29,16,256]{2,1,0:T(8,128)} %get-tuple-element.39.refs_3_), channel_id=1, source_target_pairs={{0,64},{64,0},{1,65},{65,1},{2,66},{66,2},{3,67},{67,3},{4,68},{68... | collective-permute-start | bytes 1425416 | tf_op jit(solution)/shard_map/ppermute | solution.py:920
  17.4 8.7 %copy.30 = f32[2,8,16,64,64]{4,3,2,1,0:T(8,128)} copy(f32[2,8,16,64,64]{3,4,2,1,0:T(8,128)} %bitcast.39) | data formatting | bytes 8388608 | tf_op jit(solution)/shard_map/transpose | solution.py:947
  26.1 4.2 %collective-permute-done.2.refs_1_ = f32[27,16,256]{2,1,0:T(8,128)S(1)} collective-permute-done((f32[27,16,256]{2,1,0:T(8,128)}, f32[27,16,256]{2,1,0:T(8,128)S(1)}, u32[]{:S(2)}, u32[]{:S(2)}) %collective-permute-start.2) | collective-permute-done | bytes 442400 | tf_op jit(solution)/shard_map/ppermute | solution.py:916
  30.2 0.8 copy-done.3
  31.1 2.8 %collective-permute-start.4 = (f32[27,16,256]{2,1,0:T(8,128)}, f32[27,16,256]{2,1,0:T(8,128)S(1)}, u32[]{:S(2)}, u32[]{:S(2)}) collective-permute-start(f32[27,16,256]{2,1,0:T(8,128)} %get-tuple-element.42.refs_5_), channel_id=1, source_target_pairs={{0,64},{64,0},{1,65},{65,1},{2,66},{66,2},{3,67},{67,3},{4,68},{68... | collective-permute-start | bytes 1327112 | tf_op jit(solution)/shard_map/ppermute | solution.py:920
  34.2 1.9 collective-permute-done.5.refs_8_
  36.1 1.0 copy-done.4
  37.2 1.0 copy-done.6
  38.1 4.9 %leapfrog.1 = (f32[6,4,16,256]{3,2,1,0:T(8,128)}, f32[256,128]{1,0:T(8,128)S(1)}, f32[256,128]{1,0:T(8,128)S(1)}, f32[256,128]{1,0:T(8,128)S(1)}, f32[256,128]{1,0:T(8,128)S(1)}) custom-call(s32[4]{0:T(128)S(1)} %copy-done.15, f32[4]{0:T(128)S(1)} %copy-done.16, f32[4]{0:T(128)S(1)} %copy-done.17, f32[29,16,256]{2,1,0:T(8,128)S(1)} %copy-done.9, ...), custom_call_target="tpu_custom_call" | custom-call | tf_op jit(solution)/shard_map/leapfrog/pallas_call | solution.py:122
  43.7 3.3 %collective-permute-start.6 = (f32[256,128]{1,0:T(8,128)S(1)}, f32[256,128]{1,0:T(8,128)S(1)}, u32[]{:S(2)}, u32[]{:S(2)}) collective-permute-start(f32[256,128]{1,0:T(8,128)S(1)} %get-tuple-element.46), channel_id=1, source_target_pairs={{0,32},{32,0},{64,96},{96,64},{1,33},{33,1},{65,97},{97,65},{2,34}... | collective-permute-start | bytes 393224 | tf_op jit(solution)/shard_map/ppermute | solution.py:924
  47.0 0.7 collective-permute-start.7
  48.5 2.1 collective-permute-done.6.piece1
  50.6 3.7 %collective-permute-done.8.piece3 = f32[256,128]{1,0:T(8,128)S(1)} collective-permute-done((f32[256,128]{1,0:T(8,128)S(1)}, f32[256,128]{1,0:T(8,128)S(1)}, u32[]{:S(2)}, u32[]{:S(2)}) %collective-permute-start.8) | collective-permute-done | bytes 131104 | tf_op jit(solution)/shard_map/ppermute | solution.py:924
  54.3 0.6 copy-done.20
  55.0 2.5 %input_coefs.1 = f32[256,128]{1,0:T(8,128)} custom-call(f32[256,128]{1,0:T(8,128)} %copy-done.8, f32[256,128]{1,0:T(8,128)} %copy-done.18, f32[256,128]{1,0:T(8,128)} %copy-done.19, f32[256,128]{1,0:T(8,128)} %copy-done.20, bf16[2,32,128]{2,1,0:T(8,128)(2,1)} %constant.9.clone.z_half, bf16[2,256,256]{2,1,0:T(8,128)(2,1)} %constant.26.clone.kron.refs_2_.refs_5_), custom_call_target="tpu_custom_call" | custom-call | tf_op jit(solution)/shard_map/input_coefs/pallas_call | solution.py:399
  57.5 8.8 %all-to-all-start = ((f32[32,8,128]{2,1,0:T(8,128)}), f32[32,8,128]{2,1,0:T(8,128)S(1)}, u32[]{:S(2)}, u32[]{:S(2)}) async-start(f32[32,8,128]{2,1,0:T(8,128)} %bitcast.47), calls=%async_computation | async-start | bytes 262144 | tf_op jit(solution)/shard_map/all_to_all | solution.py:975
  67.0 0.7 copy.32.weight
  67.8 4.0 %prepare_inputs.1 = (bf16[4096,256]{1,0:T(8,128)(2,1)}, f32[4096,128]{1,0:T(8,128)}) custom-call(f32[256,128]{1,0:T(8,128)} %copy-done.8, f32[256,128]{1,0:T(8,128)} %copy-done.18, f32[256,128]{1,0:T(8,128)} %copy-done.19, f32[256,128]{1,0:T(8,128)} %copy-done.20, f32[128,128]{1,0:T(8,128)} %pad.27.weight), custom_call_target="tpu_custom_call" | custom-call | tf_op jit(solution)/shard_map/prepare_inputs/pallas_call | solution.py:431
  71.8 2.1 all-to-all-done
  73.9 1.6 copy-done
  75.5 4.3 %modes_first.1 = (f32[256,128]{1,0:T(8,128)}, f32[128,128]{1,0:T(8,128)S(1)}, f32[128,128]{1,0:T(8,128)S(1)}) custom-call(s32[2,3]{1,0:T(2,128)S(1)} %copy-done.14, f32[256,128]{1,0:T(8,128)S(1)} %bitcast.33, f32[128,128]{1,0:T(8,128)S(1)} %fusion.refs_2_, f32[2,8,1024,64]{3,2,1,0:T(8,128)} %bitcast.37, bf16[2,256,256]{2,1,0:T(8,128)(2,1)S(1)} %copy-done.1, ...), custom_call_target="tpu_custom_call" | custom-call | tf_op jit(solution)/shard_map/modes_first/pallas_call | solution.py:122
  79.8 5.6 %all-to-all-start.1 = ((f32[32,8,128]{2,1,0:T(8,128)}), f32[32,8,128]{2,1,0:T(8,128)S(1)}, u32[]{:S(2)}, u32[]{:S(2)}) async-start(f32[32,8,128]{2,1,0:T(8,128)} %bitcast.8), calls=%async_computation.1 | async-start | bytes 262144 | tf_op jit(solution)/shard_map/all_to_all | solution.py:975
  86.0 4.1 %prepare_target.1 = (f32[4096,128]{1,0:T(8,128)}, f32[4096,128]{1,0:T(8,128)}) custom-call(f32[256,128]{1,0:T(8,128)} %copy-done.8, f32[256,128]{1,0:T(8,128)} %copy-done.18, f32[256,128]{1,0:T(8,128)} %copy-done.19, f32[256,128]{1,0:T(8,128)} %copy-done.20, f32[128,128]{1,0:T(8,128)} %copy.32.weight), custom_call_target="tpu_custom_call" | custom-call | tf_op jit(solution)/shard_map/prepare_target/pallas_call | solution.py:431
  90.1 2.7 %all-to-all-done.1 = f32[32,8,128]{2,1,0:T(8,128)S(1)} async-done(((f32[32,8,128]{2,1,0:T(8,128)}), f32[32,8,128]{2,1,0:T(8,128)S(1)}, u32[]{:S(2)}, u32[]{:S(2)}) %all-to-all-start.1) | async-done | bytes 131104 | tf_op jit(solution)/shard_map/all_to_all | solution.py:975
  92.8 0.7 copy-done.25
  93.4 5.3 %cells0.1 = (f32[256,128]{1,0:T(8,128)}, bf16[4096,256]{1,0:T(8,128)(2,1)}, f32[4096,128]{1,0:T(8,128)}) custom-call(f32[256,128]{1,0:T(8,128)} %bitcast.45, f32[4096,128]{1,0:T(8,128)} %get-tuple-element.49.refs_6_.refs_1_, bf16[2,256,256]{2,1,0:T(8,128)(2,1)} %constant.26.clone.kron.refs_2_.refs_5_, bf16[2,256,256]{2,1,0:T(8,128)(2,1)} %constant.29.clone.refs_3_.refs_6_, ...), custom_call_target="tpu_custom_call" | custom-call | tf_op jit(solution)/shard_map/cells0/pallas_call | solution.py:122
  98.7 5.1 %all-to-all-start.2 = ((f32[32,8,128]{2,1,0:T(8,128)}), f32[32,8,128]{2,1,0:T(8,128)S(1)}, u32[]{:S(2)}, u32[]{:S(2)}) async-start(f32[32,8,128]{2,1,0:T(8,128)} %bitcast.49), calls=%async_computation.2 | async-start | bytes 262144 | tf_op jit(solution)/shard_map/all_to_all | solution.py:975
  104.0 7.1 %all-to-all-done.2 = f32[32,8,128]{2,1,0:T(8,128)S(1)} async-done(((f32[32,8,128]{2,1,0:T(8,128)}), f32[32,8,128]{2,1,0:T(8,128)S(1)}, u32[]{:S(2)}, u32[]{:S(2)}) %all-to-all-start.2) | async-done | bytes 131104 | tf_op jit(solution)/shard_map/all_to_all | solution.py:975
  111.1 4.1 %modes_forward.1 = (f32[256,128]{1,0:T(8,128)}, f32[128,128]{1,0:T(8,128)S(1)}) custom-call(s32[2,3]{1,0:T(2,128)S(1)} %copy-done.14, f32[256,128]{1,0:T(8,128)S(1)} %bitcast.35, f32[2,8,1024,64]{3,2,1,0:T(8,128)} %bitcast.38, bf16[2,256,256]{2,1,0:T(8,128)(2,1)S(1)} %copy-done.1, bf16[2,256,256]{2,1,0:T(8,128)(2,1)S(1)} %copy-done.2), custom_call_target="tpu_custom_call" | custom-call | tf_op jit(solution)/shard_map/modes_forward/pallas_call | solution.py:122
  115.2 4.0 %all-to-all-start.3 = ((f32[32,8,128]{2,1,0:T(8,128)}), f32[32,8,128]{2,1,0:T(8,128)S(1)}, u32[]{:S(2)}, u32[]{:S(2)}) async-start(f32[32,8,128]{2,1,0:T(8,128)} %bitcast.12), calls=%async_computation.3 | async-start | bytes 262144 | tf_op jit(solution)/shard_map/all_to_all | solution.py:975
  119.2 0.7 select_maximum_fusion.1
  119.9 0.7 copy.33.refs_3_
  120.6 0.7 select_maximum_fusion.refs_4_
  121.3 5.2 %all-to-all-done.3 = f32[32,8,128]{2,1,0:T(8,128)S(1)} async-done(((f32[32,8,128]{2,1,0:T(8,128)}), f32[32,8,128]{2,1,0:T(8,128)S(1)}, u32[]{:S(2)}, u32[]{:S(2)}) %all-to-all-start.3) | async-done | bytes 131104 | tf_op jit(solution)/shard_map/all_to_all | solution.py:975
  127.2 6.9 %cells1.1 = (f32[256,128]{1,0:T(8,128)}, bf16[4096,256]{1,0:T(8,128)(2,1)}, bf16[4096,256]{1,0:T(8,128)(2,1)}) custom-call(f32[256,128]{1,0:T(8,128)} %bitcast.46, bf16[4096,256]{1,0:T(8,128)(2,1)} %get-tuple-element.54.refs_1_, f32[4096,128]{1,0:T(8,128)} %get-tuple-element.51.refs_6_.refs_2_, f32[128,128]{1,0:T(8,128)} %copy.33.refs_3_, ...), custom_call_target="tpu_custom_call" | custom-call | tf_op jit(solution)/shard_map/cells1/pallas_call | solution.py:122
  134.1 4.0 %all-to-all-start.4 = ((f32[32,8,128]{2,1,0:T(8,128)}), f32[32,8,128]{2,1,0:T(8,128)S(1)}, u32[]{:S(2)}, u32[]{:S(2)}) async-start(f32[32,8,128]{2,1,0:T(8,128)} %bitcast.48), calls=%async_computation.4 | async-start | bytes 262144 | tf_op jit(solution)/shard_map/all_to_all | solution.py:975
  138.0 3.4 %point_grad.1.refs_6_.refs_3_ = f32[32,128]{1,0:T(8,128)} custom-call(bf16[4096,256]{1,0:T(8,128)(2,1)} %get-tuple-element.57.refs_0_.refs_2_, bf16[4096,256]{1,0:T(8,128)(2,1)} %get-tuple-element.54.refs_1_), custom_call_target="tpu_custom_call" | custom-call | tf_op jit(solution)/shard_map/point_grad/pallas_call | solution.py:122
  141.4 3.9 %all-to-all-done.4 = f32[32,8,128]{2,1,0:T(8,128)S(1)} async-done(((f32[32,8,128]{2,1,0:T(8,128)}), f32[32,8,128]{2,1,0:T(8,128)S(1)}, u32[]{:S(2)}, u32[]{:S(2)}) %all-to-all-start.4) | async-done | bytes 131104 | tf_op jit(solution)/shard_map/all_to_all | solution.py:975
  145.4 0.7 copy-done.12
  146.1 4.1 %modes_backward.1 = (f32[256,128]{1,0:T(8,128)}, f32[128,128]{1,0:T(8,128)S(1)}) custom-call(s32[2,3]{1,0:T(2,128)S(1)} %copy-done.14, f32[256,128]{1,0:T(8,128)S(1)} %bitcast.34, f32[128,128]{1,0:T(8,128)S(1)} %get-tuple-element.56.refs_2_, f32[2,8,1024,64]{3,2,1,0:T(8,128)} %bitcast.40, bf16[2,256,256]{2,1,0:T(8,128)(2,1)S(1)} %copy-done.1, ...), custom_call_target="tpu_custom_call" | custom-call | tf_op jit(solution)/shard_map/modes_backward/pallas_call | solution.py:122
  150.8 3.8 %all-to-all-start.5 = ((f32[32,8,128]{2,1,0:T(8,128)}), f32[32,8,128]{2,1,0:T(8,128)S(1)}, u32[]{:S(2)}, u32[]{:S(2)}) async-start(f32[32,8,128]{2,1,0:T(8,128)} %bitcast.19), calls=%async_computation.5 | async-start | bytes 262144 | tf_op jit(solution)/shard_map/all_to_all | solution.py:975
  154.7 4.3 %proj_grad.1.refs_1_ = f32[32,8,128]{2,1,0:T(8,128)} custom-call(bf16[4096,256]{1,0:T(8,128)(2,1)} %get-tuple-element.59.refs_0_, f32[4096,128]{1,0:T(8,128)} %get-tuple-element.60.refs_1_, f32[128,128]{1,0:T(8,128)} %get-tuple-element.74.refs_2_, f32[32,128]{1,0:T(8,128)} %point_grad.1.refs_6_.refs_3_, f32[128,128]{1,0:T(8,128)} %copy-done.10), custom_call_target="tpu_custom_call" | custom-call | tf_op jit(solution)/shard_map/proj_grad/pallas_call | solution.py:122
  159.0 3.0 %all-to-all-done.5 = f32[32,8,128]{2,1,0:T(8,128)S(1)} async-done(((f32[32,8,128]{2,1,0:T(8,128)}), f32[32,8,128]{2,1,0:T(8,128)S(1)}, u32[]{:S(2)}, u32[]{:S(2)}) %all-to-all-start.5) | async-done | bytes 131104 | tf_op jit(solution)/shard_map/all_to_all | solution.py:975
  162.0 0.6 copy-done.24
  162.6 5.4 %cells2.1 = (f32[32,16,128]{2,1,0:T(8,128)}, bf16[4096,256]{1,0:T(8,128)(2,1)}) custom-call(f32[256,128]{1,0:T(8,128)} %bitcast.44, f32[32,8,128]{2,1,0:T(8,128)} %proj_grad.1.refs_1_, bf16[4096,256]{1,0:T(8,128)(2,1)} %get-tuple-element.57.refs_0_.refs_2_, f32[4096,128]{1,0:T(8,128)} %get-tuple-element.62.refs_3_, f32[128,128]{1,0:T(8,128)} %get-tuple-element.76.refs_4_, ...), custom_call_target="tpu_custom_call" | custom-call | tf_op jit(solution)/shard_map/cells2/pallas_call | solution.py:122
  168.0 4.7 %all-to-all-start.6 = ((f32[32,16,128]{2,1,0:T(8,128)}), f32[32,16,128]{2,1,0:T(8,128)S(1)}, u32[]{:S(2)}, u32[]{:S(2)}) async-start(f32[32,16,128]{2,1,0:T(8,128)} %get-tuple-element.63), calls=%async_computation.6 | async-start | bytes 524288 | tf_op jit(solution)/shard_map/all_to_all | solution.py:975
  172.8 3.0 %fusion.5.refs_4_ = f32[256,256]{1,0:T(8,128)S(1)} fusion(bf16[4096,256]{1,0:T(8,128)(2,1)} %get-tuple-element.66, bf16[4096,256]{1,0:T(8,128)(2,1)} %get-tuple-element.67), kind=kOutput, calls=%fused_computation.21 | convolution fusion | flops 536870912 | bytes 4456448 | tf_op jit(solution)/shard_map/dot_general | solution.py:1042
  175.8 5.0 %all-to-all-done.6.refs_1_ = f32[32,16,128]{2,1,0:T(8,128)S(1)} async-done(((f32[32,16,128]{2,1,0:T(8,128)}), f32[32,16,128]{2,1,0:T(8,128)S(1)}, u32[]{:S(2)}, u32[]{:S(2)}) %all-to-all-start.6) | async-done | bytes 262176 | tf_op jit(solution)/shard_map/all_to_all | solution.py:975
  180.8 3.3 %modes_last.1.tail0 = f32[264,128]{1,0:T(8,128)S(1)} custom-call(s32[2,3]{1,0:T(2,128)S(1)} %copy-done.14, f32[32,16,128]{2,1,0:T(8,128)S(1)} %all-to-all-done.6.refs_1_, f32[128,128]{1,0:T(8,128)S(1)} %get-tuple-element.64.refs_2_, f32[128,128]{1,0:T(8,128)S(1)} %get-tuple-element.65.refs_3_, f32[256,256]{1,0:T(8,128)S(1)} %fusion.5.refs_4_, ...), custom_call_target="tpu_custom_call" | custom-call | tf_op jit(solution)/shard_map/modes_last/pallas_call | solution.py:122
  184.1 2.3 %collective-permute-start.9 = (f32[264,128]{1,0:T(8,128)S(1)}, f32[264,128]{1,0:T(8,128)S(1)}, u32[]{:S(2)}, u32[]{:S(2)}) collective-permute-start(f32[264,128]{1,0:T(8,128)S(1)} %modes_last.1.tail0), channel_id=1, source_target_pairs={{0,32},{32,0},{64,96},{96,64},{1,33},{33,1},{65,97},{97,65},{2,34}... | collective-permute-start | bytes 405512 | tf_op jit(solution)/shard_map/ppermute | solution.py:924
  186.4 6.9 %collective-permute-start.10 = (f32[264,128]{1,0:T(8,128)S(1)}, f32[264,128]{1,0:T(8,128)S(1)}, u32[]{:S(2)}, u32[]{:S(2)}) collective-permute-start(f32[264,128]{1,0:T(8,128)S(1)} %modes_last.1.tail0), channel_id=1, source_target_pairs={{0,64},{32,96},{64,0},{96,32},{1,65},{33,97},{65,1},{97,33},{2,66}... | collective-permute-start | bytes 405512 | tf_op jit(solution)/shard_map/ppermute | solution.py:924
  193.3 0.7 collective-permute-start.11
  194.3 5.7 %collective-permute-done.11.tail3 = f32[264,128]{1,0:T(8,128)S(1)} collective-permute-done((f32[264,128]{1,0:T(8,128)S(1)}, f32[264,128]{1,0:T(8,128)S(1)}, u32[]{:S(2)}, u32[]{:S(2)}) %collective-permute-start.11) | collective-permute-done | bytes 135200 | tf_op jit(solution)/shard_map/ppermute | solution.py:924
  200.7 1.4 spread.1
  202.0 3.9 %all-to-all-start.7 = ((f32[32,8,128]{2,1,0:T(8,128)}), f32[32,8,128]{2,1,0:T(8,128)S(1)}, u32[]{:S(2)}, u32[]{:S(2)}) async-start(f32[32,8,128]{2,1,0:T(8,128)} %spread.1), calls=%async_computation.7 | async-start | bytes 262144 | tf_op jit(solution)/shard_map/all_to_all | solution.py:975
  205.9 6.1 %outer.1 = f32[2,8,16,64,64]{4,3,2,1,0:T(8,128)} custom-call(f32[264,128]{1,0:T(8,128)} %copy-done.7, f32[264,128]{1,0:T(8,128)} %copy-done.21, f32[264,128]{1,0:T(8,128)} %copy-done.22, f32[264,128]{1,0:T(8,128)} %copy-done.23), custom_call_target="tpu_custom_call" | custom-call | tf_op jit(solution)/shard_map/outer/pallas_call | solution.py:857
  212.0 1.4 all-to-all-done.7.late
  214.1 1.9 finish.1
  (78 shorter events, 6.9 us)
Async XLA Ops:
  2.4 5.8 %collective-permute-start = (f32[16,256]{1,0:T(8,128)}, f32[16,256]{1,0:T(8,128)S(1)}, u32[]{:S(2)}, u32[]{:S(2)}) collective-permute-start(f32[16,256]{1,0:T(8,128)} %ends.1), channel_id=1, source_target_pairs={{0,32},{32,0},{64,96},{96,64},{1,33},{33,1},{65,97},{97,65},{2,34}... | collective-permute-start | bytes 49160 | tf_op jit(solution)/shard_map/ppermute | solution.py:924
  8.2 0.6 copy-start.32
  11.0 19.3 %collective-permute-start.2 = (f32[27,16,256]{2,1,0:T(8,128)}, f32[27,16,256]{2,1,0:T(8,128)S(1)}, u32[]{:S(2)}, u32[]{:S(2)}) collective-permute-start(f32[27,16,256]{2,1,0:T(8,128)} %get-tuple-element.40), channel_id=1, source_target_pairs={{0,1},{1,2},{2,3},{3,4},{4,5},{5,6},{6,7},{7,8},{8,9},{9,10},{10,1... | collective-permute-start | bytes 1327112 | tf_op jit(solution)/shard_map/ppermute | solution.py:916
  13.9 12.2 %collective-permute-start.3 = (f32[24,16,256]{2,1,0:T(8,128)}, f32[24,16,256]{2,1,0:T(8,128)S(1)}, u32[]{:S(2)}, u32[]{:S(2)}) collective-permute-start(f32[24,16,256]{2,1,0:T(8,128)} %get-tuple-element.41), channel_id=1, source_target_pairs={{1,0},{2,1},{3,2},{4,3},{5,4},{6,5},{7,6},{8,7},{9,8},{10,9},{11,1... | collective-permute-start | bytes 1179656 | tf_op jit(solution)/shard_map/ppermute | solution.py:916
  15.2 19.0 %collective-permute-start.1 = (f32[29,16,256]{2,1,0:T(8,128)}, f32[29,16,256]{2,1,0:T(8,128)}, u32[]{:S(2)}, u32[]{:S(2)}) collective-permute-start(f32[29,16,256]{2,1,0:T(8,128)} %get-tuple-element.39.refs_3_), channel_id=1, source_target_pairs={{0,64},{64,0},{1,65},{65,1},{2,66},{66,2},{3,67},{67,3},{4,68},{68... | collective-permute-start | bytes 1425416 | tf_op jit(solution)/shard_map/ppermute | solution.py:920
  26.1 4.2 %copy-start.5 = (f32[24,16,256]{2,1,0:T(8,128)}, f32[24,16,256]{2,1,0:T(8,128)S(1)}, u32[]{:S(2)}) copy-start(f32[24,16,256]{2,1,0:T(8,128)S(1)} %collective-permute-done.3.refs_2_) | copy-start | bytes 1179652
  30.2 0.8 copy-start.3
  31.0 3.0 %copy-start.29 = (f32[6,64]{1,0:T(8,128)S(1)}, f32[6,64]{1,0:T(8,128)}, u32[]{:S(2)}) copy-start(f32[6,64]{1,0:T(8,128)} %param.27) | copy-start | bytes 4612
  31.0 3.0 %copy-start.28 = (f32[2,64,64]{2,1,0:T(8,128)S(1)}, f32[2,64,64]{2,1,0:T(8,128)}, u32[]{:S(2)}) copy-start(f32[2,64,64]{2,1,0:T(8,128)} %param.25) | copy-start | bytes 98308
  31.0 3.0 %copy-start.31 = (f32[64,6]{0,1:T(8,128)S(1)}, f32[64,6]{0,1:T(8,128)}, u32[]{:S(2)}) copy-start(f32[64,6]{0,1:T(8,128)} %param.24) | copy-start | bytes 4612
  31.0 5.1 %copy-start.9 = (f32[29,16,256]{2,1,0:T(8,128)S(1)}, f32[29,16,256]{2,1,0:T(8,128)}, u32[]{:S(2)}) copy-start(f32[29,16,256]{2,1,0:T(8,128)} %get-tuple-element.39.refs_3_) | copy-start | bytes 1425412
  31.0 5.1 %copy-start.13 = (f32[256,128]{1,0:T(8,128)S(1)}, f32[256,128]{1,0:T(8,128)}, u32[]{:S(2)}) copy-start(f32[256,128]{1,0:T(8,128)} %constant.12.clone.refs_9_) | copy-start | bytes 393220
  31.0 5.1 %copy-start.15 = (s32[4]{0:T(128)S(1)}, s32[4]{0:T(128)}, u32[]{:S(2)}) copy-start(s32[4]{0:T(128)} %refs_0_.5) | copy-start | bytes 52
  31.0 5.1 %copy-start.16 = (f32[4]{0:T(128)S(1)}, f32[4]{0:T(128)}, u32[]{:S(2)}) copy-start(f32[4]{0:T(128)} %refs_1_.1) | copy-start | bytes 52
  31.1 5.1 %copy-start.17 = (f32[4]{0:T(128)S(1)}, f32[4]{0:T(128)}, u32[]{:S(2)}) copy-start(f32[4]{0:T(128)} %refs_2_.2) | copy-start | bytes 52
  31.1 5.0 %collective-permute-start.4 = (f32[27,16,256]{2,1,0:T(8,128)}, f32[27,16,256]{2,1,0:T(8,128)S(1)}, u32[]{:S(2)}, u32[]{:S(2)}) collective-permute-start(f32[27,16,256]{2,1,0:T(8,128)} %get-tuple-element.42.refs_5_), channel_id=1, source_target_pairs={{0,64},{64,0},{1,65},{65,1},{2,66},{66,2},{3,67},{67,3},{4,68},{68... | collective-permute-start | bytes 1327112 | tf_op jit(solution)/shard_map/ppermute | solution.py:920
  33.9 2.2 %collective-permute-start.5 = (f32[24,16,256]{2,1,0:T(8,128)}, f32[24,16,256]{2,1,0:T(8,128)S(1)}, u32[]{:S(2)}, u32[]{:S(2)}) collective-permute-start(f32[24,16,256]{2,1,0:T(8,128)} %get-tuple-element.43.refs_7_), channel_id=1, source_target_pairs={{0,64},{64,0},{1,65},{65,1},{2,66},{66,2},{3,67},{67,3},{4,68},{68... | collective-permute-start | bytes 1179656 | tf_op jit(solution)/shard_map/ppermute | solution.py:920
  34.0 39.9 %copy-start.14 = (s32[2,3]{1,0:T(2,128)S(1)}, s32[2,3]{1,0:T(2,128)}, u32[]{:S(2)}) copy-start(s32[2,3]{1,0:T(2,128)} %refs_0_.9) | copy-start | bytes 76
  34.2 39.8 %copy-start.1 = (bf16[2,256,256]{2,1,0:T(8,128)(2,1)S(1)}, bf16[2,256,256]{2,1,0:T(8,128)(2,1)}, u32[]{:S(2)}) copy-start(bf16[2,256,256]{2,1,0:T(8,128)(2,1)} %constant.27.clone.refs_4_.refs_3_.refs_7_) | copy-start | bytes 786436
  34.2 39.8 %copy-start.2 = (bf16[2,256,256]{2,1,0:T(8,128)(2,1)S(1)}, bf16[2,256,256]{2,1,0:T(8,128)(2,1)}, u32[]{:S(2)}) copy-start(bf16[2,256,256]{2,1,0:T(8,128)(2,1)} %constant.28.clone.refs_5_.refs_4_.refs_8_) | copy-start | bytes 786436
  36.1 1.0 copy-start.4
  37.1 1.0 copy-start.6
  43.1 0.6 copy-start.8
  43.7 6.9 %collective-permute-start.6 = (f32[256,128]{1,0:T(8,128)S(1)}, f32[256,128]{1,0:T(8,128)S(1)}, u32[]{:S(2)}, u32[]{:S(2)}) collective-permute-start(f32[256,128]{1,0:T(8,128)S(1)} %get-tuple-element.46), channel_id=1, source_target_pairs={{0,32},{32,0},{64,96},{96,64},{1,33},{33,1},{65,97},{97,65},{2,34}... | collective-permute-start | bytes 393224 | tf_op jit(solution)/shard_map/ppermute | solution.py:924
  47.0 3.6 %collective-permute-start.7 = (f32[256,128]{1,0:T(8,128)S(1)}, f32[256,128]{1,0:T(8,128)S(1)}, u32[]{:S(2)}, u32[]{:S(2)}) collective-permute-start(f32[256,128]{1,0:T(8,128)S(1)} %get-tuple-element.47), channel_id=1, source_target_pairs={{0,64},{32,96},{64,0},{96,32},{1,65},{33,97},{65,1},{97,33},{2,66}... | collective-permute-start | bytes 393224 | tf_op jit(solution)/shard_map/ppermute | solution.py:924
  47.7 6.6 %collective-permute-start.8 = (f32[256,128]{1,0:T(8,128)S(1)}, f32[256,128]{1,0:T(8,128)S(1)}, u32[]{:S(2)}, u32[]{:S(2)}) collective-permute-start(f32[256,128]{1,0:T(8,128)S(1)} %get-tuple-element.48), channel_id=1, source_target_pairs={{0,96},{32,64},{64,32},{96,0},{1,97},{33,65},{65,33},{97,1},{2,98}... | collective-permute-start | bytes 393224 | tf_op jit(solution)/shard_map/ppermute | solution.py:924
  50.6 3.7 %copy-start.18 = (f32[256,128]{1,0:T(8,128)}, f32[256,128]{1,0:T(8,128)S(1)}, u32[]{:S(2)}) copy-start(f32[256,128]{1,0:T(8,128)S(1)} %collective-permute-done.6.piece1) | copy-start | bytes 393220
  50.6 3.7 %copy-start.19 = (f32[256,128]{1,0:T(8,128)}, f32[256,128]{1,0:T(8,128)S(1)}, u32[]{:S(2)}) copy-start(f32[256,128]{1,0:T(8,128)S(1)} %collective-permute-done.7.piece2) | copy-start | bytes 393220
  54.3 0.7 copy-start.20
  57.5 16.4 %all-to-all-start = ((f32[32,8,128]{2,1,0:T(8,128)}), f32[32,8,128]{2,1,0:T(8,128)S(1)}, u32[]{:S(2)}, u32[]{:S(2)}) async-start(f32[32,8,128]{2,1,0:T(8,128)} %bitcast.47), calls=%async_computation | async-start | bytes 262144 | tf_op jit(solution)/shard_map/all_to_all | solution.py:975
  66.4 13.4 %copy-start.30 = (f32[8,64]{1,0:T(8,128)}, f32[8,64]{1,0:T(8,128)S(1)}, u32[]{:S(2)}) copy-start(f32[8,64]{1,0:T(8,128)S(1)} %pad.25.lift) | copy-start | bytes 6148
  73.9 1.6 copy-start
  79.8 13.0 %all-to-all-start.1 = ((f32[32,8,128]{2,1,0:T(8,128)}), f32[32,8,128]{2,1,0:T(8,128)S(1)}, u32[]{:S(2)}, u32[]{:S(2)}) async-start(f32[32,8,128]{2,1,0:T(8,128)} %bitcast.8), calls=%async_computation.1 | async-start | bytes 262144 | tf_op jit(solution)/shard_map/all_to_all | solution.py:975
  92.8 0.7 copy-start.25
  98.7 12.4 %all-to-all-start.2 = ((f32[32,8,128]{2,1,0:T(8,128)}), f32[32,8,128]{2,1,0:T(8,128)S(1)}, u32[]{:S(2)}, u32[]{:S(2)}) async-start(f32[32,8,128]{2,1,0:T(8,128)} %bitcast.49), calls=%async_computation.2 | async-start | bytes 262144 | tf_op jit(solution)/shard_map/all_to_all | solution.py:975
  115.2 11.3 %all-to-all-start.3 = ((f32[32,8,128]{2,1,0:T(8,128)}), f32[32,8,128]{2,1,0:T(8,128)S(1)}, u32[]{:S(2)}, u32[]{:S(2)}) async-start(f32[32,8,128]{2,1,0:T(8,128)} %bitcast.12), calls=%async_computation.3 | async-start | bytes 262144 | tf_op jit(solution)/shard_map/all_to_all | solution.py:975
  126.5 0.6 copy-start.26
  134.1 11.3 %all-to-all-start.4 = ((f32[32,8,128]{2,1,0:T(8,128)}), f32[32,8,128]{2,1,0:T(8,128)S(1)}, u32[]{:S(2)}, u32[]{:S(2)}) async-start(f32[32,8,128]{2,1,0:T(8,128)} %bitcast.48), calls=%async_computation.4 | async-start | bytes 262144 | tf_op jit(solution)/shard_map/all_to_all | solution.py:975
  145.3 0.7 copy-start.12
  150.2 0.6 copy-start.10
  150.8 11.2 %all-to-all-start.5 = ((f32[32,8,128]{2,1,0:T(8,128)}), f32[32,8,128]{2,1,0:T(8,128)S(1)}, u32[]{:S(2)}, u32[]{:S(2)}) async-start(f32[32,8,128]{2,1,0:T(8,128)} %bitcast.19), calls=%async_computation.5 | async-start | bytes 262144 | tf_op jit(solution)/shard_map/all_to_all | solution.py:975
  162.0 0.7 copy-start.24
  168.0 12.7 %all-to-all-start.6 = ((f32[32,16,128]{2,1,0:T(8,128)}), f32[32,16,128]{2,1,0:T(8,128)S(1)}, u32[]{:S(2)}, u32[]{:S(2)}) async-start(f32[32,16,128]{2,1,0:T(8,128)} %get-tuple-element.63), calls=%async_computation.6 | async-start | bytes 524288 | tf_op jit(solution)/shard_map/all_to_all | solution.py:975
  172.8 8.0 %copy-start.11 = (f32[128,128]{1,0:T(8,128)S(1)}, f32[128,128]{1,0:T(8,128)}, u32[]{:S(2)}) copy-start(f32[128,128]{1,0:T(8,128)} %copy-done.10) | copy-start | bytes 196612
  184.1 15.9 %copy-start.7 = (f32[264,128]{1,0:T(8,128)}, f32[264,128]{1,0:T(8,128)S(1)}, u32[]{:S(2)}) copy-start(f32[264,128]{1,0:T(8,128)S(1)} %modes_last.1.tail0) | copy-start | bytes 405508
  184.1 9.9 %collective-permute-start.9 = (f32[264,128]{1,0:T(8,128)S(1)}, f32[264,128]{1,0:T(8,128)S(1)}, u32[]{:S(2)}, u32[]{:S(2)}) collective-permute-start(f32[264,128]{1,0:T(8,128)S(1)} %modes_last.1.tail0), channel_id=1, source_target_pairs={{0,32},{32,0},{64,96},{96,64},{1,33},{33,1},{65,97},{97,65},{2,34}... | collective-permute-start | bytes 405512 | tf_op jit(solution)/shard_map/ppermute | solution.py:924
  186.4 7.9 %collective-permute-start.10 = (f32[264,128]{1,0:T(8,128)S(1)}, f32[264,128]{1,0:T(8,128)S(1)}, u32[]{:S(2)}, u32[]{:S(2)}) collective-permute-start(f32[264,128]{1,0:T(8,128)S(1)} %modes_last.1.tail0), channel_id=1, source_target_pairs={{0,64},{32,96},{64,0},{96,32},{1,65},{33,97},{65,1},{97,33},{2,66}... | collective-permute-start | bytes 405512 | tf_op jit(solution)/shard_map/ppermute | solution.py:924
  193.3 6.7 %collective-permute-start.11 = (f32[264,128]{1,0:T(8,128)S(1)}, f32[264,128]{1,0:T(8,128)S(1)}, u32[]{:S(2)}, u32[]{:S(2)}) collective-permute-start(f32[264,128]{1,0:T(8,128)S(1)} %modes_last.1.tail0), channel_id=1, source_target_pairs={{0,96},{32,64},{64,32},{96,0},{1,97},{33,65},{65,33},{97,1},{2,98}... | collective-permute-start | bytes 405512 | tf_op jit(solution)/shard_map/ppermute | solution.py:924
  194.0 6.0 %copy-start.21 = (f32[264,128]{1,0:T(8,128)}, f32[264,128]{1,0:T(8,128)S(1)}, u32[]{:S(2)}) copy-start(f32[264,128]{1,0:T(8,128)S(1)} %collective-permute-done.9.tail1) | copy-start | bytes 405508
  194.3 5.7 %copy-start.22 = (f32[264,128]{1,0:T(8,128)}, f32[264,128]{1,0:T(8,128)S(1)}, u32[]{:S(2)}) copy-start(f32[264,128]{1,0:T(8,128)S(1)} %collective-permute-done.10.tail2) | copy-start | bytes 405508
  200.0 0.7 copy-start.23
  202.0 11.4 %all-to-all-start.7 = ((f32[32,8,128]{2,1,0:T(8,128)}), f32[32,8,128]{2,1,0:T(8,128)S(1)}, u32[]{:S(2)}, u32[]{:S(2)}) async-start(f32[32,8,128]{2,1,0:T(8,128)} %spread.1), calls=%async_computation.7 | async-start | bytes 262144 | tf_op jit(solution)/shard_map/all_to_all | solution.py:975
  213.4 0.6 copy-start.27

commit v4 on v3

--- a/solution.py
+++ b/solution.py
@@ -20,7 +20,7 @@
 NN = (((1,), (0,)), ((), ()))
 NT = (((1,), (1,)), ((), ()))
 TN = (((0,), (0,)), ((), ()))
-ROOM = 62 * 1024 * 1024
+ROOM = 48 * 1024 * 1024
 LEAP_ROOM = 24 * 1024 * 1024
 CELL_ROOM = 62 * 1024 * 1024
 MODE_ROOM = 48 * 1024 * 1024

time: 217 us -> 203 us (0.935)
  Pallas kernels: 70 us -> 51.1 us
  waiting for transfers between devices: 49.6 us -> 52.9 us
  local copies, waits for them, and re-layouts: 22.3 us -> 25.5 us
    pallas_call x2, Pallas kernels: 8.05 us -> 2.06 us  [prepare(): pl.pallas_call(functools.partial(prep_kernel, first_row), out_shape=[own,...]
    pallas_call x11, Pallas kernels: 46 us -> 40.8 us  [call(): pl.pallas_call(run, out_shape=[o[0] for o in outs] + [jax.ShapeDtypeStruc...]
    unnamed x66 -> x62, local copies, waits for them, and re-layouts: 10.9 us -> 15.2 us
    all_to_all x8, waiting for transfers between devices: 30.4 us -> 33.5 us  [swap(): return lax.all_to_all(value, 'tile', 0, 0, tiled=True)]
  transfers between devices with their start and end apart: 20 -> 20, of which waited for: 15 -> 15; matrix products, arithmetic and copies ran while one was open for 8% -> 8% of each run, Pallas kernels for 10% -> 5%
where the time goes in v4:
time: 203 us; the launch traced here: 202 us
  starting transfers between devices  66.3 us (33%)
  waiting for transfers between devices  52.9 us (26%)
  Pallas kernels  51.1 us (25%)
  local copies, waits for them, and re-layouts  25.5 us (13%)
  matrix products  3.37 us (2%)
    pallas_call x11, Pallas kernels, call(): pl.pallas_call(run, out_shape=[o[0] for o in outs] + [jax.ShapeDtypeStruc...  40.8 us
    all_to_all x8, starting transfers between devices, swap(): return lax.all_to_all(value, 'tile', 0, 0, tiled=True)  38.8 us
    all_to_all x8, waiting for transfers between devices, swap(): return lax.all_to_all(value, 'tile', 0, 0, tiled=True)  33.5 us
    ppermute x7, starting transfers between devices, xor_group(): return lax.ppermute(value, GROUP, [(i, i ^ d) for i in range(4)])  18.3 us
    unnamed x62, local copies, waits for them, and re-layouts  15.2 us
    ppermute x7, waiting for transfers between devices, xor_group(): return lax.ppermute(value, GROUP, [(i, i ^ d) for i in range(4)])  13.9 us
    transpose x1, local copies, waits for them, and re-layouts, local(): turned = jnp.swapaxes(spectral_weight, -1, -2).reshape(LAYERS, 8, 1024, 64)  8.66 us
    ppermute x3, starting transfers between devices, across(): return lax.ppermute(value, axis, [(0, 1), (1, 0)])  5.1 us
  transfers between devices with their start and end apart: 20, of which 15 were waited for; matrix products, arithmetic and copies ran while one was open for 8% of the time, Pallas kernels for 5%

profile of v4, /device:TPU:1, one launch (start us, length us, event | category | flops | bytes accessed | tf_op | source)
XLA Modules:
  0.0 202.0 jit_solution(7933231654174695944)
XLA Ops:
  0.6 1.0 copy-done.10
  1.6 0.8 copy-done.12
  2.6 4.5 %collective-permute-start = (f32[16,256]{1,0:T(8,128)S(1)}, f32[16,256]{1,0:T(8,128)S(1)}, u32[]{:S(2)}, u32[]{:S(2)}) collective-permute-start(f32[16,256]{1,0:T(8,128)S(1)} %ends.1), channel_id=1, source_target_pairs={{0,32},{32,0},{64,96},{96,64},{1,33},{33,1},{65,97},{97,65},{2,34}... | collective-permute-start | bytes 49160 | tf_op jit(solution)/shard_map/ppermute | solution.py:924
  7.2 1.1 collective-permute-done.ends
  8.4 2.9 %collective-permute-start.2 = (f32[27,16,256]{2,1,0:T(8,128)S(1)}, f32[27,16,256]{2,1,0:T(8,128)S(1)}, u32[]{:S(2)}, u32[]{:S(2)}) collective-permute-start(f32[27,16,256]{2,1,0:T(8,128)S(1)} %get-tuple-element.40), channel_id=1, source_target_pairs={{0,1},{1,2},{2,3},{3,4},{4,5},{5,6},{6,7},{7,8},{8,9},{9,10},{10,1... | collective-permute-start | bytes 1327112 | tf_op jit(solution)/shard_map/ppermute | solution.py:916
  11.3 1.3 collective-permute-start.3
  12.6 2.2 %collective-permute-start.1 = (f32[29,16,256]{2,1,0:T(8,128)S(1)}, f32[29,16,256]{2,1,0:T(8,128)S(1)}, u32[]{:S(2)}, u32[]{:S(2)}) collective-permute-start(f32[29,16,256]{2,1,0:T(8,128)S(1)} %get-tuple-element.39.refs_3_), channel_id=1, source_target_pairs={{0,64},{64,0},{1,65},{65,1},{2,66},{66,2},{3,67},{67,3},{4,68},{68... | collective-permute-start | bytes 1425416 | tf_op jit(solution)/shard_map/ppermute | solution.py:920
  14.8 8.7 %copy.30 = f32[2,8,16,64,64]{4,3,2,1,0:T(8,128)} copy(f32[2,8,16,64,64]{3,4,2,1,0:T(8,128)} %bitcast.42) | data formatting | bytes 8388608 | tf_op jit(solution)/shard_map/transpose | solution.py:947
  23.5 3.9 %collective-permute-done.2.refs_1_ = f32[27,16,256]{2,1,0:T(8,128)S(1)} collective-permute-done((f32[27,16,256]{2,1,0:T(8,128)S(1)}, f32[27,16,256]{2,1,0:T(8,128)S(1)}, u32[]{:S(2)}, u32[]{:S(2)}) %collective-permute-start.2) | collective-permute-done | bytes 442400 | tf_op jit(solution)/shard_map/ppermute | solution.py:916
  27.4 2.8 %collective-permute-start.4 = (f32[27,16,256]{2,1,0:T(8,128)S(1)}, f32[27,16,256]{2,1,0:T(8,128)S(1)}, u32[]{:S(2)}, u32[]{:S(2)}) collective-permute-start(f32[27,16,256]{2,1,0:T(8,128)S(1)} %get-tuple-element.42.refs_5_), channel_id=1, source_target_pairs={{0,64},{64,0},{1,65},{65,1},{2,66},{66,2},{3,67},{67,3},{4,68},{68... | collective-permute-start | bytes 1327112 | tf_op jit(solution)/shard_map/ppermute | solution.py:920
  30.5 1.7 collective-permute-done.5.refs_8_
  32.2 4.6 %leapfrog.1 = (f32[6,4,16,256]{3,2,1,0:T(8,128)}, f32[256,128]{1,0:T(8,128)S(1)}, f32[256,128]{1,0:T(8,128)}, f32[256,128]{1,0:T(8,128)}, f32[256,128]{1,0:T(8,128)S(1)}) custom-call(s32[4]{0:T(128)S(1)} %copy-done.21, f32[4]{0:T(128)S(1)} %copy-done.22, f32[4]{0:T(128)S(1)} %copy-done.23, f32[29,16,256]{2,1,0:T(8,128)S(1)} %get-tuple-element.39.refs_3_, ...), custom_call_target="tpu_custom_call" | custom-call | tf_op jit(solution)/shard_map/leapfrog/pallas_call | solution.py:122
  36.9 3.3 %collective-permute-start.6 = (f32[256,128]{1,0:T(8,128)}, f32[256,128]{1,0:T(8,128)S(1)}, u32[]{:S(2)}, u32[]{:S(2)}) collective-permute-start(f32[256,128]{1,0:T(8,128)} %get-tuple-element.46), channel_id=1, source_target_pairs={{0,32},{32,0},{64,96},{96,64},{1,33},{33,1},{65,97},{97,65},{2,34}... | collective-permute-start | bytes 393224 | tf_op jit(solution)/shard_map/ppermute | solution.py:924
  40.2 0.7 collective-permute-start.7
  41.0 2.9 %collective-permute-done.6.piece1 = f32[256,128]{1,0:T(8,128)S(1)} collective-permute-done((f32[256,128]{1,0:T(8,128)}, f32[256,128]{1,0:T(8,128)S(1)}, u32[]{:S(2)}, u32[]{:S(2)}) %collective-permute-start.6) | collective-permute-done | bytes 131104 | tf_op jit(solution)/shard_map/ppermute | solution.py:924
  44.0 3.5 %collective-permute-done.8.piece3 = f32[256,128]{1,0:T(8,128)S(1)} collective-permute-done((f32[256,128]{1,0:T(8,128)S(1)}, f32[256,128]{1,0:T(8,128)S(1)}, u32[]{:S(2)}, u32[]{:S(2)}) %collective-permute-start.8) | collective-permute-done | bytes 131104 | tf_op jit(solution)/shard_map/ppermute | solution.py:924
  47.5 1.3 input_coefs.1
  48.8 8.8 %all-to-all-start = ((f32[32,8,128]{2,1,0:T(8,128)}), f32[32,8,128]{2,1,0:T(8,128)S(1)}, u32[]{:S(2)}, u32[]{:S(2)}) async-start(f32[32,8,128]{2,1,0:T(8,128)} %bitcast.4), calls=%async_computation | async-start | bytes 262144 | tf_op jit(solution)/shard_map/all_to_all | solution.py:975
  57.9 1.0 prepare_inputs.1
  58.9 1.3 copy-done.24
  60.2 5.0 %all-to-all-done = f32[32,8,128]{2,1,0:T(8,128)S(1)} async-done(((f32[32,8,128]{2,1,0:T(8,128)}), f32[32,8,128]{2,1,0:T(8,128)S(1)}, u32[]{:S(2)}, u32[]{:S(2)}) %all-to-all-start) | async-done | bytes 131104 | tf_op jit(solution)/shard_map/all_to_all | solution.py:975
  65.2 3.6 %modes_first.1 = (f32[256,128]{1,0:T(8,128)S(1)}, f32[128,128]{1,0:T(8,128)S(1)}, f32[128,128]{1,0:T(8,128)S(1)}) custom-call(s32[2,3]{1,0:T(2,128)S(1)} %copy-done.20, f32[256,128]{1,0:T(8,128)S(1)} %bitcast.35, f32[128,128]{1,0:T(8,128)S(1)} %fusion.refs_2_, f32[2,8,1024,64]{3,2,1,0:T(8,128)} %bitcast.40, bf16[2,256,256]{2,1,0:T(8,128)(2,1)S(1)} %copy-done.4, ...), custom_call_target="tpu_custom_call" | custom-call | tf_op jit(solution)/shard_map/modes_first/pallas_call | solution.py:122
  70.1 0.6 copy-done.14
  70.8 3.9 %all-to-all-start.1 = ((f32[32,8,128]{2,1,0:T(8,128)}), f32[32,8,128]{2,1,0:T(8,128)S(1)}, u32[]{:S(2)}, u32[]{:S(2)}) async-start(f32[32,8,128]{2,1,0:T(8,128)} %bitcast.38), calls=%async_computation.1 | async-start | bytes 262144 | tf_op jit(solution)/shard_map/all_to_all | solution.py:975
  74.6 0.8 slice_bitcast_fusion.1
  75.4 1.0 prepare_target.1
  76.4 1.4 copy-done
  77.8 1.3 copy-done.7
  79.2 2.8 %all-to-all-done.1 = f32[32,8,128]{2,1,0:T(8,128)S(1)} async-done(((f32[32,8,128]{2,1,0:T(8,128)}), f32[32,8,128]{2,1,0:T(8,128)S(1)}, u32[]{:S(2)}, u32[]{:S(2)}) %all-to-all-start.1) | async-done | bytes 131104 | tf_op jit(solution)/shard_map/all_to_all | solution.py:975
  81.9 0.7 copy-done.26
  82.6 5.3 %cells0.1 = (f32[256,128]{1,0:T(8,128)}, bf16[4096,256]{1,0:T(8,128)(2,1)}, f32[4096,128]{1,0:T(8,128)}) custom-call(f32[256,128]{1,0:T(8,128)} %bitcast.46, f32[4096,128]{1,0:T(8,128)} %copy-done.3, bf16[2,256,256]{2,1,0:T(8,128)(2,1)} %constant.26.clone.kron.refs_2_.refs_5_, bf16[2,256,256]{2,1,0:T(8,128)(2,1)} %constant.29.clone.refs_3_.refs_6_, ...), custom_call_target="tpu_custom_call" | custom-call | tf_op jit(solution)/shard_map/cells0/pallas_call | solution.py:122
  87.9 5.0 %all-to-all-start.2 = ((f32[32,8,128]{2,1,0:T(8,128)}), f32[32,8,128]{2,1,0:T(8,128)S(1)}, u32[]{:S(2)}, u32[]{:S(2)}) async-start(f32[32,8,128]{2,1,0:T(8,128)} %bitcast.49), calls=%async_computation.2 | async-start | bytes 262144 | tf_op jit(solution)/shard_map/all_to_all | solution.py:975
  93.1 7.1 %all-to-all-done.2 = f32[32,8,128]{2,1,0:T(8,128)S(1)} async-done(((f32[32,8,128]{2,1,0:T(8,128)}), f32[32,8,128]{2,1,0:T(8,128)S(1)}, u32[]{:S(2)}, u32[]{:S(2)}) %all-to-all-start.2) | async-done | bytes 131104 | tf_op jit(solution)/shard_map/all_to_all | solution.py:975
  100.2 4.1 %modes_forward.1 = (f32[256,128]{1,0:T(8,128)}, f32[128,128]{1,0:T(8,128)S(1)}) custom-call(s32[2,3]{1,0:T(2,128)S(1)} %copy-done.20, f32[256,128]{1,0:T(8,128)S(1)} %bitcast.37, f32[2,8,1024,64]{3,2,1,0:T(8,128)} %bitcast.41, bf16[2,256,256]{2,1,0:T(8,128)(2,1)S(1)} %copy-done.4, bf16[2,256,256]{2,1,0:T(8,128)(2,1)S(1)} %copy-done.5), custom_call_target="tpu_custom_call" | custom-call | tf_op jit(solution)/shard_map/modes_forward/pallas_call | solution.py:122
  104.3 4.0 %all-to-all-start.3 = ((f32[32,8,128]{2,1,0:T(8,128)}), f32[32,8,128]{2,1,0:T(8,128)S(1)}, u32[]{:S(2)}, u32[]{:S(2)}) async-start(f32[32,8,128]{2,1,0:T(8,128)} %bitcast.12), calls=%async_computation.3 | async-start | bytes 262144 | tf_op jit(solution)/shard_map/all_to_all | solution.py:975
  108.3 0.7 select_maximum_fusion.1
  109.0 0.7 copy.33.refs_3_
  109.7 0.7 select_maximum_fusion.refs_4_
  110.4 5.2 %all-to-all-done.3 = f32[32,8,128]{2,1,0:T(8,128)S(1)} async-done(((f32[32,8,128]{2,1,0:T(8,128)}), f32[32,8,128]{2,1,0:T(8,128)S(1)}, u32[]{:S(2)}, u32[]{:S(2)}) %all-to-all-start.3) | async-done | bytes 131104 | tf_op jit(solution)/shard_map/all_to_all | solution.py:975
  116.2 6.9 %cells1.1 = (f32[256,128]{1,0:T(8,128)}, bf16[4096,256]{1,0:T(8,128)(2,1)}, bf16[4096,256]{1,0:T(8,128)(2,1)}) custom-call(f32[256,128]{1,0:T(8,128)} %bitcast.47, bf16[4096,256]{1,0:T(8,128)(2,1)} %get-tuple-element.54.refs_1_, f32[4096,128]{1,0:T(8,128)} %copy-done, f32[128,128]{1,0:T(8,128)} %copy.33.refs_3_, f32[128,128]{1,0:T(8,128)} %select_maximum_fusion.refs_4_, ...), custom_call_target="tpu_custom_call" | custom-call | tf_op jit(solution)/shard_map/cells1/pallas_call | solution.py:122
  123.2 3.8 %all-to-all-start.4 = ((f32[32,8,128]{2,1,0:T(8,128)}), f32[32,8,128]{2,1,0:T(8,128)S(1)}, u32[]{:S(2)}, u32[]{:S(2)}) async-start(f32[32,8,128]{2,1,0:T(8,128)} %bitcast.48), calls=%async_computation.4 | async-start | bytes 262144 | tf_op jit(solution)/shard_map/all_to_all | solution.py:975
  127.0 1.6 copy-done.1
  128.6 1.6 copy-done.2
  130.2 1.1 point_grad.1.refs_6_.refs_3_
  131.3 3.0 %all-to-all-done.4 = f32[32,8,128]{2,1,0:T(8,128)S(1)} async-done(((f32[32,8,128]{2,1,0:T(8,128)}), f32[32,8,128]{2,1,0:T(8,128)S(1)}, u32[]{:S(2)}, u32[]{:S(2)}) %all-to-all-start.4) | async-done | bytes 131104 | tf_op jit(solution)/shard_map/all_to_all | solution.py:975
  134.3 4.3 %modes_backward.1 = (f32[256,128]{1,0:T(8,128)}, f32[128,128]{1,0:T(8,128)S(1)}) custom-call(s32[2,3]{1,0:T(2,128)S(1)} %copy-done.20, f32[256,128]{1,0:T(8,128)S(1)} %bitcast.36, f32[128,128]{1,0:T(8,128)S(1)} %get-tuple-element.56.refs_2_, f32[2,8,1024,64]{3,2,1,0:T(8,128)} %bitcast.43, bf16[2,256,256]{2,1,0:T(8,128)(2,1)S(1)} %copy-done.4, ...), custom_call_target="tpu_custom_call" | custom-call | tf_op jit(solution)/shard_map/modes_backward/pallas_call | solution.py:122
  138.6 4.7 %all-to-all-start.5 = ((f32[32,8,128]{2,1,0:T(8,128)}), f32[32,8,128]{2,1,0:T(8,128)S(1)}, u32[]{:S(2)}, u32[]{:S(2)}) async-start(f32[32,8,128]{2,1,0:T(8,128)} %bitcast.19), calls=%async_computation.5 | async-start | bytes 262144 | tf_op jit(solution)/shard_map/all_to_all | solution.py:975
  143.3 1.6 copy-done.9
  144.9 2.1 %proj_grad.1.refs_1_ = f32[32,8,128]{2,1,0:T(8,128)S(1)} custom-call(bf16[4096,256]{1,0:T(8,128)(2,1)S(1)} %copy-done.9, f32[4096,128]{1,0:T(8,128)S(1)} %copy-done.8, f32[128,128]{1,0:T(8,128)S(1)} %get-tuple-element.74.refs_2_, f32[32,128]{1,0:T(8,128)S(1)} %point_grad.1.refs_6_.refs_3_, f32[128,128]{1,0:T(8,128)S(1)} %get-tuple-element.61.refs_4_.refs_5_), custom_call_target="tpu_custom_call" | custom-call | tf_op jit(solution)/shard_map/proj_grad/pallas_call | solution.py:122
  147.7 3.0 %all-to-all-done.5 = f32[32,8,128]{2,1,0:T(8,128)S(1)} async-done(((f32[32,8,128]{2,1,0:T(8,128)}), f32[32,8,128]{2,1,0:T(8,128)S(1)}, u32[]{:S(2)}, u32[]{:S(2)}) %all-to-all-start.5) | async-done | bytes 131104 | tf_op jit(solution)/shard_map/all_to_all | solution.py:975
  150.6 0.6 copy-done.25
  151.3 5.4 %cells2.1 = (f32[32,16,128]{2,1,0:T(8,128)}, bf16[4096,256]{1,0:T(8,128)(2,1)}) custom-call(f32[256,128]{1,0:T(8,128)} %bitcast.45, f32[32,8,128]{2,1,0:T(8,128)} %copy-done.11, bf16[4096,256]{1,0:T(8,128)(2,1)} %get-tuple-element.57.refs_0_.refs_2_, f32[4096,128]{1,0:T(8,128)} %get-tuple-element.62.refs_3_, f32[128,128]{1,0:T(8,128)} %get-tuple-element.76.refs_4_, ...), custom_call_target="tpu_custom_call" | custom-call | tf_op jit(solution)/shard_map/cells2/pallas_call | solution.py:122
  156.7 4.8 %all-to-all-start.6 = ((f32[32,16,128]{2,1,0:T(8,128)}), f32[32,16,128]{2,1,0:T(8,128)S(1)}, u32[]{:S(2)}, u32[]{:S(2)}) async-start(f32[32,16,128]{2,1,0:T(8,128)} %get-tuple-element.63), calls=%async_computation.6 | async-start | bytes 524288 | tf_op jit(solution)/shard_map/all_to_all | solution.py:975
  161.5 3.0 %fusion.5.refs_4_ = f32[256,256]{1,0:T(8,128)S(1)} fusion(bf16[4096,256]{1,0:T(8,128)(2,1)} %copy-done.24, bf16[4096,256]{1,0:T(8,128)(2,1)} %get-tuple-element.67), kind=kOutput, calls=%fused_computation.21 | convolution fusion | flops 536870912 | bytes 4456448 | tf_op jit(solution)/shard_map/dot_general | solution.py:1042
  164.5 5.0 %all-to-all-done.6.refs_1_ = f32[32,16,128]{2,1,0:T(8,128)S(1)} async-done(((f32[32,16,128]{2,1,0:T(8,128)}), f32[32,16,128]{2,1,0:T(8,128)S(1)}, u32[]{:S(2)}, u32[]{:S(2)}) %all-to-all-start.6) | async-done | bytes 262176 | tf_op jit(solution)/shard_map/all_to_all | solution.py:975
  169.5 3.3 %modes_last.1.tail0 = f32[264,128]{1,0:T(8,128)S(1)} custom-call(s32[2,3]{1,0:T(2,128)S(1)} %copy-done.20, f32[32,16,128]{2,1,0:T(8,128)S(1)} %all-to-all-done.6.refs_1_, f32[128,128]{1,0:T(8,128)S(1)} %copy-done.18, f32[128,128]{1,0:T(8,128)S(1)} %copy-done.16, f32[256,256]{1,0:T(8,128)S(1)} %fusion.5.refs_4_, ...), custom_call_target="tpu_custom_call" | custom-call | tf_op jit(solution)/shard_map/modes_last/pallas_call | solution.py:122
  172.8 2.6 %collective-permute-start.9 = (f32[264,128]{1,0:T(8,128)S(1)}, f32[264,128]{1,0:T(8,128)S(1)}, u32[]{:S(2)}, u32[]{:S(2)}) collective-permute-start(f32[264,128]{1,0:T(8,128)S(1)} %modes_last.1.tail0), channel_id=1, source_target_pairs={{0,32},{32,0},{64,96},{96,64},{1,33},{33,1},{65,97},{97,65},{2,34}... | collective-permute-start | bytes 405512 | tf_op jit(solution)/shard_map/ppermute | solution.py:924
  175.4 6.8 %collective-permute-start.10 = (f32[264,128]{1,0:T(8,128)S(1)}, f32[264,128]{1,0:T(8,128)S(1)}, u32[]{:S(2)}, u32[]{:S(2)}) collective-permute-start(f32[264,128]{1,0:T(8,128)S(1)} %modes_last.1.tail0), channel_id=1, source_target_pairs={{0,64},{32,96},{64,0},{96,32},{1,65},{33,97},{65,1},{97,33},{2,66}... | collective-permute-start | bytes 405512 | tf_op jit(solution)/shard_map/ppermute | solution.py:924
  183.2 5.7 %collective-permute-done.11.tail3 = f32[264,128]{1,0:T(8,128)S(1)} collective-permute-done((f32[264,128]{1,0:T(8,128)S(1)}, f32[264,128]{1,0:T(8,128)S(1)}, u32[]{:S(2)}, u32[]{:S(2)}) %collective-permute-start.11) | collective-permute-done | bytes 135200 | tf_op jit(solution)/shard_map/ppermute | solution.py:924
  188.9 0.7 spread.1
  189.6 3.8 %all-to-all-start.7 = ((f32[32,8,128]{2,1,0:T(8,128)}), f32[32,8,128]{2,1,0:T(8,128)S(1)}, u32[]{:S(2)}, u32[]{:S(2)}) async-start(f32[32,8,128]{2,1,0:T(8,128)} %spread.1), calls=%async_computation.7 | async-start | bytes 262144 | tf_op jit(solution)/shard_map/all_to_all | solution.py:975
  193.5 5.0 %outer.1 = f32[2,8,16,64,64]{4,3,2,1,0:T(8,128)} custom-call(f32[264,128]{1,0:T(8,128)S(1)} %modes_last.1.tail0, f32[264,128]{1,0:T(8,128)S(1)} %collective-permute-done.9.tail1, f32[264,128]{1,0:T(8,128)S(1)} %collective-permute-done.10.tail2, f32[264,128]{1,0:T(8,128)S(1)} %collective-permute-done.11.tail3), custom_call_target="tpu_custom_call" | custom-call | tf_op jit(solution)/shard_map/outer/pallas_call | solution.py:857
  198.5 2.5 %all-to-all-done.7.late = f32[32,8,128]{2,1,0:T(8,128)S(1)} async-done(((f32[32,8,128]{2,1,0:T(8,128)}), f32[32,8,128]{2,1,0:T(8,128)S(1)}, u32[]{:S(2)}, u32[]{:S(2)}) %all-to-all-start.7) | async-done | bytes 131104 | tf_op jit(solution)/shard_map/all_to_all | solution.py:975
  201.0 1.0 finish.1
  (74 shorter events, 4.8 us)
Async XLA Ops:
  0.6 1.0 copy-start.10
  1.6 0.8 copy-start.12
  2.6 5.6 %collective-permute-start = (f32[16,256]{1,0:T(8,128)S(1)}, f32[16,256]{1,0:T(8,128)S(1)}, u32[]{:S(2)}, u32[]{:S(2)}) collective-permute-start(f32[16,256]{1,0:T(8,128)S(1)} %ends.1), channel_id=1, source_target_pairs={{0,32},{32,0},{64,96},{96,64},{1,33},{33,1},{65,97},{97,65},{2,34}... | collective-permute-start | bytes 49160 | tf_op jit(solution)/shard_map/ppermute | solution.py:924
  8.4 19.0 %collective-permute-start.2 = (f32[27,16,256]{2,1,0:T(8,128)S(1)}, f32[27,16,256]{2,1,0:T(8,128)S(1)}, u32[]{:S(2)}, u32[]{:S(2)}) collective-permute-start(f32[27,16,256]{2,1,0:T(8,128)S(1)} %get-tuple-element.40), channel_id=1, source_target_pairs={{0,1},{1,2},{2,3},{3,4},{4,5},{5,6},{6,7},{7,8},{8,9},{9,10},{10,1... | collective-permute-start | bytes 1327112 | tf_op jit(solution)/shard_map/ppermute | solution.py:916
  11.3 12.2 %collective-permute-start.3 = (f32[24,16,256]{2,1,0:T(8,128)S(1)}, f32[24,16,256]{2,1,0:T(8,128)S(1)}, u32[]{:S(2)}, u32[]{:S(2)}) collective-permute-start(f32[24,16,256]{2,1,0:T(8,128)S(1)} %get-tuple-element.41), channel_id=1, source_target_pairs={{1,0},{2,1},{3,2},{4,3},{5,4},{6,5},{7,6},{8,7},{9,8},{10,9},{11,1... | collective-permute-start | bytes 1179656 | tf_op jit(solution)/shard_map/ppermute | solution.py:916
  12.6 17.9 %collective-permute-start.1 = (f32[29,16,256]{2,1,0:T(8,128)S(1)}, f32[29,16,256]{2,1,0:T(8,128)S(1)}, u32[]{:S(2)}, u32[]{:S(2)}) collective-permute-start(f32[29,16,256]{2,1,0:T(8,128)S(1)} %get-tuple-element.39.refs_3_), channel_id=1, source_target_pairs={{0,64},{64,0},{1,65},{65,1},{2,66},{66,2},{3,67},{67,3},{4,68},{68... | collective-permute-start | bytes 1425416 | tf_op jit(solution)/shard_map/ppermute | solution.py:920
  27.3 3.0 %copy-start.29 = (f32[6,64]{1,0:T(8,128)S(1)}, f32[6,64]{1,0:T(8,128)}, u32[]{:S(2)}) copy-start(f32[6,64]{1,0:T(8,128)} %param.27) | copy-start | bytes 4612
  27.3 3.0 %copy-start.28 = (f32[2,64,64]{2,1,0:T(8,128)S(1)}, f32[2,64,64]{2,1,0:T(8,128)}, u32[]{:S(2)}) copy-start(f32[2,64,64]{2,1,0:T(8,128)} %param.25) | copy-start | bytes 98308
  27.3 3.0 %copy-start.30 = (f32[64,6]{0,1:T(8,128)S(1)}, f32[64,6]{0,1:T(8,128)}, u32[]{:S(2)}) copy-start(f32[64,6]{0,1:T(8,128)} %param.24) | copy-start | bytes 4612
  27.3 4.9 %copy-start.13 = (f32[256,128]{1,0:T(8,128)S(1)}, f32[256,128]{1,0:T(8,128)}, u32[]{:S(2)}) copy-start(f32[256,128]{1,0:T(8,128)} %constant.12.clone.refs_9_) | copy-start | bytes 393220
  27.3 4.9 %copy-start.21 = (s32[4]{0:T(128)S(1)}, s32[4]{0:T(128)}, u32[]{:S(2)}) copy-start(s32[4]{0:T(128)} %refs_0_.5) | copy-start | bytes 52
  27.4 4.9 %copy-start.22 = (f32[4]{0:T(128)S(1)}, f32[4]{0:T(128)}, u32[]{:S(2)}) copy-start(f32[4]{0:T(128)} %refs_1_.1) | copy-start | bytes 52
  27.4 4.9 %copy-start.23 = (f32[4]{0:T(128)S(1)}, f32[4]{0:T(128)}, u32[]{:S(2)}) copy-start(f32[4]{0:T(128)} %refs_2_.2) | copy-start | bytes 52
  27.4 20.1 %copy-start.6 = (bf16[2,256,256]{2,1,0:T(8,128)(2,1)S(1)}, bf16[2,256,256]{2,1,0:T(8,128)(2,1)}, u32[]{:S(2)}) copy-start(bf16[2,256,256]{2,1,0:T(8,128)(2,1)} %constant.26.clone.kron.refs_2_.refs_5_) | copy-start | bytes 786436
  27.4 20.1 %copy-start.19 = (bf16[2,32,128]{2,1,0:T(8,128)(2,1)S(1)}, bf16[2,32,128]{2,1,0:T(8,128)(2,1)}, u32[]{:S(2)}) copy-start(bf16[2,32,128]{2,1,0:T(8,128)(2,1)} %constant.9.clone.z_half) | copy-start | bytes 49156
  27.4 4.8 %collective-permute-start.4 = (f32[27,16,256]{2,1,0:T(8,128)S(1)}, f32[27,16,256]{2,1,0:T(8,128)S(1)}, u32[]{:S(2)}, u32[]{:S(2)}) collective-permute-start(f32[27,16,256]{2,1,0:T(8,128)S(1)} %get-tuple-element.42.refs_5_), channel_id=1, source_target_pairs={{0,64},{64,0},{1,65},{65,1},{2,66},{66,2},{3,67},{67,3},{4,68},{68... | collective-permute-start | bytes 1327112 | tf_op jit(solution)/shard_map/ppermute | solution.py:920
  30.2 2.0 collective-permute-start.5
  30.5 34.7 %copy-start.4 = (bf16[2,256,256]{2,1,0:T(8,128)(2,1)S(1)}, bf16[2,256,256]{2,1,0:T(8,128)(2,1)}, u32[]{:S(2)}) copy-start(bf16[2,256,256]{2,1,0:T(8,128)(2,1)} %constant.27.clone.refs_4_.refs_3_.refs_7_) | copy-start | bytes 786436
  30.5 34.7 %copy-start.5 = (bf16[2,256,256]{2,1,0:T(8,128)(2,1)S(1)}, bf16[2,256,256]{2,1,0:T(8,128)(2,1)}, u32[]{:S(2)}) copy-start(bf16[2,256,256]{2,1,0:T(8,128)(2,1)} %constant.28.clone.refs_5_.refs_4_.refs_8_) | copy-start | bytes 786436
  30.5 34.7 %copy-start.20 = (s32[2,3]{1,0:T(2,128)S(1)}, s32[2,3]{1,0:T(2,128)}, u32[]{:S(2)}) copy-start(s32[2,3]{1,0:T(2,128)} %refs_0_.9) | copy-start | bytes 76
  36.9 7.1 %collective-permute-start.6 = (f32[256,128]{1,0:T(8,128)}, f32[256,128]{1,0:T(8,128)S(1)}, u32[]{:S(2)}, u32[]{:S(2)}) collective-permute-start(f32[256,128]{1,0:T(8,128)} %get-tuple-element.46), channel_id=1, source_target_pairs={{0,32},{32,0},{64,96},{96,64},{1,33},{33,1},{65,97},{97,65},{2,34}... | collective-permute-start | bytes 393224 | tf_op jit(solution)/shard_map/ppermute | solution.py:924
  40.2 3.8 %collective-permute-start.7 = (f32[256,128]{1,0:T(8,128)}, f32[256,128]{1,0:T(8,128)S(1)}, u32[]{:S(2)}, u32[]{:S(2)}) collective-permute-start(f32[256,128]{1,0:T(8,128)} %get-tuple-element.47), channel_id=1, source_target_pairs={{0,64},{32,96},{64,0},{96,32},{1,65},{33,97},{65,1},{97,33},{2,66}... | collective-permute-start | bytes 393224 | tf_op jit(solution)/shard_map/ppermute | solution.py:924
  40.8 6.6 %collective-permute-start.8 = (f32[256,128]{1,0:T(8,128)S(1)}, f32[256,128]{1,0:T(8,128)S(1)}, u32[]{:S(2)}, u32[]{:S(2)}) collective-permute-start(f32[256,128]{1,0:T(8,128)S(1)} %get-tuple-element.48), channel_id=1, source_target_pairs={{0,96},{32,64},{64,32},{96,0},{1,97},{33,65},{65,33},{97,1},{2,98}... | collective-permute-start | bytes 393224 | tf_op jit(solution)/shard_map/ppermute | solution.py:924
  48.8 16.4 %all-to-all-start = ((f32[32,8,128]{2,1,0:T(8,128)}), f32[32,8,128]{2,1,0:T(8,128)S(1)}, u32[]{:S(2)}, u32[]{:S(2)}) async-start(f32[32,8,128]{2,1,0:T(8,128)} %bitcast.4), calls=%async_computation | async-start | bytes 262144 | tf_op jit(solution)/shard_map/all_to_all | solution.py:975
  58.9 1.3 copy-start.24
  60.2 8.6 %copy-start.3 = (f32[4096,128]{1,0:T(8,128)}, f32[4096,128]{1,0:T(8,128)S(1)}, u32[]{:S(2)}) copy-start(f32[4096,128]{1,0:T(8,128)S(1)} %get-tuple-element.49.refs_6_.refs_1_) | copy-start | bytes 6291460
  68.9 0.6 copy-start.15
  69.5 0.6 copy-start.17
  70.1 0.7 copy-start.14
  70.8 11.2 %all-to-all-start.1 = ((f32[32,8,128]{2,1,0:T(8,128)}), f32[32,8,128]{2,1,0:T(8,128)S(1)}, u32[]{:S(2)}, u32[]{:S(2)}) async-start(f32[32,8,128]{2,1,0:T(8,128)} %bitcast.38), calls=%async_computation.1 | async-start | bytes 262144 | tf_op jit(solution)/shard_map/all_to_all | solution.py:975
  76.4 1.4 copy-start
  77.8 1.3 copy-start.7
  81.9 0.7 copy-start.26
  87.9 12.3 %all-to-all-start.2 = ((f32[32,8,128]{2,1,0:T(8,128)}), f32[32,8,128]{2,1,0:T(8,128)S(1)}, u32[]{:S(2)}, u32[]{:S(2)}) async-start(f32[32,8,128]{2,1,0:T(8,128)} %bitcast.49), calls=%async_computation.2 | async-start | bytes 262144 | tf_op jit(solution)/shard_map/all_to_all | solution.py:975
  104.3 11.3 %all-to-all-start.3 = ((f32[32,8,128]{2,1,0:T(8,128)}), f32[32,8,128]{2,1,0:T(8,128)S(1)}, u32[]{:S(2)}, u32[]{:S(2)}) async-start(f32[32,8,128]{2,1,0:T(8,128)} %bitcast.12), calls=%async_computation.3 | async-start | bytes 262144 | tf_op jit(solution)/shard_map/all_to_all | solution.py:975
  115.6 0.6 copy-start.27
  123.2 11.2 %all-to-all-start.4 = ((f32[32,8,128]{2,1,0:T(8,128)}), f32[32,8,128]{2,1,0:T(8,128)S(1)}, u32[]{:S(2)}, u32[]{:S(2)}) async-start(f32[32,8,128]{2,1,0:T(8,128)} %bitcast.48), calls=%async_computation.4 | async-start | bytes 262144 | tf_op jit(solution)/shard_map/all_to_all | solution.py:975
  127.0 1.6 copy-start.1
  128.6 1.6 copy-start.2
  134.3 9.0 %copy-start.8 = (f32[4096,128]{1,0:T(8,128)S(1)}, f32[4096,128]{1,0:T(8,128)}, u32[]{:S(2)}) copy-start(f32[4096,128]{1,0:T(8,128)} %copy-done.7) | copy-start | bytes 6291460
  138.6 12.0 %all-to-all-start.5 = ((f32[32,8,128]{2,1,0:T(8,128)}), f32[32,8,128]{2,1,0:T(8,128)S(1)}, u32[]{:S(2)}, u32[]{:S(2)}) async-start(f32[32,8,128]{2,1,0:T(8,128)} %bitcast.19), calls=%async_computation.5 | async-start | bytes 262144 | tf_op jit(solution)/shard_map/all_to_all | solution.py:975
  143.3 1.6 copy-start.9
  147.0 0.6 copy-start.11
  150.6 0.6 copy-start.25
  156.7 12.8 %all-to-all-start.6 = ((f32[32,16,128]{2,1,0:T(8,128)}), f32[32,16,128]{2,1,0:T(8,128)S(1)}, u32[]{:S(2)}, u32[]{:S(2)}) async-start(f32[32,16,128]{2,1,0:T(8,128)} %get-tuple-element.63), calls=%async_computation.6 | async-start | bytes 524288 | tf_op jit(solution)/shard_map/all_to_all | solution.py:975
  161.5 8.0 %copy-start.16 = (f32[128,128]{1,0:T(8,128)S(1)}, f32[128,128]{1,0:T(8,128)}, u32[]{:S(2)}) copy-start(f32[128,128]{1,0:T(8,128)} %copy-done.15) | copy-start | bytes 196612
  161.5 8.0 %copy-start.18 = (f32[128,128]{1,0:T(8,128)S(1)}, f32[128,128]{1,0:T(8,128)}, u32[]{:S(2)}) copy-start(f32[128,128]{1,0:T(8,128)} %copy-done.17) | copy-start | bytes 196612
  172.8 9.8 %collective-permute-start.9 = (f32[264,128]{1,0:T(8,128)S(1)}, f32[264,128]{1,0:T(8,128)S(1)}, u32[]{:S(2)}, u32[]{:S(2)}) collective-permute-start(f32[264,128]{1,0:T(8,128)S(1)} %modes_last.1.tail0), channel_id=1, source_target_pairs={{0,32},{32,0},{64,96},{96,64},{1,33},{33,1},{65,97},{97,65},{2,34}... | collective-permute-start | bytes 405512 | tf_op jit(solution)/shard_map/ppermute | solution.py:924
  175.4 7.8 %collective-permute-start.10 = (f32[264,128]{1,0:T(8,128)S(1)}, f32[264,128]{1,0:T(8,128)S(1)}, u32[]{:S(2)}, u32[]{:S(2)}) collective-permute-start(f32[264,128]{1,0:T(8,128)S(1)} %modes_last.1.tail0), channel_id=1, source_target_pairs={{0,64},{32,96},{64,0},{96,32},{1,65},{33,97},{65,1},{97,33},{2,66}... | collective-permute-start | bytes 405512 | tf_op jit(solution)/shard_map/ppermute | solution.py:924
  182.2 6.7 %collective-permute-start.11 = (f32[264,128]{1,0:T(8,128)S(1)}, f32[264,128]{1,0:T(8,128)S(1)}, u32[]{:S(2)}, u32[]{:S(2)}) collective-permute-start(f32[264,128]{1,0:T(8,128)S(1)} %modes_last.1.tail0), channel_id=1, source_target_pairs={{0,96},{32,64},{64,32},{96,0},{1,97},{33,65},{65,33},{97,1},{2,98}... | collective-permute-start | bytes 405512 | tf_op jit(solution)/shard_map/ppermute | solution.py:924
  189.6 11.4 %all-to-all-start.7 = ((f32[32,8,128]{2,1,0:T(8,128)}), f32[32,8,128]{2,1,0:T(8,128)S(1)}, u32[]{:S(2)}, u32[]{:S(2)}) async-start(f32[32,8,128]{2,1,0:T(8,128)} %spread.1), calls=%async_computation.7 | async-start | bytes 262144 | tf_op jit(solution)/shard_map/all_to_all | solution.py:975

commit v5 on v4

--- a/solution.py
+++ b/solution.py
@@ -21,8 +21,8 @@
 NT = (((1,), (1,)), ((), ()))
 TN = (((0,), (0,)), ((), ()))
 ROOM = 48 * 1024 * 1024
-LEAP_ROOM = 24 * 1024 * 1024
-CELL_ROOM = 62 * 1024 * 1024
+LEAP_ROOM = 40 * 1024 * 1024
+CELL_ROOM = 56 * 1024 * 1024
 MODE_ROOM = 48 * 1024 * 1024
 GROUP = ("role", "rep")
 EVERY = ("role", "rep", "tile")

time: 203 us -> 202 us (level)
  local copies, waits for them, and re-layouts: 25.5 us -> 23.3 us
    unnamed x62 -> x58, local copies, waits for them, and re-layouts: 15.2 us -> 12.9 us
where the time goes in v5:
time: 202 us; the launch traced here: 201 us
  starting transfers between devices  66.2 us (33%)
  waiting for transfers between devices  54.5 us (27%)
  Pallas kernels  51.1 us (25%)
  local copies, waits for them, and re-layouts  23.3 us (12%)
  matrix products  3.37 us (2%)
    pallas_call x11, Pallas kernels, call(): pl.pallas_call(run, out_shape=[o[0] for o in outs] + [jax.ShapeDtypeStruc...  40.8 us
    all_to_all x8, starting transfers between devices, swap(): return lax.all_to_all(value, 'tile', 0, 0, tiled=True)  37.9 us
    all_to_all x8, waiting for transfers between devices, swap(): return lax.all_to_all(value, 'tile', 0, 0, tiled=True)  35.2 us
    ppermute x7, starting transfers between devices, xor_group(): return lax.ppermute(value, GROUP, [(i, i ^ d) for i in range(4)])  19 us
    ppermute x7, waiting for transfers between devices, xor_group(): return lax.ppermute(value, GROUP, [(i, i ^ d) for i in range(4)])  13.8 us
    unnamed x58, local copies, waits for them, and re-layouts  12.9 us
    transpose x1, local copies, waits for them, and re-layouts, local(): turned = jnp.swapaxes(spectral_weight, -1, -2).reshape(LAYERS, 8, 1024, 64)  8.66 us
    ppermute x3, starting transfers between devices, across(): return lax.ppermute(value, axis, [(0, 1), (1, 0)])  5.1 us
  transfers between devices with their start and end apart: 20, of which 15 were waited for; matrix products, arithmetic and copies ran while one was open for 8% of the time, Pallas kernels for 5%

profile of v5, /device:TPU:1, one launch (start us, length us, event | category | flops | bytes accessed | tf_op | source)
XLA Modules:
  0.0 201.2 jit_solution(2127144821645300083)
XLA Ops:
  0.6 1.0 copy-done.10
  1.6 0.8 copy-done.12
  2.6 4.5 %collective-permute-start = (f32[16,256]{1,0:T(8,128)S(1)}, f32[16,256]{1,0:T(8,128)S(1)}, u32[]{:S(2)}, u32[]{:S(2)}) collective-permute-start(f32[16,256]{1,0:T(8,128)S(1)} %ends.1), channel_id=1, source_target_pairs={{0,32},{32,0},{64,96},{96,64},{1,33},{33,1},{65,97},{97,65},{2,34}... | collective-permute-start | bytes 49160 | tf_op jit(solution)/shard_map/ppermute | solution.py:924
  7.2 1.1 collective-permute-done.ends
  8.4 2.9 %collective-permute-start.2 = (f32[27,16,256]{2,1,0:T(8,128)S(1)}, f32[27,16,256]{2,1,0:T(8,128)S(1)}, u32[]{:S(2)}, u32[]{:S(2)}) collective-permute-start(f32[27,16,256]{2,1,0:T(8,128)S(1)} %get-tuple-element.40), channel_id=1, source_target_pairs={{0,1},{1,2},{2,3},{3,4},{4,5},{5,6},{6,7},{7,8},{8,9},{9,10},{10,1... | collective-permute-start | bytes 1327112 | tf_op jit(solution)/shard_map/ppermute | solution.py:916
  11.3 1.3 collective-permute-start.3
  12.6 2.2 %collective-permute-start.1 = (f32[29,16,256]{2,1,0:T(8,128)S(1)}, f32[29,16,256]{2,1,0:T(8,128)S(1)}, u32[]{:S(2)}, u32[]{:S(2)}) collective-permute-start(f32[29,16,256]{2,1,0:T(8,128)S(1)} %get-tuple-element.39.refs_3_), channel_id=1, source_target_pairs={{0,64},{64,0},{1,65},{65,1},{2,66},{66,2},{3,67},{67,3},{4,68},{68... | collective-permute-start | bytes 1425416 | tf_op jit(solution)/shard_map/ppermute | solution.py:920
  14.8 8.7 %copy.30 = f32[2,8,16,64,64]{4,3,2,1,0:T(8,128)} copy(f32[2,8,16,64,64]{3,4,2,1,0:T(8,128)} %bitcast.42) | data formatting | bytes 8388608 | tf_op jit(solution)/shard_map/transpose | solution.py:947
  23.5 3.9 %collective-permute-done.2.refs_1_ = f32[27,16,256]{2,1,0:T(8,128)S(1)} collective-permute-done((f32[27,16,256]{2,1,0:T(8,128)S(1)}, f32[27,16,256]{2,1,0:T(8,128)S(1)}, u32[]{:S(2)}, u32[]{:S(2)}) %collective-permute-start.2) | collective-permute-done | bytes 442400 | tf_op jit(solution)/shard_map/ppermute | solution.py:916
  27.4 2.8 %collective-permute-start.4 = (f32[27,16,256]{2,1,0:T(8,128)S(1)}, f32[27,16,256]{2,1,0:T(8,128)S(1)}, u32[]{:S(2)}, u32[]{:S(2)}) collective-permute-start(f32[27,16,256]{2,1,0:T(8,128)S(1)} %get-tuple-element.42.refs_5_), channel_id=1, source_target_pairs={{0,64},{64,0},{1,65},{65,1},{2,66},{66,2},{3,67},{67,3},{4,68},{68... | collective-permute-start | bytes 1327112 | tf_op jit(solution)/shard_map/ppermute | solution.py:920
  30.5 1.7 collective-permute-done.5.refs_8_
  32.2 4.5 %leapfrog.1 = (f32[6,4,16,256]{3,2,1,0:T(8,128)}, f32[256,128]{1,0:T(8,128)S(1)}, f32[256,128]{1,0:T(8,128)S(1)}, f32[256,128]{1,0:T(8,128)S(1)}, f32[256,128]{1,0:T(8,128)S(1)}) custom-call(s32[4]{0:T(128)S(1)} %copy-done.19, f32[4]{0:T(128)S(1)} %copy-done.20, f32[4]{0:T(128)S(1)} %copy-done.21, f32[29,16,256]{2,1,0:T(8,128)S(1)} %get-tuple-element.39.refs_3_, ...), custom_call_target="tpu_custom_call" | custom-call | tf_op jit(solution)/shard_map/leapfrog/pallas_call | solution.py:122
  36.7 3.3 %collective-permute-start.6 = (f32[256,128]{1,0:T(8,128)S(1)}, f32[256,128]{1,0:T(8,128)S(1)}, u32[]{:S(2)}, u32[]{:S(2)}) collective-permute-start(f32[256,128]{1,0:T(8,128)S(1)} %get-tuple-element.46), channel_id=1, source_target_pairs={{0,32},{32,0},{64,96},{96,64},{1,33},{33,1},{65,97},{97,65},{2,34}... | collective-permute-start | bytes 393224 | tf_op jit(solution)/shard_map/ppermute | solution.py:924
  40.0 0.7 collective-permute-start.7
  40.9 2.7 %collective-permute-done.6.piece1 = f32[256,128]{1,0:T(8,128)S(1)} collective-permute-done((f32[256,128]{1,0:T(8,128)S(1)}, f32[256,128]{1,0:T(8,128)S(1)}, u32[]{:S(2)}, u32[]{:S(2)}) %collective-permute-start.6) | collective-permute-done | bytes 131104 | tf_op jit(solution)/shard_map/ppermute | solution.py:924
  43.6 3.7 %collective-permute-done.8.piece3 = f32[256,128]{1,0:T(8,128)S(1)} collective-permute-done((f32[256,128]{1,0:T(8,128)S(1)}, f32[256,128]{1,0:T(8,128)S(1)}, u32[]{:S(2)}, u32[]{:S(2)}) %collective-permute-start.8) | collective-permute-done | bytes 131104 | tf_op jit(solution)/shard_map/ppermute | solution.py:924
  47.3 1.3 input_coefs.1
  48.6 8.8 %all-to-all-start = ((f32[32,8,128]{2,1,0:T(8,128)}), f32[32,8,128]{2,1,0:T(8,128)S(1)}, u32[]{:S(2)}, u32[]{:S(2)}) async-start(f32[32,8,128]{2,1,0:T(8,128)} %bitcast.4), calls=%async_computation | async-start | bytes 262144 | tf_op jit(solution)/shard_map/all_to_all | solution.py:975
  57.7 1.0 prepare_inputs.1
  58.8 1.3 copy-done.22
  60.1 5.0 %all-to-all-done = f32[32,8,128]{2,1,0:T(8,128)S(1)} async-done(((f32[32,8,128]{2,1,0:T(8,128)}), f32[32,8,128]{2,1,0:T(8,128)S(1)}, u32[]{:S(2)}, u32[]{:S(2)}) %all-to-all-start) | async-done | bytes 131104 | tf_op jit(solution)/shard_map/all_to_all | solution.py:975
  65.1 3.6 %modes_first.1 = (f32[256,128]{1,0:T(8,128)S(1)}, f32[128,128]{1,0:T(8,128)S(1)}, f32[128,128]{1,0:T(8,128)S(1)}) custom-call(s32[2,3]{1,0:T(2,128)S(1)} %copy-done.18, f32[256,128]{1,0:T(8,128)S(1)} %bitcast.35, f32[128,128]{1,0:T(8,128)S(1)} %fusion.refs_2_, f32[2,8,1024,64]{3,2,1,0:T(8,128)} %bitcast.40, bf16[2,256,256]{2,1,0:T(8,128)(2,1)S(1)} %copy-done.4, ...), custom_call_target="tpu_custom_call" | custom-call | tf_op jit(solution)/shard_map/modes_first/pallas_call | solution.py:122
  68.7 0.6 copy-done.14
  70.0 3.8 %all-to-all-start.1 = ((f32[32,8,128]{2,1,0:T(8,128)}), f32[32,8,128]{2,1,0:T(8,128)S(1)}, u32[]{:S(2)}, u32[]{:S(2)}) async-start(f32[32,8,128]{2,1,0:T(8,128)} %bitcast.38), calls=%async_computation.1 | async-start | bytes 262144 | tf_op jit(solution)/shard_map/all_to_all | solution.py:975
  73.8 0.8 slice_bitcast_fusion.1
  74.6 1.0 prepare_target.1
  75.7 1.4 copy-done
  77.0 1.4 copy-done.7
  78.4 2.8 %all-to-all-done.1 = f32[32,8,128]{2,1,0:T(8,128)S(1)} async-done(((f32[32,8,128]{2,1,0:T(8,128)}), f32[32,8,128]{2,1,0:T(8,128)S(1)}, u32[]{:S(2)}, u32[]{:S(2)}) %all-to-all-start.1) | async-done | bytes 131104 | tf_op jit(solution)/shard_map/all_to_all | solution.py:975
  81.1 0.7 copy-done.24
  81.8 5.3 %cells0.1 = (f32[256,128]{1,0:T(8,128)}, bf16[4096,256]{1,0:T(8,128)(2,1)}, f32[4096,128]{1,0:T(8,128)}) custom-call(f32[256,128]{1,0:T(8,128)} %bitcast.46, f32[4096,128]{1,0:T(8,128)} %copy-done.3, bf16[2,256,256]{2,1,0:T(8,128)(2,1)} %constant.26.clone.kron.refs_2_.refs_5_, bf16[2,256,256]{2,1,0:T(8,128)(2,1)} %constant.29.clone.refs_3_.refs_6_, ...), custom_call_target="tpu_custom_call" | custom-call | tf_op jit(solution)/shard_map/cells0/pallas_call | solution.py:122
  87.1 5.0 %all-to-all-start.2 = ((f32[32,8,128]{2,1,0:T(8,128)}), f32[32,8,128]{2,1,0:T(8,128)S(1)}, u32[]{:S(2)}, u32[]{:S(2)}) async-start(f32[32,8,128]{2,1,0:T(8,128)} %bitcast.49), calls=%async_computation.2 | async-start | bytes 262144 | tf_op jit(solution)/shard_map/all_to_all | solution.py:975
  92.3 7.1 %all-to-all-done.2 = f32[32,8,128]{2,1,0:T(8,128)S(1)} async-done(((f32[32,8,128]{2,1,0:T(8,128)}), f32[32,8,128]{2,1,0:T(8,128)S(1)}, u32[]{:S(2)}, u32[]{:S(2)}) %all-to-all-start.2) | async-done | bytes 131104 | tf_op jit(solution)/shard_map/all_to_all | solution.py:975
  99.4 4.1 %modes_forward.1 = (f32[256,128]{1,0:T(8,128)}, f32[128,128]{1,0:T(8,128)S(1)}) custom-call(s32[2,3]{1,0:T(2,128)S(1)} %copy-done.18, f32[256,128]{1,0:T(8,128)S(1)} %bitcast.37, f32[2,8,1024,64]{3,2,1,0:T(8,128)} %bitcast.41, bf16[2,256,256]{2,1,0:T(8,128)(2,1)S(1)} %copy-done.4, bf16[2,256,256]{2,1,0:T(8,128)(2,1)S(1)} %copy-done.5), custom_call_target="tpu_custom_call" | custom-call | tf_op jit(solution)/shard_map/modes_forward/pallas_call | solution.py:122
  103.5 4.0 %all-to-all-start.3 = ((f32[32,8,128]{2,1,0:T(8,128)}), f32[32,8,128]{2,1,0:T(8,128)S(1)}, u32[]{:S(2)}, u32[]{:S(2)}) async-start(f32[32,8,128]{2,1,0:T(8,128)} %bitcast.12), calls=%async_computation.3 | async-start | bytes 262144 | tf_op jit(solution)/shard_map/all_to_all | solution.py:975
  107.5 0.7 select_maximum_fusion.1
  108.2 0.7 copy.33.refs_3_
  108.9 0.7 select_maximum_fusion.refs_4_
  109.6 5.2 %all-to-all-done.3 = f32[32,8,128]{2,1,0:T(8,128)S(1)} async-done(((f32[32,8,128]{2,1,0:T(8,128)}), f32[32,8,128]{2,1,0:T(8,128)S(1)}, u32[]{:S(2)}, u32[]{:S(2)}) %all-to-all-start.3) | async-done | bytes 131104 | tf_op jit(solution)/shard_map/all_to_all | solution.py:975
  114.8 0.6 copy-done.25
  115.5 7.1 %cells1.1 = (f32[256,128]{1,0:T(8,128)}, bf16[4096,256]{1,0:T(8,128)(2,1)}, bf16[4096,256]{1,0:T(8,128)(2,1)}) custom-call(f32[256,128]{1,0:T(8,128)} %bitcast.47, bf16[4096,256]{1,0:T(8,128)(2,1)} %get-tuple-element.54.refs_1_, f32[4096,128]{1,0:T(8,128)} %copy-done, f32[128,128]{1,0:T(8,128)} %copy.33.refs_3_, f32[128,128]{1,0:T(8,128)} %select_maximum_fusion.refs_4_, ...), custom_call_target="tpu_custom_call" | custom-call | tf_op jit(solution)/shard_map/cells1/pallas_call | solution.py:122
  122.6 3.8 %all-to-all-start.4 = ((f32[32,8,128]{2,1,0:T(8,128)}), f32[32,8,128]{2,1,0:T(8,128)S(1)}, u32[]{:S(2)}, u32[]{:S(2)}) async-start(f32[32,8,128]{2,1,0:T(8,128)} %bitcast.48), calls=%async_computation.4 | async-start | bytes 262144 | tf_op jit(solution)/shard_map/all_to_all | solution.py:975
  126.4 1.6 copy-done.2
  128.0 1.1 point_grad.1.refs_6_.refs_3_
  129.1 4.6 %all-to-all-done.4 = f32[32,8,128]{2,1,0:T(8,128)S(1)} async-done(((f32[32,8,128]{2,1,0:T(8,128)}), f32[32,8,128]{2,1,0:T(8,128)S(1)}, u32[]{:S(2)}, u32[]{:S(2)}) %all-to-all-start.4) | async-done | bytes 131104 | tf_op jit(solution)/shard_map/all_to_all | solution.py:975
  133.7 4.3 %modes_backward.1 = (f32[256,128]{1,0:T(8,128)}, f32[128,128]{1,0:T(8,128)S(1)}) custom-call(s32[2,3]{1,0:T(2,128)S(1)} %copy-done.18, f32[256,128]{1,0:T(8,128)S(1)} %bitcast.36, f32[128,128]{1,0:T(8,128)S(1)} %get-tuple-element.56.refs_2_, f32[2,8,1024,64]{3,2,1,0:T(8,128)} %bitcast.43, bf16[2,256,256]{2,1,0:T(8,128)(2,1)S(1)} %copy-done.4, ...), custom_call_target="tpu_custom_call" | custom-call | tf_op jit(solution)/shard_map/modes_backward/pallas_call | solution.py:122
  138.0 3.9 %all-to-all-start.5 = ((f32[32,8,128]{2,1,0:T(8,128)}), f32[32,8,128]{2,1,0:T(8,128)S(1)}, u32[]{:S(2)}, u32[]{:S(2)}) async-start(f32[32,8,128]{2,1,0:T(8,128)} %bitcast.19), calls=%async_computation.5 | async-start | bytes 262144 | tf_op jit(solution)/shard_map/all_to_all | solution.py:975
  141.9 1.6 copy-done.9
  143.5 2.1 %proj_grad.1.refs_1_ = f32[32,8,128]{2,1,0:T(8,128)S(1)} custom-call(bf16[4096,256]{1,0:T(8,128)(2,1)S(1)} %copy-done.9, f32[4096,128]{1,0:T(8,128)S(1)} %copy-done.8, f32[128,128]{1,0:T(8,128)S(1)} %get-tuple-element.74.refs_2_, f32[32,128]{1,0:T(8,128)S(1)} %point_grad.1.refs_6_.refs_3_, f32[128,128]{1,0:T(8,128)S(1)} %get-tuple-element.61.refs_4_.refs_5_), custom_call_target="tpu_custom_call" | custom-call | tf_op jit(solution)/shard_map/proj_grad/pallas_call | solution.py:122
  146.2 3.0 %all-to-all-done.5 = f32[32,8,128]{2,1,0:T(8,128)S(1)} async-done(((f32[32,8,128]{2,1,0:T(8,128)}), f32[32,8,128]{2,1,0:T(8,128)S(1)}, u32[]{:S(2)}, u32[]{:S(2)}) %all-to-all-start.5) | async-done | bytes 131104 | tf_op jit(solution)/shard_map/all_to_all | solution.py:975
  149.2 0.6 copy-done.23
  149.8 5.4 %cells2.1 = (f32[32,16,128]{2,1,0:T(8,128)}, bf16[4096,256]{1,0:T(8,128)(2,1)}) custom-call(f32[256,128]{1,0:T(8,128)} %bitcast.45, f32[32,8,128]{2,1,0:T(8,128)} %copy-done.11, bf16[4096,256]{1,0:T(8,128)(2,1)} %get-tuple-element.57.refs_0_.refs_2_, f32[4096,128]{1,0:T(8,128)} %get-tuple-element.62.refs_3_, f32[128,128]{1,0:T(8,128)} %get-tuple-element.76.refs_4_, ...), custom_call_target="tpu_custom_call" | custom-call | tf_op jit(solution)/shard_map/cells2/pallas_call | solution.py:122
  155.3 4.8 %all-to-all-start.6 = ((f32[32,16,128]{2,1,0:T(8,128)}), f32[32,16,128]{2,1,0:T(8,128)S(1)}, u32[]{:S(2)}, u32[]{:S(2)}) async-start(f32[32,16,128]{2,1,0:T(8,128)} %get-tuple-element.63), calls=%async_computation.6 | async-start | bytes 524288 | tf_op jit(solution)/shard_map/all_to_all | solution.py:975
  160.0 3.0 %fusion.5.refs_4_ = f32[256,256]{1,0:T(8,128)S(1)} fusion(bf16[4096,256]{1,0:T(8,128)(2,1)} %copy-done.22, bf16[4096,256]{1,0:T(8,128)(2,1)} %get-tuple-element.67), kind=kOutput, calls=%fused_computation.21 | convolution fusion | flops 536870912 | bytes 4456448 | tf_op jit(solution)/shard_map/dot_general | solution.py:1042
  163.0 5.0 %all-to-all-done.6.refs_1_ = f32[32,16,128]{2,1,0:T(8,128)S(1)} async-done(((f32[32,16,128]{2,1,0:T(8,128)}), f32[32,16,128]{2,1,0:T(8,128)S(1)}, u32[]{:S(2)}, u32[]{:S(2)}) %all-to-all-start.6) | async-done | bytes 262176 | tf_op jit(solution)/shard_map/all_to_all | solution.py:975
  168.0 3.3 %modes_last.1.tail0 = f32[264,128]{1,0:T(8,128)S(1)} custom-call(s32[2,3]{1,0:T(2,128)S(1)} %copy-done.18, f32[32,16,128]{2,1,0:T(8,128)S(1)} %all-to-all-done.6.refs_1_, f32[128,128]{1,0:T(8,128)S(1)} %copy-done.16, f32[128,128]{1,0:T(8,128)S(1)} %get-tuple-element.65.refs_3_, f32[256,256]{1,0:T(8,128)S(1)} %fusion.5.refs_4_, ...), custom_call_target="tpu_custom_call" | custom-call | tf_op jit(solution)/shard_map/modes_last/pallas_call | solution.py:122
  171.3 2.4 %collective-permute-start.9 = (f32[264,128]{1,0:T(8,128)S(1)}, f32[264,128]{1,0:T(8,128)S(1)}, u32[]{:S(2)}, u32[]{:S(2)}) collective-permute-start(f32[264,128]{1,0:T(8,128)S(1)} %modes_last.1.tail0), channel_id=1, source_target_pairs={{0,32},{32,0},{64,96},{96,64},{1,33},{33,1},{65,97},{97,65},{2,34}... | collective-permute-start | bytes 405512 | tf_op jit(solution)/shard_map/ppermute | solution.py:924
  173.8 7.6 %collective-permute-start.10 = (f32[264,128]{1,0:T(8,128)S(1)}, f32[264,128]{1,0:T(8,128)S(1)}, u32[]{:S(2)}, u32[]{:S(2)}) collective-permute-start(f32[264,128]{1,0:T(8,128)S(1)} %modes_last.1.tail0), channel_id=1, source_target_pairs={{0,64},{32,96},{64,0},{96,32},{1,65},{33,97},{65,1},{97,33},{2,66}... | collective-permute-start | bytes 405512 | tf_op jit(solution)/shard_map/ppermute | solution.py:924
  182.3 5.7 %collective-permute-done.11.tail3 = f32[264,128]{1,0:T(8,128)S(1)} collective-permute-done((f32[264,128]{1,0:T(8,128)S(1)}, f32[264,128]{1,0:T(8,128)S(1)}, u32[]{:S(2)}, u32[]{:S(2)}) %collective-permute-start.11) | collective-permute-done | bytes 135200 | tf_op jit(solution)/shard_map/ppermute | solution.py:924
  188.1 0.7 spread.1
  188.7 3.8 %all-to-all-start.7 = ((f32[32,8,128]{2,1,0:T(8,128)}), f32[32,8,128]{2,1,0:T(8,128)S(1)}, u32[]{:S(2)}, u32[]{:S(2)}) async-start(f32[32,8,128]{2,1,0:T(8,128)} %spread.1), calls=%async_computation.7 | async-start | bytes 262144 | tf_op jit(solution)/shard_map/all_to_all | solution.py:975
  192.6 5.0 %outer.1 = f32[2,8,16,64,64]{4,3,2,1,0:T(8,128)} custom-call(f32[264,128]{1,0:T(8,128)S(1)} %modes_last.1.tail0, f32[264,128]{1,0:T(8,128)S(1)} %collective-permute-done.9.tail1, f32[264,128]{1,0:T(8,128)S(1)} %collective-permute-done.10.tail2, f32[264,128]{1,0:T(8,128)S(1)} %collective-permute-done.11.tail3), custom_call_target="tpu_custom_call" | custom-call | tf_op jit(solution)/shard_map/outer/pallas_call | solution.py:857
  197.6 2.6 %all-to-all-done.7.late = f32[32,8,128]{2,1,0:T(8,128)S(1)} async-done(((f32[32,8,128]{2,1,0:T(8,128)}), f32[32,8,128]{2,1,0:T(8,128)S(1)}, u32[]{:S(2)}, u32[]{:S(2)}) %all-to-all-start.7) | async-done | bytes 131104 | tf_op jit(solution)/shard_map/all_to_all | solution.py:975
  200.2 1.0 finish.1
  (70 shorter events, 3.5 us)
Async XLA Ops:
  0.6 1.0 copy-start.10
  1.6 0.8 copy-start.12
  2.6 5.6 %collective-permute-start = (f32[16,256]{1,0:T(8,128)S(1)}, f32[16,256]{1,0:T(8,128)S(1)}, u32[]{:S(2)}, u32[]{:S(2)}) collective-permute-start(f32[16,256]{1,0:T(8,128)S(1)} %ends.1), channel_id=1, source_target_pairs={{0,32},{32,0},{64,96},{96,64},{1,33},{33,1},{65,97},{97,65},{2,34}... | collective-permute-start | bytes 49160 | tf_op jit(solution)/shard_map/ppermute | solution.py:924
  8.4 19.0 %collective-permute-start.2 = (f32[27,16,256]{2,1,0:T(8,128)S(1)}, f32[27,16,256]{2,1,0:T(8,128)S(1)}, u32[]{:S(2)}, u32[]{:S(2)}) collective-permute-start(f32[27,16,256]{2,1,0:T(8,128)S(1)} %get-tuple-element.40), channel_id=1, source_target_pairs={{0,1},{1,2},{2,3},{3,4},{4,5},{5,6},{6,7},{7,8},{8,9},{9,10},{10,1... | collective-permute-start | bytes 1327112 | tf_op jit(solution)/shard_map/ppermute | solution.py:916
  11.3 12.2 %collective-permute-start.3 = (f32[24,16,256]{2,1,0:T(8,128)S(1)}, f32[24,16,256]{2,1,0:T(8,128)S(1)}, u32[]{:S(2)}, u32[]{:S(2)}) collective-permute-start(f32[24,16,256]{2,1,0:T(8,128)S(1)} %get-tuple-element.41), channel_id=1, source_target_pairs={{1,0},{2,1},{3,2},{4,3},{5,4},{6,5},{7,6},{8,7},{9,8},{10,9},{11,1... | collective-permute-start | bytes 1179656 | tf_op jit(solution)/shard_map/ppermute | solution.py:916
  12.6 17.9 %collective-permute-start.1 = (f32[29,16,256]{2,1,0:T(8,128)S(1)}, f32[29,16,256]{2,1,0:T(8,128)S(1)}, u32[]{:S(2)}, u32[]{:S(2)}) collective-permute-start(f32[29,16,256]{2,1,0:T(8,128)S(1)} %get-tuple-element.39.refs_3_), channel_id=1, source_target_pairs={{0,64},{64,0},{1,65},{65,1},{2,66},{66,2},{3,67},{67,3},{4,68},{68... | collective-permute-start | bytes 1425416 | tf_op jit(solution)/shard_map/ppermute | solution.py:920
  27.3 3.0 %copy-start.27 = (f32[6,64]{1,0:T(8,128)S(1)}, f32[6,64]{1,0:T(8,128)}, u32[]{:S(2)}) copy-start(f32[6,64]{1,0:T(8,128)} %param.27) | copy-start | bytes 4612
  27.3 3.0 %copy-start.26 = (f32[2,64,64]{2,1,0:T(8,128)S(1)}, f32[2,64,64]{2,1,0:T(8,128)}, u32[]{:S(2)}) copy-start(f32[2,64,64]{2,1,0:T(8,128)} %param.25) | copy-start | bytes 98308
  27.3 3.0 %copy-start.28 = (f32[64,6]{0,1:T(8,128)S(1)}, f32[64,6]{0,1:T(8,128)}, u32[]{:S(2)}) copy-start(f32[64,6]{0,1:T(8,128)} %param.24) | copy-start | bytes 4612
  27.3 4.9 %copy-start.13 = (f32[256,128]{1,0:T(8,128)S(1)}, f32[256,128]{1,0:T(8,128)}, u32[]{:S(2)}) copy-start(f32[256,128]{1,0:T(8,128)} %constant.12.clone.refs_9_) | copy-start | bytes 393220
  27.3 4.9 %copy-start.19 = (s32[4]{0:T(128)S(1)}, s32[4]{0:T(128)}, u32[]{:S(2)}) copy-start(s32[4]{0:T(128)} %refs_0_.5) | copy-start | bytes 52
  27.4 4.9 %copy-start.20 = (f32[4]{0:T(128)S(1)}, f32[4]{0:T(128)}, u32[]{:S(2)}) copy-start(f32[4]{0:T(128)} %refs_1_.1) | copy-start | bytes 52
  27.4 4.9 %copy-start.21 = (f32[4]{0:T(128)S(1)}, f32[4]{0:T(128)}, u32[]{:S(2)}) copy-start(f32[4]{0:T(128)} %refs_2_.2) | copy-start | bytes 52
  27.4 19.9 %copy-start.6 = (bf16[2,256,256]{2,1,0:T(8,128)(2,1)S(1)}, bf16[2,256,256]{2,1,0:T(8,128)(2,1)}, u32[]{:S(2)}) copy-start(bf16[2,256,256]{2,1,0:T(8,128)(2,1)} %constant.26.clone.kron.refs_2_.refs_5_) | copy-start | bytes 786436
  27.4 19.9 %copy-start.17 = (bf16[2,32,128]{2,1,0:T(8,128)(2,1)S(1)}, bf16[2,32,128]{2,1,0:T(8,128)(2,1)}, u32[]{:S(2)}) copy-start(bf16[2,32,128]{2,1,0:T(8,128)(2,1)} %constant.9.clone.z_half) | copy-start | bytes 49156
  27.4 4.8 %collective-permute-start.4 = (f32[27,16,256]{2,1,0:T(8,128)S(1)}, f32[27,16,256]{2,1,0:T(8,128)S(1)}, u32[]{:S(2)}, u32[]{:S(2)}) collective-permute-start(f32[27,16,256]{2,1,0:T(8,128)S(1)} %get-tuple-element.42.refs_5_), channel_id=1, source_target_pairs={{0,64},{64,0},{1,65},{65,1},{2,66},{66,2},{3,67},{67,3},{4,68},{68... | collective-permute-start | bytes 1327112 | tf_op jit(solution)/shard_map/ppermute | solution.py:920
  30.2 2.0 collective-permute-start.5
  30.5 34.6 %copy-start.4 = (bf16[2,256,256]{2,1,0:T(8,128)(2,1)S(1)}, bf16[2,256,256]{2,1,0:T(8,128)(2,1)}, u32[]{:S(2)}) copy-start(bf16[2,256,256]{2,1,0:T(8,128)(2,1)} %constant.27.clone.refs_4_.refs_3_.refs_7_) | copy-start | bytes 786436
  30.5 34.6 %copy-start.5 = (bf16[2,256,256]{2,1,0:T(8,128)(2,1)S(1)}, bf16[2,256,256]{2,1,0:T(8,128)(2,1)}, u32[]{:S(2)}) copy-start(bf16[2,256,256]{2,1,0:T(8,128)(2,1)} %constant.28.clone.refs_5_.refs_4_.refs_8_) | copy-start | bytes 786436
  30.5 34.5 %copy-start.18 = (s32[2,3]{1,0:T(2,128)S(1)}, s32[2,3]{1,0:T(2,128)}, u32[]{:S(2)}) copy-start(s32[2,3]{1,0:T(2,128)} %refs_0_.9) | copy-start | bytes 76
  36.7 6.9 %collective-permute-start.6 = (f32[256,128]{1,0:T(8,128)S(1)}, f32[256,128]{1,0:T(8,128)S(1)}, u32[]{:S(2)}, u32[]{:S(2)}) collective-permute-start(f32[256,128]{1,0:T(8,128)S(1)} %get-tuple-element.46), channel_id=1, source_target_pairs={{0,32},{32,0},{64,96},{96,64},{1,33},{33,1},{65,97},{97,65},{2,34}... | collective-permute-start | bytes 393224 | tf_op jit(solution)/shard_map/ppermute | solution.py:924
  40.0 3.6 %collective-permute-start.7 = (f32[256,128]{1,0:T(8,128)S(1)}, f32[256,128]{1,0:T(8,128)S(1)}, u32[]{:S(2)}, u32[]{:S(2)}) collective-permute-start(f32[256,128]{1,0:T(8,128)S(1)} %get-tuple-element.47), channel_id=1, source_target_pairs={{0,64},{32,96},{64,0},{96,32},{1,65},{33,97},{65,1},{97,33},{2,66}... | collective-permute-start | bytes 393224 | tf_op jit(solution)/shard_map/ppermute | solution.py:924
  40.7 6.6 %collective-permute-start.8 = (f32[256,128]{1,0:T(8,128)S(1)}, f32[256,128]{1,0:T(8,128)S(1)}, u32[]{:S(2)}, u32[]{:S(2)}) collective-permute-start(f32[256,128]{1,0:T(8,128)S(1)} %get-tuple-element.48), channel_id=1, source_target_pairs={{0,96},{32,64},{64,32},{96,0},{1,97},{33,65},{65,33},{97,1},{2,98}... | collective-permute-start | bytes 393224 | tf_op jit(solution)/shard_map/ppermute | solution.py:924
  48.6 16.4 %all-to-all-start = ((f32[32,8,128]{2,1,0:T(8,128)}), f32[32,8,128]{2,1,0:T(8,128)S(1)}, u32[]{:S(2)}, u32[]{:S(2)}) async-start(f32[32,8,128]{2,1,0:T(8,128)} %bitcast.4), calls=%async_computation | async-start | bytes 262144 | tf_op jit(solution)/shard_map/all_to_all | solution.py:975
  58.8 1.3 copy-start.22
  60.1 8.6 %copy-start.3 = (f32[4096,128]{1,0:T(8,128)}, f32[4096,128]{1,0:T(8,128)S(1)}, u32[]{:S(2)}) copy-start(f32[4096,128]{1,0:T(8,128)S(1)} %get-tuple-element.49.refs_6_.refs_1_) | copy-start | bytes 6291460
  68.7 0.6 copy-start.14
  69.4 0.6 copy-start.15
  70.0 11.2 %all-to-all-start.1 = ((f32[32,8,128]{2,1,0:T(8,128)}), f32[32,8,128]{2,1,0:T(8,128)S(1)}, u32[]{:S(2)}, u32[]{:S(2)}) async-start(f32[32,8,128]{2,1,0:T(8,128)} %bitcast.38), calls=%async_computation.1 | async-start | bytes 262144 | tf_op jit(solution)/shard_map/all_to_all | solution.py:975
  75.6 1.4 copy-start
  77.0 1.4 copy-start.7
  81.1 0.7 copy-start.24
  87.1 12.3 %all-to-all-start.2 = ((f32[32,8,128]{2,1,0:T(8,128)}), f32[32,8,128]{2,1,0:T(8,128)S(1)}, u32[]{:S(2)}, u32[]{:S(2)}) async-start(f32[32,8,128]{2,1,0:T(8,128)} %bitcast.49), calls=%async_computation.2 | async-start | bytes 262144 | tf_op jit(solution)/shard_map/all_to_all | solution.py:975
  103.5 11.3 %all-to-all-start.3 = ((f32[32,8,128]{2,1,0:T(8,128)}), f32[32,8,128]{2,1,0:T(8,128)S(1)}, u32[]{:S(2)}, u32[]{:S(2)}) async-start(f32[32,8,128]{2,1,0:T(8,128)} %bitcast.12), calls=%async_computation.3 | async-start | bytes 262144 | tf_op jit(solution)/shard_map/all_to_all | solution.py:975
  114.8 0.6 copy-start.25
  115.5 11.0 %copy-start.1 = (bf16[4096,256]{1,0:T(8,128)(2,1)S(1)}, bf16[4096,256]{1,0:T(8,128)(2,1)}, u32[]{:S(2)}) copy-start(bf16[4096,256]{1,0:T(8,128)(2,1)} %get-tuple-element.54.refs_1_) | copy-start | bytes 6291460
  122.6 11.2 %all-to-all-start.4 = ((f32[32,8,128]{2,1,0:T(8,128)}), f32[32,8,128]{2,1,0:T(8,128)S(1)}, u32[]{:S(2)}, u32[]{:S(2)}) async-start(f32[32,8,128]{2,1,0:T(8,128)} %bitcast.48), calls=%async_computation.4 | async-start | bytes 262144 | tf_op jit(solution)/shard_map/all_to_all | solution.py:975
  126.4 1.6 copy-start.2
  133.7 8.2 %copy-start.8 = (f32[4096,128]{1,0:T(8,128)S(1)}, f32[4096,128]{1,0:T(8,128)}, u32[]{:S(2)}) copy-start(f32[4096,128]{1,0:T(8,128)} %copy-done.7) | copy-start | bytes 6291460
  138.0 11.2 %all-to-all-start.5 = ((f32[32,8,128]{2,1,0:T(8,128)}), f32[32,8,128]{2,1,0:T(8,128)S(1)}, u32[]{:S(2)}, u32[]{:S(2)}) async-start(f32[32,8,128]{2,1,0:T(8,128)} %bitcast.19), calls=%async_computation.5 | async-start | bytes 262144 | tf_op jit(solution)/shard_map/all_to_all | solution.py:975
  141.9 1.6 copy-start.9
  145.6 0.6 copy-start.11
  149.2 0.6 copy-start.23
  155.3 12.8 %all-to-all-start.6 = ((f32[32,16,128]{2,1,0:T(8,128)}), f32[32,16,128]{2,1,0:T(8,128)S(1)}, u32[]{:S(2)}, u32[]{:S(2)}) async-start(f32[32,16,128]{2,1,0:T(8,128)} %get-tuple-element.63), calls=%async_computation.6 | async-start | bytes 524288 | tf_op jit(solution)/shard_map/all_to_all | solution.py:975
  160.0 8.0 %copy-start.16 = (f32[128,128]{1,0:T(8,128)S(1)}, f32[128,128]{1,0:T(8,128)}, u32[]{:S(2)}) copy-start(f32[128,128]{1,0:T(8,128)} %copy-done.15) | copy-start | bytes 196612
  171.3 10.5 %collective-permute-start.9 = (f32[264,128]{1,0:T(8,128)S(1)}, f32[264,128]{1,0:T(8,128)S(1)}, u32[]{:S(2)}, u32[]{:S(2)}) collective-permute-start(f32[264,128]{1,0:T(8,128)S(1)} %modes_last.1.tail0), channel_id=1, source_target_pairs={{0,32},{32,0},{64,96},{96,64},{1,33},{33,1},{65,97},{97,65},{2,34}... | collective-permute-start | bytes 405512 | tf_op jit(solution)/shard_map/ppermute | solution.py:924
  173.8 8.6 %collective-permute-start.10 = (f32[264,128]{1,0:T(8,128)S(1)}, f32[264,128]{1,0:T(8,128)S(1)}, u32[]{:S(2)}, u32[]{:S(2)}) collective-permute-start(f32[264,128]{1,0:T(8,128)S(1)} %modes_last.1.tail0), channel_id=1, source_target_pairs={{0,64},{32,96},{64,0},{96,32},{1,65},{33,97},{65,1},{97,33},{2,66}... | collective-permute-start | bytes 405512 | tf_op jit(solution)/shard_map/ppermute | solution.py:924
  181.4 6.7 %collective-permute-start.11 = (f32[264,128]{1,0:T(8,128)S(1)}, f32[264,128]{1,0:T(8,128)S(1)}, u32[]{:S(2)}, u32[]{:S(2)}) collective-permute-start(f32[264,128]{1,0:T(8,128)S(1)} %modes_last.1.tail0), channel_id=1, source_target_pairs={{0,96},{32,64},{64,32},{96,0},{1,97},{33,65},{65,33},{97,1},{2,98}... | collective-permute-start | bytes 405512 | tf_op jit(solution)/shard_map/ppermute | solution.py:924
  188.7 11.5 %all-to-all-start.7 = ((f32[32,8,128]{2,1,0:T(8,128)}), f32[32,8,128]{2,1,0:T(8,128)S(1)}, u32[]{:S(2)}, u32[]{:S(2)}) async-start(f32[32,8,128]{2,1,0:T(8,128)} %spread.1), calls=%async_computation.7 | async-start | bytes 262144 | tf_op jit(solution)/shard_map/all_to_all | solution.py:975

commit v6 on v5

--- a/solution.py
+++ b/solution.py
@@ -730,7 +730,7 @@
     out[...] = dot3((kron_t[0], kron_t[1]), halves(blocks))
 
 
-def modes_first_kernel(counts, coef, lift, weights, kron, kron_t, out, out_in, out_a, a_scr, b_scr):
+def modes_first_kernel(counts, coef, lift, weights, kron, kron_t, out, out_a, a_scr, b_scr):
     step = pl.program_id(0)
 
     @pl.when(step == 0)
@@ -738,10 +738,9 @@
         rows = dot3((kron[0], kron[1]), halves(coef[...]))
         picked = jnp.where(lanes_of((128, 128)) < 8, rows[0:128], rows[128:256])
         picked = picked * kept_modes(counts, 0)
-        out_in[...] = picked
         lifted = dot3(halves(picked), halves(lift[...]))
         a_scr[...] = lifted
-        out_a[...] = lifted
+        out_a[...] = jnp.where(lanes_of((128, 128)) < 64, picked, lifted)
 
     mix(a_scr, b_scr, weights, step)
 
@@ -792,7 +791,7 @@
 
 
 def modes_last_kernel(
-    counts, coef, saved, inputs, point, pair1, weights, kron, kron_t, out, g_scr, b_scr
+    counts, coef, saved, point, pair1, weights, kron, kron_t, out, g_scr, b_scr
 ):
     step = pl.program_id(0)
 
@@ -807,7 +806,7 @@
 
     @pl.when(step == pl.num_programs(0) - 1)
     def _():
-        turned = jnp.transpose(inputs[...])[0:16]
+        turned = jnp.transpose(saved[...])[0:16]
         lift = dot3(halves(turned), halves(b_scr[...]))
         lift = lift[0:8] + lift[8:16]
         direct = fold(point[0:16, :] + point[128:144, :])
@@ -978,14 +977,14 @@
         return swap(value).reshape(256, 128)
 
     inputs, pre0 = prepare(pieces, 0, first, True, "prepare_inputs")
-    spectrum, a_in, a0 = mode_call(
+    spectrum, a0 = mode_call(
         modes_first_kernel,
         "modes_first",
         0,
         mode_counts,
         (swap_flat(coef), lift_pad),
         turned,
-        ((256, 128), (128, 128), (128, 128)),
+        ((256, 128), (128, 128)),
         after=(pre0,),
     )
     target, pull = prepare(pieces, 128, proj_t * scale, False, "prepare_target")
@@ -1045,7 +1044,7 @@
         "modes_last",
         0,
         mode_counts,
-        (swap(coef), a0, a_in, direct, pair1),
+        (swap(coef), a0, direct, pair1),
         plain,
         ((264, 128),),
     )

time: 202 us -> 202 us (level)
    unnamed x58 -> x54, local copies, waits for them, and re-layouts: 12.9 us -> 12.4 us
where the time goes in v6:
time: 202 us; the launch traced here: 200 us
  starting transfers between devices  66.2 us (33%)
  waiting for transfers between devices  54.4 us (27%)
  Pallas kernels  51.1 us (25%)
  local copies, waits for them, and re-layouts  22.7 us (11%)
  matrix products  3.33 us (2%)
    pallas_call x11, Pallas kernels, call(): pl.pallas_call(run, out_shape=[o[0] for o in outs] + [jax.ShapeDtypeStruc...  40.8 us
    all_to_all x8, starting transfers between devices, swap(): return lax.all_to_all(value, 'tile', 0, 0, tiled=True)  37.9 us
    all_to_all x8, waiting for transfers between devices, swap(): return lax.all_to_all(value, 'tile', 0, 0, tiled=True)  35.1 us
    ppermute x7, starting transfers between devices, xor_group(): return lax.ppermute(value, GROUP, [(i, i ^ d) for i in range(4)])  19 us
    ppermute x7, waiting for transfers between devices, xor_group(): return lax.ppermute(value, GROUP, [(i, i ^ d) for i in range(4)])  13.8 us
    unnamed x54, local copies, waits for them, and re-layouts  12.4 us
    transpose x1, local copies, waits for them, and re-layouts, local(): turned = jnp.swapaxes(spectral_weight, -1, -2).reshape(LAYERS, 8, 1024, 64)  8.66 us
    ppermute x3, starting transfers between devices, across(): return lax.ppermute(value, axis, [(0, 1), (1, 0)])  5.1 us
  transfers between devices with their start and end apart: 20, of which 15 were waited for; matrix products, arithmetic and copies ran while one was open for 8% of the time, Pallas kernels for 5%

profile of v6, /device:TPU:1, one launch (start us, length us, event | category | flops | bytes accessed | tf_op | source)
XLA Modules:
  0.0 200.5 jit_solution(3103960097248961359)
XLA Ops:
  0.6 1.0 copy-done.10
  1.6 0.8 copy-done.12
  2.6 4.5 %collective-permute-start = (f32[16,256]{1,0:T(8,128)S(1)}, f32[16,256]{1,0:T(8,128)S(1)}, u32[]{:S(2)}, u32[]{:S(2)}) collective-permute-start(f32[16,256]{1,0:T(8,128)S(1)} %ends.1), channel_id=1, source_target_pairs={{0,32},{32,0},{64,96},{96,64},{1,33},{33,1},{65,97},{97,65},{2,34}... | collective-permute-start | bytes 49160 | tf_op jit(solution)/shard_map/ppermute | solution.py:923
  7.2 1.1 collective-permute-done.ends
  8.4 2.9 %collective-permute-start.2 = (f32[27,16,256]{2,1,0:T(8,128)S(1)}, f32[27,16,256]{2,1,0:T(8,128)S(1)}, u32[]{:S(2)}, u32[]{:S(2)}) collective-permute-start(f32[27,16,256]{2,1,0:T(8,128)S(1)} %get-tuple-element.39), channel_id=1, source_target_pairs={{0,1},{1,2},{2,3},{3,4},{4,5},{5,6},{6,7},{7,8},{8,9},{9,10},{10,1... | collective-permute-start | bytes 1327112 | tf_op jit(solution)/shard_map/ppermute | solution.py:915
  11.3 1.3 collective-permute-start.3
  12.6 2.2 %collective-permute-start.1 = (f32[29,16,256]{2,1,0:T(8,128)S(1)}, f32[29,16,256]{2,1,0:T(8,128)S(1)}, u32[]{:S(2)}, u32[]{:S(2)}) collective-permute-start(f32[29,16,256]{2,1,0:T(8,128)S(1)} %get-tuple-element.38.refs_3_), channel_id=1, source_target_pairs={{0,64},{64,0},{1,65},{65,1},{2,66},{66,2},{3,67},{67,3},{4,68},{68... | collective-permute-start | bytes 1425416 | tf_op jit(solution)/shard_map/ppermute | solution.py:919
  14.8 8.7 %copy.30 = f32[2,8,16,64,64]{4,3,2,1,0:T(8,128)} copy(f32[2,8,16,64,64]{3,4,2,1,0:T(8,128)} %bitcast.42) | data formatting | bytes 8388608 | tf_op jit(solution)/shard_map/transpose | solution.py:946
  23.5 3.9 %collective-permute-done.2.refs_1_ = f32[27,16,256]{2,1,0:T(8,128)S(1)} collective-permute-done((f32[27,16,256]{2,1,0:T(8,128)S(1)}, f32[27,16,256]{2,1,0:T(8,128)S(1)}, u32[]{:S(2)}, u32[]{:S(2)}) %collective-permute-start.2) | collective-permute-done | bytes 442400 | tf_op jit(solution)/shard_map/ppermute | solution.py:915
  27.4 2.8 %collective-permute-start.4 = (f32[27,16,256]{2,1,0:T(8,128)S(1)}, f32[27,16,256]{2,1,0:T(8,128)S(1)}, u32[]{:S(2)}, u32[]{:S(2)}) collective-permute-start(f32[27,16,256]{2,1,0:T(8,128)S(1)} %get-tuple-element.41.refs_5_), channel_id=1, source_target_pairs={{0,64},{64,0},{1,65},{65,1},{2,66},{66,2},{3,67},{67,3},{4,68},{68... | collective-permute-start | bytes 1327112 | tf_op jit(solution)/shard_map/ppermute | solution.py:919
  30.5 1.7 collective-permute-done.5.refs_8_
  32.2 4.5 %leapfrog.1 = (f32[6,4,16,256]{3,2,1,0:T(8,128)}, f32[256,128]{1,0:T(8,128)S(1)}, f32[256,128]{1,0:T(8,128)S(1)}, f32[256,128]{1,0:T(8,128)S(1)}, f32[256,128]{1,0:T(8,128)S(1)}) custom-call(s32[4]{0:T(128)S(1)} %copy-done.17, f32[4]{0:T(128)S(1)} %copy-done.18, f32[4]{0:T(128)S(1)} %copy-done.19, f32[29,16,256]{2,1,0:T(8,128)S(1)} %get-tuple-element.38.refs_3_, ...), custom_call_target="tpu_custom_call" | custom-call | tf_op jit(solution)/shard_map/leapfrog/pallas_call | solution.py:122
  36.7 3.3 %collective-permute-start.6 = (f32[256,128]{1,0:T(8,128)S(1)}, f32[256,128]{1,0:T(8,128)S(1)}, u32[]{:S(2)}, u32[]{:S(2)}) collective-permute-start(f32[256,128]{1,0:T(8,128)S(1)} %get-tuple-element.45), channel_id=1, source_target_pairs={{0,32},{32,0},{64,96},{96,64},{1,33},{33,1},{65,97},{97,65},{2,34}... | collective-permute-start | bytes 393224 | tf_op jit(solution)/shard_map/ppermute | solution.py:923
  40.0 0.7 collective-permute-start.7
  40.9 2.7 %collective-permute-done.6.piece1 = f32[256,128]{1,0:T(8,128)S(1)} collective-permute-done((f32[256,128]{1,0:T(8,128)S(1)}, f32[256,128]{1,0:T(8,128)S(1)}, u32[]{:S(2)}, u32[]{:S(2)}) %collective-permute-start.6) | collective-permute-done | bytes 131104 | tf_op jit(solution)/shard_map/ppermute | solution.py:923
  43.6 3.7 %collective-permute-done.8.piece3 = f32[256,128]{1,0:T(8,128)S(1)} collective-permute-done((f32[256,128]{1,0:T(8,128)S(1)}, f32[256,128]{1,0:T(8,128)S(1)}, u32[]{:S(2)}, u32[]{:S(2)}) %collective-permute-start.8) | collective-permute-done | bytes 131104 | tf_op jit(solution)/shard_map/ppermute | solution.py:923
  47.3 1.3 input_coefs.1
  48.6 8.8 %all-to-all-start = ((f32[32,8,128]{2,1,0:T(8,128)}), f32[32,8,128]{2,1,0:T(8,128)S(1)}, u32[]{:S(2)}, u32[]{:S(2)}) async-start(f32[32,8,128]{2,1,0:T(8,128)} %bitcast.4), calls=%async_computation | async-start | bytes 262144 | tf_op jit(solution)/shard_map/all_to_all | solution.py:974
  57.7 1.0 prepare_inputs.1
  58.8 1.3 copy-done.20
  60.1 4.9 %all-to-all-done = f32[32,8,128]{2,1,0:T(8,128)S(1)} async-done(((f32[32,8,128]{2,1,0:T(8,128)}), f32[32,8,128]{2,1,0:T(8,128)S(1)}, u32[]{:S(2)}, u32[]{:S(2)}) %all-to-all-start) | async-done | bytes 131104 | tf_op jit(solution)/shard_map/all_to_all | solution.py:974
  65.1 3.6 %modes_first.1 = (f32[256,128]{1,0:T(8,128)S(1)}, f32[128,128]{1,0:T(8,128)S(1)}) custom-call(s32[2,3]{1,0:T(2,128)S(1)} %copy-done.16, f32[256,128]{1,0:T(8,128)S(1)} %bitcast.35, f32[128,128]{1,0:T(8,128)S(1)} %fusion.refs_2_, f32[2,8,1024,64]{3,2,1,0:T(8,128)} %bitcast.40, bf16[2,256,256]{2,1,0:T(8,128)(2,1)S(1)} %copy-done.4, ...), custom_call_target="tpu_custom_call" | custom-call | tf_op jit(solution)/shard_map/modes_first/pallas_call | solution.py:122
  68.7 0.6 copy-done.14
  69.4 3.9 %all-to-all-start.1 = ((f32[32,8,128]{2,1,0:T(8,128)}), f32[32,8,128]{2,1,0:T(8,128)S(1)}, u32[]{:S(2)}, u32[]{:S(2)}) async-start(f32[32,8,128]{2,1,0:T(8,128)} %bitcast.38), calls=%async_computation.1 | async-start | bytes 262144 | tf_op jit(solution)/shard_map/all_to_all | solution.py:974
  73.2 0.8 slice_bitcast_fusion.1
  74.0 1.0 prepare_target.1
  75.1 1.4 copy-done
  76.4 1.4 copy-done.7
  77.8 2.8 %all-to-all-done.1 = f32[32,8,128]{2,1,0:T(8,128)S(1)} async-done(((f32[32,8,128]{2,1,0:T(8,128)}), f32[32,8,128]{2,1,0:T(8,128)S(1)}, u32[]{:S(2)}, u32[]{:S(2)}) %all-to-all-start.1) | async-done | bytes 131104 | tf_op jit(solution)/shard_map/all_to_all | solution.py:974
  80.6 0.6 copy-done.22
  81.2 5.3 %cells0.1 = (f32[256,128]{1,0:T(8,128)}, bf16[4096,256]{1,0:T(8,128)(2,1)}, f32[4096,128]{1,0:T(8,128)}) custom-call(f32[256,128]{1,0:T(8,128)} %bitcast.46, f32[4096,128]{1,0:T(8,128)} %copy-done.3, bf16[2,256,256]{2,1,0:T(8,128)(2,1)} %constant.26.clone.kron.refs_2_.refs_5_, bf16[2,256,256]{2,1,0:T(8,128)(2,1)} %constant.29.clone.refs_3_.refs_6_, ...), custom_call_target="tpu_custom_call" | custom-call | tf_op jit(solution)/shard_map/cells0/pallas_call | solution.py:122
  86.5 5.0 %all-to-all-start.2 = ((f32[32,8,128]{2,1,0:T(8,128)}), f32[32,8,128]{2,1,0:T(8,128)S(1)}, u32[]{:S(2)}, u32[]{:S(2)}) async-start(f32[32,8,128]{2,1,0:T(8,128)} %bitcast.49), calls=%async_computation.2 | async-start | bytes 262144 | tf_op jit(solution)/shard_map/all_to_all | solution.py:974
  91.7 7.1 %all-to-all-done.2 = f32[32,8,128]{2,1,0:T(8,128)S(1)} async-done(((f32[32,8,128]{2,1,0:T(8,128)}), f32[32,8,128]{2,1,0:T(8,128)S(1)}, u32[]{:S(2)}, u32[]{:S(2)}) %all-to-all-start.2) | async-done | bytes 131104 | tf_op jit(solution)/shard_map/all_to_all | solution.py:974
  98.8 4.1 %modes_forward.1 = (f32[256,128]{1,0:T(8,128)}, f32[128,128]{1,0:T(8,128)S(1)}) custom-call(s32[2,3]{1,0:T(2,128)S(1)} %copy-done.16, f32[256,128]{1,0:T(8,128)S(1)} %bitcast.37, f32[2,8,1024,64]{3,2,1,0:T(8,128)} %bitcast.41, bf16[2,256,256]{2,1,0:T(8,128)(2,1)S(1)} %copy-done.4, bf16[2,256,256]{2,1,0:T(8,128)(2,1)S(1)} %copy-done.5), custom_call_target="tpu_custom_call" | custom-call | tf_op jit(solution)/shard_map/modes_forward/pallas_call | solution.py:122
  102.9 4.0 %all-to-all-start.3 = ((f32[32,8,128]{2,1,0:T(8,128)}), f32[32,8,128]{2,1,0:T(8,128)S(1)}, u32[]{:S(2)}, u32[]{:S(2)}) async-start(f32[32,8,128]{2,1,0:T(8,128)} %bitcast.12), calls=%async_computation.3 | async-start | bytes 262144 | tf_op jit(solution)/shard_map/all_to_all | solution.py:974
  106.9 0.7 select_maximum_fusion.1
  107.6 0.7 copy.33.refs_3_
  108.3 0.7 select_maximum_fusion.refs_4_
  109.0 5.2 %all-to-all-done.3 = f32[32,8,128]{2,1,0:T(8,128)S(1)} async-done(((f32[32,8,128]{2,1,0:T(8,128)}), f32[32,8,128]{2,1,0:T(8,128)S(1)}, u32[]{:S(2)}, u32[]{:S(2)}) %all-to-all-start.3) | async-done | bytes 131104 | tf_op jit(solution)/shard_map/all_to_all | solution.py:974
  114.2 0.6 copy-done.23
  114.8 7.1 %cells1.1 = (f32[256,128]{1,0:T(8,128)}, bf16[4096,256]{1,0:T(8,128)(2,1)}, bf16[4096,256]{1,0:T(8,128)(2,1)}) custom-call(f32[256,128]{1,0:T(8,128)} %bitcast.47, bf16[4096,256]{1,0:T(8,128)(2,1)} %get-tuple-element.53.refs_1_, f32[4096,128]{1,0:T(8,128)} %copy-done, f32[128,128]{1,0:T(8,128)} %copy.33.refs_3_, f32[128,128]{1,0:T(8,128)} %select_maximum_fusion.refs_4_, ...), custom_call_target="tpu_custom_call" | custom-call | tf_op jit(solution)/shard_map/cells1/pallas_call | solution.py:122
  121.9 3.9 %all-to-all-start.4 = ((f32[32,8,128]{2,1,0:T(8,128)}), f32[32,8,128]{2,1,0:T(8,128)S(1)}, u32[]{:S(2)}, u32[]{:S(2)}) async-start(f32[32,8,128]{2,1,0:T(8,128)} %bitcast.48), calls=%async_computation.4 | async-start | bytes 262144 | tf_op jit(solution)/shard_map/all_to_all | solution.py:974
  125.8 1.6 copy-done.2
  127.4 1.1 point_grad.1.refs_6_.refs_3_
  128.5 4.6 %all-to-all-done.4 = f32[32,8,128]{2,1,0:T(8,128)S(1)} async-done(((f32[32,8,128]{2,1,0:T(8,128)}), f32[32,8,128]{2,1,0:T(8,128)S(1)}, u32[]{:S(2)}, u32[]{:S(2)}) %all-to-all-start.4) | async-done | bytes 131104 | tf_op jit(solution)/shard_map/all_to_all | solution.py:974
  133.1 4.3 %modes_backward.1 = (f32[256,128]{1,0:T(8,128)}, f32[128,128]{1,0:T(8,128)S(1)}) custom-call(s32[2,3]{1,0:T(2,128)S(1)} %copy-done.16, f32[256,128]{1,0:T(8,128)S(1)} %bitcast.36, f32[128,128]{1,0:T(8,128)S(1)} %get-tuple-element.55.refs_2_, f32[2,8,1024,64]{3,2,1,0:T(8,128)} %bitcast.43, bf16[2,256,256]{2,1,0:T(8,128)(2,1)S(1)} %copy-done.4, ...), custom_call_target="tpu_custom_call" | custom-call | tf_op jit(solution)/shard_map/modes_backward/pallas_call | solution.py:122
  137.4 3.9 %all-to-all-start.5 = ((f32[32,8,128]{2,1,0:T(8,128)}), f32[32,8,128]{2,1,0:T(8,128)S(1)}, u32[]{:S(2)}, u32[]{:S(2)}) async-start(f32[32,8,128]{2,1,0:T(8,128)} %bitcast.19), calls=%async_computation.5 | async-start | bytes 262144 | tf_op jit(solution)/shard_map/all_to_all | solution.py:974
  141.3 1.6 copy-done.9
  142.8 2.1 %proj_grad.1.refs_1_ = f32[32,8,128]{2,1,0:T(8,128)S(1)} custom-call(bf16[4096,256]{1,0:T(8,128)(2,1)S(1)} %copy-done.9, f32[4096,128]{1,0:T(8,128)S(1)} %copy-done.8, f32[128,128]{1,0:T(8,128)S(1)} %get-tuple-element.72.refs_2_, f32[32,128]{1,0:T(8,128)S(1)} %point_grad.1.refs_6_.refs_3_, f32[128,128]{1,0:T(8,128)S(1)} %get-tuple-element.60.refs_4_), custom_call_target="tpu_custom_call" | custom-call | tf_op jit(solution)/shard_map/proj_grad/pallas_call | solution.py:122
  145.6 3.0 %all-to-all-done.5 = f32[32,8,128]{2,1,0:T(8,128)S(1)} async-done(((f32[32,8,128]{2,1,0:T(8,128)}), f32[32,8,128]{2,1,0:T(8,128)S(1)}, u32[]{:S(2)}, u32[]{:S(2)}) %all-to-all-start.5) | async-done | bytes 131104 | tf_op jit(solution)/shard_map/all_to_all | solution.py:974
  148.6 0.6 copy-done.21
  149.2 5.5 %cells2.1 = (f32[32,16,128]{2,1,0:T(8,128)}, bf16[4096,256]{1,0:T(8,128)(2,1)}) custom-call(f32[256,128]{1,0:T(8,128)} %bitcast.45, f32[32,8,128]{2,1,0:T(8,128)} %copy-done.11, bf16[4096,256]{1,0:T(8,128)(2,1)} %get-tuple-element.56.refs_0_.refs_2_, f32[4096,128]{1,0:T(8,128)} %get-tuple-element.61.refs_3_, f32[128,128]{1,0:T(8,128)} %get-tuple-element.74.refs_4_, ...), custom_call_target="tpu_custom_call" | custom-call | tf_op jit(solution)/shard_map/cells2/pallas_call | solution.py:122
  154.6 4.8 %all-to-all-start.6 = ((f32[32,16,128]{2,1,0:T(8,128)}), f32[32,16,128]{2,1,0:T(8,128)S(1)}, u32[]{:S(2)}, u32[]{:S(2)}) async-start(f32[32,16,128]{2,1,0:T(8,128)} %get-tuple-element.62), calls=%async_computation.6 | async-start | bytes 524288 | tf_op jit(solution)/shard_map/all_to_all | solution.py:974
  159.4 3.0 %fusion.5.refs_3_ = f32[256,256]{1,0:T(8,128)S(1)} fusion(bf16[4096,256]{1,0:T(8,128)(2,1)} %copy-done.20, bf16[4096,256]{1,0:T(8,128)(2,1)} %get-tuple-element.65), kind=kOutput, calls=%fused_computation.21 | convolution fusion | flops 536870912 | bytes 4456448 | tf_op jit(solution)/shard_map/dot_general | solution.py:1041
  162.4 5.0 %all-to-all-done.6.refs_1_ = f32[32,16,128]{2,1,0:T(8,128)S(1)} async-done(((f32[32,16,128]{2,1,0:T(8,128)}), f32[32,16,128]{2,1,0:T(8,128)S(1)}, u32[]{:S(2)}, u32[]{:S(2)}) %all-to-all-start.6) | async-done | bytes 262176 | tf_op jit(solution)/shard_map/all_to_all | solution.py:974
  167.4 3.3 %modes_last.1.tail0 = f32[264,128]{1,0:T(8,128)S(1)} custom-call(s32[2,3]{1,0:T(2,128)S(1)} %copy-done.16, f32[32,16,128]{2,1,0:T(8,128)S(1)} %all-to-all-done.6.refs_1_, f32[128,128]{1,0:T(8,128)S(1)} %get-tuple-element.63.refs_2_, f32[256,256]{1,0:T(8,128)S(1)} %fusion.5.refs_3_, f32[128,128]{1,0:T(8,128)S(1)} %get-tuple-element.60.refs_4_, ...), custom_call_target="tpu_custom_call" | custom-call | tf_op jit(solution)/shard_map/modes_last/pallas_call | solution.py:122
  170.7 2.4 %collective-permute-start.9 = (f32[264,128]{1,0:T(8,128)S(1)}, f32[264,128]{1,0:T(8,128)S(1)}, u32[]{:S(2)}, u32[]{:S(2)}) collective-permute-start(f32[264,128]{1,0:T(8,128)S(1)} %modes_last.1.tail0), channel_id=1, source_target_pairs={{0,32},{32,0},{64,96},{96,64},{1,33},{33,1},{65,97},{97,65},{2,34}... | collective-permute-start | bytes 405512 | tf_op jit(solution)/shard_map/ppermute | solution.py:923
  173.1 7.6 %collective-permute-start.10 = (f32[264,128]{1,0:T(8,128)S(1)}, f32[264,128]{1,0:T(8,128)S(1)}, u32[]{:S(2)}, u32[]{:S(2)}) collective-permute-start(f32[264,128]{1,0:T(8,128)S(1)} %modes_last.1.tail0), channel_id=1, source_target_pairs={{0,64},{32,96},{64,0},{96,32},{1,65},{33,97},{65,1},{97,33},{2,66}... | collective-permute-start | bytes 405512 | tf_op jit(solution)/shard_map/ppermute | solution.py:923
  181.7 5.7 %collective-permute-done.11.tail3 = f32[264,128]{1,0:T(8,128)S(1)} collective-permute-done((f32[264,128]{1,0:T(8,128)S(1)}, f32[264,128]{1,0:T(8,128)S(1)}, u32[]{:S(2)}, u32[]{:S(2)}) %collective-permute-start.11) | collective-permute-done | bytes 135200 | tf_op jit(solution)/shard_map/ppermute | solution.py:923
  187.4 0.7 spread.1
  188.1 3.8 %all-to-all-start.7 = ((f32[32,8,128]{2,1,0:T(8,128)}), f32[32,8,128]{2,1,0:T(8,128)S(1)}, u32[]{:S(2)}, u32[]{:S(2)}) async-start(f32[32,8,128]{2,1,0:T(8,128)} %spread.1), calls=%async_computation.7 | async-start | bytes 262144 | tf_op jit(solution)/shard_map/all_to_all | solution.py:974
  191.9 5.0 %outer.1 = f32[2,8,16,64,64]{4,3,2,1,0:T(8,128)} custom-call(f32[264,128]{1,0:T(8,128)S(1)} %modes_last.1.tail0, f32[264,128]{1,0:T(8,128)S(1)} %collective-permute-done.9.tail1, f32[264,128]{1,0:T(8,128)S(1)} %collective-permute-done.10.tail2, f32[264,128]{1,0:T(8,128)S(1)} %collective-permute-done.11.tail3), custom_call_target="tpu_custom_call" | custom-call | tf_op jit(solution)/shard_map/outer/pallas_call | solution.py:856
  197.0 2.5 %all-to-all-done.7.late = f32[32,8,128]{2,1,0:T(8,128)S(1)} async-done(((f32[32,8,128]{2,1,0:T(8,128)}), f32[32,8,128]{2,1,0:T(8,128)S(1)}, u32[]{:S(2)}, u32[]{:S(2)}) %all-to-all-start.7) | async-done | bytes 131104 | tf_op jit(solution)/shard_map/all_to_all | solution.py:974
  199.5 1.0 finish.1
  (66 shorter events, 2.9 us)
Async XLA Ops:
  0.6 1.0 copy-start.10
  1.6 0.8 copy-start.12
  2.6 5.6 %collective-permute-start = (f32[16,256]{1,0:T(8,128)S(1)}, f32[16,256]{1,0:T(8,128)S(1)}, u32[]{:S(2)}, u32[]{:S(2)}) collective-permute-start(f32[16,256]{1,0:T(8,128)S(1)} %ends.1), channel_id=1, source_target_pairs={{0,32},{32,0},{64,96},{96,64},{1,33},{33,1},{65,97},{97,65},{2,34}... | collective-permute-start | bytes 49160 | tf_op jit(solution)/shard_map/ppermute | solution.py:923
  8.4 19.0 %collective-permute-start.2 = (f32[27,16,256]{2,1,0:T(8,128)S(1)}, f32[27,16,256]{2,1,0:T(8,128)S(1)}, u32[]{:S(2)}, u32[]{:S(2)}) collective-permute-start(f32[27,16,256]{2,1,0:T(8,128)S(1)} %get-tuple-element.39), channel_id=1, source_target_pairs={{0,1},{1,2},{2,3},{3,4},{4,5},{5,6},{6,7},{7,8},{8,9},{9,10},{10,1... | collective-permute-start | bytes 1327112 | tf_op jit(solution)/shard_map/ppermute | solution.py:915
  11.3 12.2 %collective-permute-start.3 = (f32[24,16,256]{2,1,0:T(8,128)S(1)}, f32[24,16,256]{2,1,0:T(8,128)S(1)}, u32[]{:S(2)}, u32[]{:S(2)}) collective-permute-start(f32[24,16,256]{2,1,0:T(8,128)S(1)} %get-tuple-element.40), channel_id=1, source_target_pairs={{1,0},{2,1},{3,2},{4,3},{5,4},{6,5},{7,6},{8,7},{9,8},{10,9},{11,1... | collective-permute-start | bytes 1179656 | tf_op jit(solution)/shard_map/ppermute | solution.py:915
  12.6 17.9 %collective-permute-start.1 = (f32[29,16,256]{2,1,0:T(8,128)S(1)}, f32[29,16,256]{2,1,0:T(8,128)S(1)}, u32[]{:S(2)}, u32[]{:S(2)}) collective-permute-start(f32[29,16,256]{2,1,0:T(8,128)S(1)} %get-tuple-element.38.refs_3_), channel_id=1, source_target_pairs={{0,64},{64,0},{1,65},{65,1},{2,66},{66,2},{3,67},{67,3},{4,68},{68... | collective-permute-start | bytes 1425416 | tf_op jit(solution)/shard_map/ppermute | solution.py:919
  27.3 3.0 %copy-start.25 = (f32[6,64]{1,0:T(8,128)S(1)}, f32[6,64]{1,0:T(8,128)}, u32[]{:S(2)}) copy-start(f32[6,64]{1,0:T(8,128)} %param.27) | copy-start | bytes 4612
  27.3 3.0 %copy-start.24 = (f32[2,64,64]{2,1,0:T(8,128)S(1)}, f32[2,64,64]{2,1,0:T(8,128)}, u32[]{:S(2)}) copy-start(f32[2,64,64]{2,1,0:T(8,128)} %param.25) | copy-start | bytes 98308
  27.3 3.0 %copy-start.26 = (f32[64,6]{0,1:T(8,128)S(1)}, f32[64,6]{0,1:T(8,128)}, u32[]{:S(2)}) copy-start(f32[64,6]{0,1:T(8,128)} %param.24) | copy-start | bytes 4612
  27.3 4.9 %copy-start.13 = (f32[256,128]{1,0:T(8,128)S(1)}, f32[256,128]{1,0:T(8,128)}, u32[]{:S(2)}) copy-start(f32[256,128]{1,0:T(8,128)} %constant.12.clone.refs_9_) | copy-start | bytes 393220
  27.3 4.9 %copy-start.17 = (s32[4]{0:T(128)S(1)}, s32[4]{0:T(128)}, u32[]{:S(2)}) copy-start(s32[4]{0:T(128)} %refs_0_.5) | copy-start | bytes 52
  27.4 4.9 %copy-start.18 = (f32[4]{0:T(128)S(1)}, f32[4]{0:T(128)}, u32[]{:S(2)}) copy-start(f32[4]{0:T(128)} %refs_1_.1) | copy-start | bytes 52
  27.4 4.9 %copy-start.19 = (f32[4]{0:T(128)S(1)}, f32[4]{0:T(128)}, u32[]{:S(2)}) copy-start(f32[4]{0:T(128)} %refs_2_.2) | copy-start | bytes 52
  27.4 19.9 %copy-start.6 = (bf16[2,256,256]{2,1,0:T(8,128)(2,1)S(1)}, bf16[2,256,256]{2,1,0:T(8,128)(2,1)}, u32[]{:S(2)}) copy-start(bf16[2,256,256]{2,1,0:T(8,128)(2,1)} %constant.26.clone.kron.refs_2_.refs_5_) | copy-start | bytes 786436
  27.4 19.9 %copy-start.15 = (bf16[2,32,128]{2,1,0:T(8,128)(2,1)S(1)}, bf16[2,32,128]{2,1,0:T(8,128)(2,1)}, u32[]{:S(2)}) copy-start(bf16[2,32,128]{2,1,0:T(8,128)(2,1)} %constant.9.clone.z_half) | copy-start | bytes 49156
  27.4 4.8 %collective-permute-start.4 = (f32[27,16,256]{2,1,0:T(8,128)S(1)}, f32[27,16,256]{2,1,0:T(8,128)S(1)}, u32[]{:S(2)}, u32[]{:S(2)}) collective-permute-start(f32[27,16,256]{2,1,0:T(8,128)S(1)} %get-tuple-element.41.refs_5_), channel_id=1, source_target_pairs={{0,64},{64,0},{1,65},{65,1},{2,66},{66,2},{3,67},{67,3},{4,68},{68... | collective-permute-start | bytes 1327112 | tf_op jit(solution)/shard_map/ppermute | solution.py:919
  30.2 2.0 collective-permute-start.5
  30.5 34.6 %copy-start.4 = (bf16[2,256,256]{2,1,0:T(8,128)(2,1)S(1)}, bf16[2,256,256]{2,1,0:T(8,128)(2,1)}, u32[]{:S(2)}) copy-start(bf16[2,256,256]{2,1,0:T(8,128)(2,1)} %constant.27.clone.refs_4_.refs_3_.refs_6_) | copy-start | bytes 786436
  30.5 34.6 %copy-start.5 = (bf16[2,256,256]{2,1,0:T(8,128)(2,1)S(1)}, bf16[2,256,256]{2,1,0:T(8,128)(2,1)}, u32[]{:S(2)}) copy-start(bf16[2,256,256]{2,1,0:T(8,128)(2,1)} %constant.28.clone.refs_5_.refs_4_.refs_7_) | copy-start | bytes 786436
  30.5 34.6 %copy-start.16 = (s32[2,3]{1,0:T(2,128)S(1)}, s32[2,3]{1,0:T(2,128)}, u32[]{:S(2)}) copy-start(s32[2,3]{1,0:T(2,128)} %refs_0_.9) | copy-start | bytes 76
  36.7 6.9 %collective-permute-start.6 = (f32[256,128]{1,0:T(8,128)S(1)}, f32[256,128]{1,0:T(8,128)S(1)}, u32[]{:S(2)}, u32[]{:S(2)}) collective-permute-start(f32[256,128]{1,0:T(8,128)S(1)} %get-tuple-element.45), channel_id=1, source_target_pairs={{0,32},{32,0},{64,96},{96,64},{1,33},{33,1},{65,97},{97,65},{2,34}... | collective-permute-start | bytes 393224 | tf_op jit(solution)/shard_map/ppermute | solution.py:923
  40.0 3.6 %collective-permute-start.7 = (f32[256,128]{1,0:T(8,128)S(1)}, f32[256,128]{1,0:T(8,128)S(1)}, u32[]{:S(2)}, u32[]{:S(2)}) collective-permute-start(f32[256,128]{1,0:T(8,128)S(1)} %get-tuple-element.46), channel_id=1, source_target_pairs={{0,64},{32,96},{64,0},{96,32},{1,65},{33,97},{65,1},{97,33},{2,66}... | collective-permute-start | bytes 393224 | tf_op jit(solution)/shard_map/ppermute | solution.py:923
  40.7 6.6 %collective-permute-start.8 = (f32[256,128]{1,0:T(8,128)S(1)}, f32[256,128]{1,0:T(8,128)S(1)}, u32[]{:S(2)}, u32[]{:S(2)}) collective-permute-start(f32[256,128]{1,0:T(8,128)S(1)} %get-tuple-element.47), channel_id=1, source_target_pairs={{0,96},{32,64},{64,32},{96,0},{1,97},{33,65},{65,33},{97,1},{2,98}... | collective-permute-start | bytes 393224 | tf_op jit(solution)/shard_map/ppermute | solution.py:923
  48.6 16.4 %all-to-all-start = ((f32[32,8,128]{2,1,0:T(8,128)}), f32[32,8,128]{2,1,0:T(8,128)S(1)}, u32[]{:S(2)}, u32[]{:S(2)}) async-start(f32[32,8,128]{2,1,0:T(8,128)} %bitcast.4), calls=%async_computation | async-start | bytes 262144 | tf_op jit(solution)/shard_map/all_to_all | solution.py:974
  58.8 1.3 copy-start.20
  60.1 8.6 %copy-start.3 = (f32[4096,128]{1,0:T(8,128)}, f32[4096,128]{1,0:T(8,128)S(1)}, u32[]{:S(2)}) copy-start(f32[4096,128]{1,0:T(8,128)S(1)} %get-tuple-element.48.refs_6_.refs_1_) | copy-start | bytes 6291460
  68.7 0.7 copy-start.14
  69.4 11.2 %all-to-all-start.1 = ((f32[32,8,128]{2,1,0:T(8,128)}), f32[32,8,128]{2,1,0:T(8,128)S(1)}, u32[]{:S(2)}, u32[]{:S(2)}) async-start(f32[32,8,128]{2,1,0:T(8,128)} %bitcast.38), calls=%async_computation.1 | async-start | bytes 262144 | tf_op jit(solution)/shard_map/all_to_all | solution.py:974
  75.1 1.4 copy-start
  76.4 1.4 copy-start.7
  80.6 0.6 copy-start.22
  86.5 12.3 %all-to-all-start.2 = ((f32[32,8,128]{2,1,0:T(8,128)}), f32[32,8,128]{2,1,0:T(8,128)S(1)}, u32[]{:S(2)}, u32[]{:S(2)}) async-start(f32[32,8,128]{2,1,0:T(8,128)} %bitcast.49), calls=%async_computation.2 | async-start | bytes 262144 | tf_op jit(solution)/shard_map/all_to_all | solution.py:974
  102.9 11.3 %all-to-all-start.3 = ((f32[32,8,128]{2,1,0:T(8,128)}), f32[32,8,128]{2,1,0:T(8,128)S(1)}, u32[]{:S(2)}, u32[]{:S(2)}) async-start(f32[32,8,128]{2,1,0:T(8,128)} %bitcast.12), calls=%async_computation.3 | async-start | bytes 262144 | tf_op jit(solution)/shard_map/all_to_all | solution.py:974
  114.2 0.6 copy-start.23
  114.8 10.9 %copy-start.1 = (bf16[4096,256]{1,0:T(8,128)(2,1)S(1)}, bf16[4096,256]{1,0:T(8,128)(2,1)}, u32[]{:S(2)}) copy-start(bf16[4096,256]{1,0:T(8,128)(2,1)} %get-tuple-element.53.refs_1_) | copy-start | bytes 6291460
  121.9 11.2 %all-to-all-start.4 = ((f32[32,8,128]{2,1,0:T(8,128)}), f32[32,8,128]{2,1,0:T(8,128)S(1)}, u32[]{:S(2)}, u32[]{:S(2)}) async-start(f32[32,8,128]{2,1,0:T(8,128)} %bitcast.48), calls=%async_computation.4 | async-start | bytes 262144 | tf_op jit(solution)/shard_map/all_to_all | solution.py:974
  125.8 1.6 copy-start.2
  133.1 8.1 %copy-start.8 = (f32[4096,128]{1,0:T(8,128)S(1)}, f32[4096,128]{1,0:T(8,128)}, u32[]{:S(2)}) copy-start(f32[4096,128]{1,0:T(8,128)} %copy-done.7) | copy-start | bytes 6291460
  137.4 11.2 %all-to-all-start.5 = ((f32[32,8,128]{2,1,0:T(8,128)}), f32[32,8,128]{2,1,0:T(8,128)S(1)}, u32[]{:S(2)}, u32[]{:S(2)}) async-start(f32[32,8,128]{2,1,0:T(8,128)} %bitcast.19), calls=%async_computation.5 | async-start | bytes 262144 | tf_op jit(solution)/shard_map/all_to_all | solution.py:974
  141.2 1.6 copy-start.9
  145.0 0.6 copy-start.11
  148.6 0.6 copy-start.21
  154.6 12.8 %all-to-all-start.6 = ((f32[32,16,128]{2,1,0:T(8,128)}), f32[32,16,128]{2,1,0:T(8,128)S(1)}, u32[]{:S(2)}, u32[]{:S(2)}) async-start(f32[32,16,128]{2,1,0:T(8,128)} %get-tuple-element.62), calls=%async_computation.6 | async-start | bytes 524288 | tf_op jit(solution)/shard_map/all_to_all | solution.py:974
  170.7 10.5 %collective-permute-start.9 = (f32[264,128]{1,0:T(8,128)S(1)}, f32[264,128]{1,0:T(8,128)S(1)}, u32[]{:S(2)}, u32[]{:S(2)}) collective-permute-start(f32[264,128]{1,0:T(8,128)S(1)} %modes_last.1.tail0), channel_id=1, source_target_pairs={{0,32},{32,0},{64,96},{96,64},{1,33},{33,1},{65,97},{97,65},{2,34}... | collective-permute-start | bytes 405512 | tf_op jit(solution)/shard_map/ppermute | solution.py:923
  173.1 8.6 %collective-permute-start.10 = (f32[264,128]{1,0:T(8,128)S(1)}, f32[264,128]{1,0:T(8,128)S(1)}, u32[]{:S(2)}, u32[]{:S(2)}) collective-permute-start(f32[264,128]{1,0:T(8,128)S(1)} %modes_last.1.tail0), channel_id=1, source_target_pairs={{0,64},{32,96},{64,0},{96,32},{1,65},{33,97},{65,1},{97,33},{2,66}... | collective-permute-start | bytes 405512 | tf_op jit(solution)/shard_map/ppermute | solution.py:923
  180.7 6.7 %collective-permute-start.11 = (f32[264,128]{1,0:T(8,128)S(1)}, f32[264,128]{1,0:T(8,128)S(1)}, u32[]{:S(2)}, u32[]{:S(2)}) collective-permute-start(f32[264,128]{1,0:T(8,128)S(1)} %modes_last.1.tail0), channel_id=1, source_target_pairs={{0,96},{32,64},{64,32},{96,0},{1,97},{33,65},{65,33},{97,1},{2,98}... | collective-permute-start | bytes 405512 | tf_op jit(solution)/shard_map/ppermute | solution.py:923
  188.1 11.4 %all-to-all-start.7 = ((f32[32,8,128]{2,1,0:T(8,128)}), f32[32,8,128]{2,1,0:T(8,128)S(1)}, u32[]{:S(2)}, u32[]{:S(2)}) async-start(f32[32,8,128]{2,1,0:T(8,128)} %spread.1), calls=%async_computation.7 | async-start | bytes 262144 | tf_op jit(solution)/shard_map/all_to_all | solution.py:974
